TPU v7x, 32 devices: a whole 2x2x4 slice. The times are simulated.
32 devices in a mesh: groups: 2 (over y), node: 4 (over x, core), local: 4 (over z).
Axes of the slice: x: 2, y: 2, z: 4, core: 2. Of those that a mesh axis runs over, the one named last changes fastest.
Arguments:
- tokens: bfloat16 [128, 7168], P(('groups', 'node', 'local')), parts along dimension 0, may hold values from -6 to 6
- node_list: int32 [128, 2], P(('groups', 'node', 'local')), parts along dimension 0, may hold values from 0 to 3, all different within a row; in each aligned block of 4 rows (0 to 3, 4 to 7, ...) at most 3 rows name the same one
- gates: bfloat16 [128, 4], P(('groups', 'node', 'local')), parts along dimension 0, may hold values from 0.099609375 to 1
- row_source: int32 [32, 4], P(('groups', 'node', 'local')), parts along dimension 0, may hold values from 0 to 3, each once within a row
- expert_in: bfloat16 [8, 7168, 2, 1024], P('node', None, None, 'local'), may hold values from -0.0625 to 0.0625
- expert_out: bfloat16 [8, 1024, 7168], P('node', 'local'), may hold values from -0.1875 to 0.1875
Outputs:
- mixed: bfloat16 [128, 7168], P(('groups', 'node', 'local')), parts along dimension 0
There are 2 independent parts, one for each index of `groups`. A program takes and returns all parts, laid end to end along the dimension named above; an argument that names none is the same for every part. Nothing has to cross between parts.
Inputs may be any that keep to these rules, and one draw needn't show every extreme that they name: `node_list`: each row lists 2 different nodes. Among the 4 rows of one device no node is listed more than 3 times, and on some device some node is listed exactly 3 times. `row_source`: each row is a permutation of 0 to 3.
All inputs are finite; a program needn't handle non-finite values.
Results may differ from a plain program's by a relative error of at most 0.0095.
Values may be sent and summed in bfloat16 or wider, within the bound.
No kernel may reach another device: no remote copies, remote signals or barrier semaphores. Data moves between devices by JAX's collectives and lax.ppermute only.
A program may use at most 64 MiB of HBM per device.

v0:
```python
import jax
import jax.numpy as jnp
from jax import lax
from jax.sharding import PartitionSpec as P


def expert_hidden(rows, pairs, weight_in):
    proj = jnp.einsum("rd,edgf->regf", rows, weight_in, preferred_element_type=jnp.float32)
    active = jax.nn.silu(proj[:, :, 0]) * proj[:, :, 1] * pairs.astype(jnp.float32)[:, :, None]
    return active.astype(jnp.bfloat16).reshape(rows.shape[0], -1)


def shards(tokens, node_list, gates, row_source, expert_in, expert_out):
    row_count, width = tokens.shape
    slot_count = node_list.shape[1]
    pair_size = expert_in.shape[0]
    node_count = lax.axis_size("node")
    local_count = lax.axis_size("local")
    capacity = max(2, 3 * row_count * slot_count // (2 * node_count))
    buffer_rows = node_count * capacity
    messages = row_count * slot_count
    flat_node = node_list.reshape(messages)
    node_hits = (flat_node[:, None] == jnp.arange(node_count, dtype=jnp.int32)[None, :]).astype(
        jnp.int32
    )
    earlier = jnp.cumsum(node_hits, axis=0) - node_hits
    rank = jnp.sum(earlier * node_hits, axis=1)
    position = flat_node * capacity + rank
    route = (jnp.arange(buffer_rows, dtype=jnp.int32)[:, None] == position[None, :]).astype(
        jnp.float32
    )
    placement = jnp.sum(route.reshape(buffer_rows, row_count, slot_count), axis=2)
    send_rows = jnp.dot(
        placement.astype(jnp.bfloat16), tokens, preferred_element_type=jnp.float32
    ).astype(jnp.bfloat16)
    send_pairs = jnp.dot(
        route,
        gates.reshape(messages, pair_size).astype(jnp.float32),
        precision=lax.Precision.HIGHEST,
    ).astype(jnp.bfloat16)
    weight_down = expert_out.reshape(-1, width)
    peers = node_count * local_count
    spread_rows = jnp.broadcast_to(
        send_rows.reshape(node_count, 1, capacity, width),
        (node_count, local_count, capacity, width),
    ).reshape(peers, capacity, width)
    spread_pairs = jnp.broadcast_to(
        send_pairs.reshape(node_count, 1, capacity, pair_size),
        (node_count, local_count, capacity, pair_size),
    ).reshape(peers, capacity, pair_size)
    given_rows = lax.all_to_all(
        spread_rows, ("node", "local"), split_axis=0, concat_axis=0, tiled=True
    )
    given_pairs = lax.all_to_all(
        spread_pairs, ("node", "local"), split_axis=0, concat_axis=0, tiled=True
    )
    count = given_rows.shape[1]
    hidden = expert_hidden(
        given_rows.reshape(peers * count, width),
        given_pairs.reshape(peers * count, pair_size),
        expert_in,
    )
    partial_out = jnp.dot(hidden, weight_down, preferred_element_type=jnp.float32).astype(
        jnp.bfloat16
    )
    gathered = lax.all_to_all(
        partial_out.reshape(peers, count, width),
        ("node", "local"),
        split_axis=0,
        concat_axis=0,
        tiled=True,
    )
    returned = jnp.sum(
        gathered.reshape(node_count, local_count, capacity, width).astype(jnp.float32), axis=1
    )
    returned = returned.reshape(buffer_rows, width).astype(jnp.bfloat16)
    invert = (
        row_source.reshape(row_count)[:, None] == jnp.arange(row_count, dtype=jnp.int32)[None, :]
    ).astype(jnp.float32)
    gather_plan = jnp.dot(invert, placement.T, precision=lax.Precision.HIGHEST)
    mixed = jnp.dot(gather_plan.astype(jnp.bfloat16), returned, preferred_element_type=jnp.float32)
    return mixed.astype(jnp.bfloat16)


def solution(mesh):
    return jax.shard_map(
        shards,
        mesh=mesh,
        in_specs=(
            P(("groups", "node", "local"), None),
            P(("groups", "node", "local"), None),
            P(("groups", "node", "local"), None),
            P(("groups", "node", "local"), None),
            P("node", None, None, "local"),
            P("node", "local", None),
        ),
        out_specs=P(("groups", "node", "local"), None),
        check_vma=False,
    )
```

profile of v0, /device:TPU:0, one launch (start us, length us, event | category | flops | bytes accessed | tf_op | source)
XLA Modules:
  0.0 85.8 jit_solution(14412939411978609501)
XLA Ops:
  0.0 0.8 copy.41
  0.8 0.1 eq.55
  0.9 0.2 reduce_window_sum.11
  1.1 0.8 reshape.57
  1.8 0.2 convolution_convert_fusion.3
  2.0 0.1 broadcast_in_dim.10
  2.1 0.6 broadcast_in_dim.22.clone
  2.7 7.4 %all-to-all-start.1 = ((bf16[16,3,2]{1,2,0:T(2,128)(2,1)}), bf16[16,3,2]{1,2,0:T(2,128)(2,1)S(1)}, u32[]{:S(2)}, u32[]{:S(2)}) async-start(bf16[16,3,2]{1,2,0:T(2,128)(2,1)} %bitcast.5), calls=%async_computation.1 | async-start | bytes 16384 | tf_op jit(solution)/shard_map/all_to_all | solution.py:54
  10.1 0.1 reduce_sum.30
  10.2 0.1 copy.43
  10.3 0.1 convert_reduce_fusion
  10.4 0.3 convolution_convert_fusion
  10.6 0.1 broadcast_in_dim.8
  10.8 5.6 %all-to-all-done.1 = bf16[16,3,2]{1,2,0:T(2,128)(2,1)S(1)} async-done(((bf16[16,3,2]{1,2,0:T(2,128)(2,1)}), bf16[16,3,2]{1,2,0:T(2,128)(2,1)S(1)}, u32[]{:S(2)}, u32[]{:S(2)}) %all-to-all-start.1) | async-done | bytes 224 | tf_op jit(solution)/shard_map/all_to_all | solution.py:54
  16.4 1.2 %broadcast_in_dim.9 = bf16[4,4,3,7168]{3,2,1,0:T(4,128)(2,1)} broadcast(bf16[4,3,7168]{2,1,0:T(4,128)(2,1)S(1)} %broadcast_in_dim.8), dimensions={0,2,3} | broadcast | bytes 860160 | tf_op jit(solution)/shard_map/broadcast_in_dim | solution.py:43
  17.6 3.6 %all-to-all-start = ((bf16[16,3,7168]{2,1,0:T(4,128)(2,1)}), bf16[16,3,7168]{2,1,0:T(4,128)(2,1)S(1)}, u32[]{:S(2)}, u32[]{:S(2)}) async-start(bf16[16,3,7168]{2,1,0:T(4,128)(2,1)} %bitcast.1), calls=%async_computation | async-start | bytes 1835008 | tf_op jit(solution)/shard_map/all_to_all | solution.py:51
  21.2 0.1 copy.48
  21.3 0.1 copy.49
  21.4 0.1 reshape.60
  21.5 23.8 %all-to-all-done = bf16[16,3,7168]{2,1,0:T(4,128)(2,1)S(1)} async-done(((bf16[16,3,7168]{2,1,0:T(4,128)(2,1)}), bf16[16,3,7168]{2,1,0:T(4,128)(2,1)S(1)}, u32[]{:S(2)}, u32[]{:S(2)}) %all-to-all-start) | async-done | bytes 688160 | tf_op jit(solution)/shard_map/all_to_all | solution.py:51
  45.3 0.6 reshape.61
  45.9 0.0 copy-start.1
  46.0 0.0 copy-start.2
  46.0 8.0 %fusion = f32[48,2,2,256]{3,0,2,1:T(8,128)S(1)} fusion(bf16[2,7168,2,256]{3,2,1,0:T(2,128)(2,1)} %param.10, bf16[48,7168,1,1]{1,0,2,3:T(8,128)(2,1)S(1)} %reshape.61), kind=kOutput, calls=%fused_computation | convolution fusion | flops 704643072 | bytes 15564800 | tf_op jit(solution)/shard_map/rd,edgf->regf/dot_general | solution.py:8
  54.0 1.4 %fusion.2 = bf16[48,7168]{1,0:T(8,128)(2,1)S(1)} fusion(bf16[2,256,7168]{2,1,0:T(8,128)(2,1)S(1)} %copy-done.1, f32[48,2,2,256]{3,0,2,1:T(8,128)S(1)} %fusion, f32[48,2]{0,1:T(2,128)S(1)} %reshape.60), kind=kOutput, calls=%fused_computation.3 | convolution fusion | flops 352837632 | bytes 8225152 | tf_op jit(solution)/shard_map/dot_general | solution.py:63
  55.5 1.2 %reshape.59 = bf16[16,3,7168]{2,1,0:T(4,128)(2,1)} reshape(bf16[48,7168]{1,0:T(8,128)(2,1)S(1)} %fusion.2) | data formatting | bytes 1376256 | tf_op jit(solution)/shard_map/reshape | solution.py:67
  56.7 3.6 %all-to-all-start.2 = ((bf16[16,3,7168]{2,1,0:T(4,128)(2,1)}), bf16[16,3,7168]{2,1,0:T(4,128)(2,1)S(1)}, u32[]{:S(2)}, u32[]{:S(2)}) async-start(bf16[16,3,7168]{2,1,0:T(4,128)(2,1)} %reshape.59), calls=%async_computation.2 | async-start | bytes 1835008 | tf_op jit(solution)/shard_map/all_to_all | solution.py:66
  60.3 0.2 convolution_convert_fusion.2
  60.5 23.9 %all-to-all-done.2 = bf16[16,3,7168]{2,1,0:T(4,128)(2,1)S(1)} async-done(((bf16[16,3,7168]{2,1,0:T(4,128)(2,1)}), bf16[16,3,7168]{2,1,0:T(4,128)(2,1)S(1)}, u32[]{:S(2)}, u32[]{:S(2)}) %all-to-all-start.2) | async-done | bytes 688160 | tf_op jit(solution)/shard_map/all_to_all | solution.py:66
  84.4 0.5 bitcast_reduce_fusion
  84.9 0.2 convert_element_type.65
  85.0 0.8 convolution_convert_fusion.1
  (9 shorter events, 0.1 us)
Async XLA Ops:
  0.0 10.4 %copy-start = (bf16[4,7168]{1,0:T(4,128)(2,1)S(1)}, bf16[4,7168]{1,0:T(4,128)(2,1)}, u32[]{:S(2)}) copy-start(bf16[4,7168]{1,0:T(4,128)(2,1)} %param.6) | copy-start | bytes 172036
  2.7 13.7 %all-to-all-start.1 = ((bf16[16,3,2]{1,2,0:T(2,128)(2,1)}), bf16[16,3,2]{1,2,0:T(2,128)(2,1)S(1)}, u32[]{:S(2)}, u32[]{:S(2)}) async-start(bf16[16,3,2]{1,2,0:T(2,128)(2,1)} %bitcast.5), calls=%async_computation.1 | async-start | bytes 16384 | tf_op jit(solution)/shard_map/all_to_all | solution.py:54
  17.6 27.8 %all-to-all-start = ((bf16[16,3,7168]{2,1,0:T(4,128)(2,1)}), bf16[16,3,7168]{2,1,0:T(4,128)(2,1)S(1)}, u32[]{:S(2)}, u32[]{:S(2)}) async-start(bf16[16,3,7168]{2,1,0:T(4,128)(2,1)} %bitcast.1), calls=%async_computation | async-start | bytes 1835008 | tf_op jit(solution)/shard_map/all_to_all | solution.py:51
  45.9 8.1 %copy-start.1 = (bf16[2,256,7168]{2,1,0:T(8,128)(2,1)S(1)}, bf16[2,256,7168]{2,1,0:T(8,128)(2,1)}, u32[]{:S(2)}) copy-start(bf16[2,256,7168]{2,1,0:T(8,128)(2,1)} %param.11) | copy-start | bytes 22020100
  46.0 14.4 %copy-start.2 = (s32[1,4]{1,0:T(1,128)S(1)}, s32[1,4]{1,0:T(1,128)}, u32[]{:S(2)}) copy-start(s32[1,4]{1,0:T(1,128)} %param.9) | copy-start | bytes 52
  56.7 27.8 %all-to-all-start.2 = ((bf16[16,3,7168]{2,1,0:T(4,128)(2,1)}), bf16[16,3,7168]{2,1,0:T(4,128)(2,1)S(1)}, u32[]{:S(2)}, u32[]{:S(2)}) async-start(bf16[16,3,7168]{2,1,0:T(4,128)(2,1)} %reshape.59), calls=%async_computation.2 | async-start | bytes 1835008 | tf_op jit(solution)/shard_map/all_to_all | solution.py:66
where the time goes:
time: 86.2 us; the launch traced here: 85.8 us
  waiting for transfers between devices  53.4 us (62%)
  starting transfers between devices  14.6 us (17%)
  matrix products  10.9 us (13%)
  local copies, waits for them, and re-layouts  6.08 us (7%)
    all_to_all x1, waiting for transfers between devices, shards(): lax.all_to_all(partial_out.reshape(peers, count, width), ('node', 'local'...  23.9 us
    all_to_all x1, waiting for transfers between devices, shards(): lax.all_to_all(spread_rows, ('node', 'local'), split_axis=0, concat_axis=...  23.8 us
    dot_general x1, matrix products, expert_hidden(): jnp.einsum('rd,edgf->regf', rows, weight_in, preferred_element_type=jnp.f...  8.02 us
    all_to_all x1, starting transfers between devices, shards(): lax.all_to_all(spread_pairs, ('node', 'local'), split_axis=0, concat_axis...  7.36 us
    all_to_all x1, waiting for transfers between devices, shards(): lax.all_to_all(spread_pairs, ('node', 'local'), split_axis=0, concat_axis...  5.63 us
    all_to_all x1, starting transfers between devices, shards(): lax.all_to_all(spread_rows, ('node', 'local'), split_axis=0, concat_axis=...  3.63 us
    all_to_all x1, starting transfers between devices, shards(): lax.all_to_all(partial_out.reshape(peers, count, width), ('node', 'local'...  3.63 us
  transfers between devices with their start and end apart: 3, of which 3 were waited for; matrix products, arithmetic and copies ran while one was open for 1% of the time, Pallas kernels for 0%

commit v1 on v0

v1 whole, which is shorter than its diff:
```python
import jax
import jax.numpy as jnp
from jax import lax
from jax.sharding import PartitionSpec as P

AXES = ("node", "local")


def swap(value, mask, count):
    return lax.ppermute(value, AXES, [(i, i ^ mask) for i in range(count)])


def shards(tokens, node_list, gates, row_source, expert_in, expert_out):
    rows, width = tokens.shape
    slots = node_list.shape[1]
    pair = expert_in.shape[0]
    units = expert_in.shape[3]
    nodes = lax.axis_size("node")
    locals_ = lax.axis_size("local")
    count = nodes * locals_
    hit = (node_list[:, :, None] == jnp.arange(nodes, dtype=jnp.int32)).astype(jnp.float32)
    dense = jnp.sum(
        hit[:, :, :, None] * gates.reshape(rows, slots, 1, pair).astype(jnp.float32), axis=1
    ).reshape(rows, nodes * pair)
    extra = -(-nodes * pair // 128) * 128
    message = jnp.concatenate(
        [tokens, jnp.pad(dense, ((0, 0), (0, extra - nodes * pair))).astype(jnp.bfloat16)], axis=1
    )
    pick = (row_source.reshape(rows)[:, None] == jnp.arange(rows, dtype=jnp.int32)).astype(
        jnp.bfloat16
    )
    message = jnp.dot(pick, message, preferred_element_type=jnp.float32).astype(jnp.bfloat16)
    along = jnp.concatenate(
        [message] + [swap(message, k, count) for k in range(1, locals_)], axis=0
    )
    across = jnp.concatenate(
        [along] + [swap(along, k * 2 * locals_, count) for k in range(1, nodes // 2)], axis=0
    )
    everything = jnp.concatenate([across, swap(across, locals_, count)], axis=0)
    total = everything.shape[0]
    mine = (jnp.arange(nodes) == lax.axis_index("node")).astype(jnp.float32)
    weight = jnp.sum(
        everything[:, width : width + nodes * pair].astype(jnp.float32).reshape(total, nodes, pair)
        * mine[None, :, None],
        axis=1,
    )
    proj = jnp.einsum(
        "rd,edgf->regf", everything[:, :width], expert_in, preferred_element_type=jnp.float32
    )
    hidden = (
        (jax.nn.silu(proj[:, :, 0]) * proj[:, :, 1] * weight[:, :, None])
        .astype(jnp.bfloat16)
        .reshape(total, pair * units)
    )
    out = jnp.dot(
        hidden, expert_out.reshape(pair * units, width), preferred_element_type=jnp.float32
    ).astype(jnp.bfloat16)
    half = total // 2
    out = (
        out[:half].astype(jnp.float32) + swap(out[half:], locals_, count).astype(jnp.float32)
    ).astype(jnp.bfloat16)
    step = rows * locals_
    parts = [out[:step]] + [
        swap(out[k * step : (k + 1) * step], k * 2 * locals_, count) for k in range(1, nodes // 2)
    ]
    out = sum(p.astype(jnp.float32) for p in parts).astype(jnp.bfloat16)
    parts = [out[:rows]] + [
        swap(out[k * rows : (k + 1) * rows], k, count) for k in range(1, locals_)
    ]
    return sum(p.astype(jnp.float32) for p in parts).astype(jnp.bfloat16)


def solution(mesh):
    spec = P(("groups", "node", "local"), None)
    return jax.shard_map(
        shards,
        mesh=mesh,
        in_specs=(spec, spec, spec, spec, P("node", None, None, "local"), P("node", "local", None)),
        out_specs=spec,
        check_vma=False,
    )
```

time: 86.2 us -> 76.5 us (0.89)
  waiting for transfers between devices: 53.4 us -> 22 us
  local copies, waits for them, and re-layouts: 6.08 us -> 23.7 us
  matrix products: 10.9 us -> 14.5 us
  other arithmetic: 0.76 us -> 1.92 us
    all_to_all x3 -> x0, waiting for transfers between devices: 53.4 us -> none  [the longest x1 23.9 us: shards(): lax.all_to_all(partial_out.reshape(peers, count, width), ('node', 'local'...]
    ppermute x0 -> x10, waiting for transfers between devices: none -> 22 us  [swap(): return lax.ppermute(value, AXES, [(i, i ^ mask) for i in range(count)])]
    all_to_all x3 -> x0, starting transfers between devices: 14.6 us -> none  [the longest x1 7.36 us: shards(): lax.all_to_all(spread_pairs, ('node', 'local'), split_axis=0, concat_axis...]
    ppermute x0 -> x10, starting transfers between devices: none -> 13.8 us  [swap(): return lax.ppermute(value, AXES, [(i, i ^ mask) for i in range(count)])]
    concatenate x0 -> x2, local copies, waits for them, and re-layouts: none -> 11.9 us  [the longest x1 11.7 us: shards(): everything = jnp.concatenate([across, swap(across, locals_, count)], axis=0)]
    ppermute x0 -> x5, local copies, waits for them, and re-layouts: none -> 9.33 us  [swap(): return lax.ppermute(value, AXES, [(i, i ^ mask) for i in range(count)])]
    dot_general x6 -> x3, matrix products: 10.9 us -> 14.5 us  [the longest x1 8.29 us: shards(): jnp.einsum('rd,edgf->regf', everything[:, :width], expert_in, preferred_e...]
    reshape x3 -> x0, local copies, waits for them, and re-layouts: 2.59 us -> none  [the longest x1 1.22 us: shards(): partial_out.reshape(peers, count, width)]
  transfers between devices with their start and end apart: 3 -> 10, of which waited for: 3 -> 7; matrix products, arithmetic and copies ran while one was open for 1% -> 10% of each run, Pallas kernels for 0% -> 0%
where the time goes in v1:
time: 76.5 us; the launch traced here: 76 us
  local copies, waits for them, and re-layouts  23.7 us (31%)
  waiting for transfers between devices  22 us (29%)
  matrix products  14.5 us (19%)
  starting transfers between devices  13.8 us (18%)
  other arithmetic  1.92 us (3%)
    ppermute x10, waiting for transfers between devices, swap(): return lax.ppermute(value, AXES, [(i, i ^ mask) for i in range(count)])  22 us
    ppermute x10, starting transfers between devices, swap(): return lax.ppermute(value, AXES, [(i, i ^ mask) for i in range(count)])  13.8 us
    concatenate x1, local copies, waits for them, and re-layouts, shards(): everything = jnp.concatenate([across, swap(across, locals_, count)], axis=0)  11.7 us
    ppermute x5, local copies, waits for them, and re-layouts, swap(): return lax.ppermute(value, AXES, [(i, i ^ mask) for i in range(count)])  9.33 us
    dot_general x1, matrix products, shards(): jnp.einsum('rd,edgf->regf', everything[:, :width], expert_in, preferred_e...  8.29 us
    dot_general x1, matrix products, shards(): jnp.dot(hidden, expert_out.reshape(pair * units, width), preferred_elemen...  4.52 us
    dot_general x1, matrix products, shards(): jnp.dot(pick, message, preferred_element_type=jnp.float32)  1.7 us
  transfers between devices with their start and end apart: 10, of which 7 were waited for; matrix products, arithmetic and copies ran while one was open for 10% of the time, Pallas kernels for 0%

profile of v1, /device:TPU:0, one launch (start us, length us, event | category | flops | bytes accessed | tf_op | source)
XLA Modules:
  0.0 76.0 jit_solution(4536659958441371006)
XLA Ops:
  0.0 0.7 fusion.17
  0.8 0.8 %copy.33 = f32[4,4]{0,1:T(4,128)S(1)} copy(bf16[4,4]{1,0:T(4,128)(2,1)} %param.8) | data formatting | bytes 96 | tf_op jit(solution)/shard_map/convert_element_type | solution.py:23
  1.6 0.1 copy.34
  1.7 0.1 copy.54
  1.8 1.7 %convolution_convert_fusion = bf16[4,7296]{0,1:T(8,128)(2,1)S(1)} fusion(bf16[4,8]{1,0:T(4,128)(2,1)S(1)} %copy.54, bf16[4,7168]{1,0:T(4,128)(2,1)} %param.6, s32[4]{0:T(128)} %bitcast.32), kind=kOutput, calls=%fused_computation.2 | convolution fusion | flops 437776 | bytes 115792 | tf_op jit(solution)/shard_map/dot_general | solution.py:32
  3.5 1.3 %copy.37 = bf16[4,7296]{1,0:T(4,128)(2,1)S(1)} copy(bf16[4,7296]{0,1:T(8,128)(2,1)S(1)} %convolution_convert_fusion) | data formatting | bytes 116736 | tf_op jit(solution)/shard_map/convert_element_type | solution.py:32
  4.9 3.1 %collective-permute-start = (bf16[4,7296]{1,0:T(4,128)(2,1)S(1)}, bf16[4,7296]{1,0:T(4,128)(2,1)S(1)}, u32[]{:S(2)}, u32[]{:S(2)}) collective-permute-start(bf16[4,7296]{1,0:T(4,128)(2,1)S(1)} %copy.37), channel_id=1, source_target_pairs={{0,1},{1,0},{2,3},{3,2},{4,5},{5,4},{6,7},{7,6},{8,9},{9,8},{10,11... | collective-permute-start | bytes 175112 | tf_op jit(solution)/shard_map/ppermute | solution.py:10
  7.9 2.6 %collective-permute-start.1 = (bf16[4,7296]{1,0:T(4,128)(2,1)S(1)}, bf16[4,7296]{1,0:T(4,128)(2,1)S(1)}, u32[]{:S(2)}, u32[]{:S(2)}) collective-permute-start(bf16[4,7296]{1,0:T(4,128)(2,1)S(1)} %copy.37), channel_id=1, source_target_pairs={{0,2},{1,3},{2,0},{3,1},{4,6},{5,7},{6,4},{7,5},{8,10},{9,11},{10,... | collective-permute-start | bytes 175112 | tf_op jit(solution)/shard_map/ppermute | solution.py:10
  10.5 3.6 %collective-permute-done.1 = bf16[4,7296]{1,0:T(4,128)(2,1)S(1)} collective-permute-done((bf16[4,7296]{1,0:T(4,128)(2,1)S(1)}, bf16[4,7296]{1,0:T(4,128)(2,1)S(1)}, u32[]{:S(2)}, u32[]{:S(2)}) %collective-permute-start.1) | collective-permute-done | bytes 58400 | tf_op jit(solution)/shard_map/ppermute | solution.py:10
  14.2 2.4 %collective-permute-done.2 = bf16[4,7296]{1,0:T(4,128)(2,1)S(1)} collective-permute-done((bf16[4,7296]{1,0:T(4,128)(2,1)S(1)}, bf16[4,7296]{1,0:T(4,128)(2,1)S(1)}, u32[]{:S(2)}, u32[]{:S(2)}) %collective-permute-start.2) | collective-permute-done | bytes 58400 | tf_op jit(solution)/shard_map/ppermute | solution.py:10
  16.5 0.1 pad_maximum_fusion
  16.7 1.6 %collective-permute-start.3 = (bf16[16,7296]{1,0:T(8,128)(2,1)S(1)}, bf16[16,7296]{1,0:T(8,128)(2,1)S(1)}, u32[]{:S(2)}, u32[]{:S(2)}) collective-permute-start(bf16[16,7296]{1,0:T(8,128)(2,1)S(1)} %pad_maximum_fusion), channel_id=1, source_target_pairs={{0,8},{1,9},{2,10},{3,11},{4,12},{5,13},{6,14},{7,15},{8,0},{9,1},... | collective-permute-start | bytes 700424 | tf_op jit(solution)/shard_map/ppermute | solution.py:10
  18.2 4.6 %collective-permute-done.3 = bf16[16,7296]{1,0:T(8,128)(2,1)S(1)} collective-permute-done((bf16[16,7296]{1,0:T(8,128)(2,1)S(1)}, bf16[16,7296]{1,0:T(8,128)(2,1)S(1)}, u32[]{:S(2)}, u32[]{:S(2)}) %collective-permute-start.3) | collective-permute-done | bytes 233504 | tf_op jit(solution)/shard_map/ppermute | solution.py:10
  22.8 0.3 concatenate.16
  23.2 1.9 %copy.42 = bf16[4,7296]{0,1:T(8,128)(2,1)} copy(bf16[4,7296]{1,0:T(4,128)(2,1)S(1)} %collective-permute-done) | data formatting | bytes 116736 | tf_op jit(solution)/shard_map/ppermute | solution.py:10
  25.1 1.8 %copy.43 = bf16[4,7296]{0,1:T(8,128)(2,1)} copy(bf16[4,7296]{1,0:T(4,128)(2,1)S(1)} %collective-permute-done.1) | data formatting | bytes 116736 | tf_op jit(solution)/shard_map/ppermute | solution.py:10
  26.9 1.9 %copy.44 = bf16[4,7296]{0,1:T(8,128)(2,1)} copy(bf16[4,7296]{1,0:T(4,128)(2,1)S(1)} %collective-permute-done.2) | data formatting | bytes 116736 | tf_op jit(solution)/shard_map/ppermute | solution.py:10
  28.8 1.8 %copy.45 = bf16[16,7296]{0,1:T(8,128)(2,1)} copy(bf16[16,7296]{1,0:T(8,128)(2,1)S(1)} %collective-permute-done.3) | data formatting | bytes 466944 | tf_op jit(solution)/shard_map/ppermute | solution.py:10
  30.6 1.9 %copy.46 = bf16[32,7296]{0,1:T(8,128)(2,1)} copy(bf16[32,7296]{1,0:T(8,128)(2,1)S(1)} %collective-permute-done.4) | data formatting | bytes 933888 | tf_op jit(solution)/shard_map/ppermute | solution.py:10
  32.5 11.7 %concatenate.17 = bf16[64,7296]{0,1:T(8,128)(2,1)} concatenate(bf16[4,7296]{0,1:T(8,128)(2,1)S(1)} %convolution_convert_fusion, bf16[4,7296]{0,1:T(8,128)(2,1)} %copy.42, bf16[4,7296]{0,1:T(8,128)(2,1)} %copy.43, bf16[4,7296]{0,1:T(8,128)(2,1)} %copy.44, bf16[16,7296]{0,1:T(8,128)(2,1)} %copy.45, bf16[32,7296]{0,1:T(8,128)(2,1)} %copy.46), dimensions={0} | concatenate | bytes 1867776 | tf_op jit(solution)/shard_map/concatenate | solution.py:39
  44.2 8.3 %fusion = f32[64,2,2,256]{3,0,2,1:T(8,128)S(1)} fusion(bf16[2,7168,2,256]{3,2,1,0:T(2,128)(2,1)} %param.10, bf16[64,7296]{0,1:T(8,128)(2,1)} %concatenate.17), kind=kOutput, calls=%fused_computation | convolution fusion | flops 939524096 | bytes 16777216 | tf_op jit(solution)/shard_map/rd,edgf->regf/dot_general | solution.py:47
  52.5 4.5 %fusion.2 = bf16[64,7168]{1,0:T(8,128)(2,1)S(1)} fusion(bf16[2,256,7168]{2,1,0:T(8,128)(2,1)} %param.11, f32[64,2,2,256]{3,0,2,1:T(8,128)S(1)} %fusion, f32[64,2]{0,1:T(2,128)S(1)} %fusion.16), kind=kOutput, calls=%fused_computation.4 | convolution fusion | flops 470450176 | bytes 8520192 | tf_op jit(solution)/shard_map/dot_general | solution.py:55
  57.1 0.5 collective-permute-start.5
  57.6 1.4 %collective-permute-done.5 = bf16[32,7168]{1,0:T(8,128)(2,1)S(1)} collective-permute-done((bf16[32,7168]{1,0:T(8,128)(2,1)S(1)}, bf16[32,7168]{1,0:T(8,128)(2,1)S(1)}, u32[]{:S(2)}, u32[]{:S(2)}) %collective-permute-start.5) | collective-permute-done | bytes 458784 | tf_op jit(solution)/shard_map/ppermute | solution.py:10
  59.1 0.1 add_convert_fusion
  59.2 1.6 %collective-permute-start.6 = (bf16[16,7168]{1,0:T(8,128)(2,1)S(1)}, bf16[16,7168]{1,0:T(8,128)(2,1)S(1)}, u32[]{:S(2)}, u32[]{:S(2)}) collective-permute-start(bf16[16,7168]{1,0:T(8,128)(2,1)S(1)} %slice.55), channel_id=1, source_target_pairs={{0,8},{1,9},{2,10},{3,11},{4,12},{5,13},{6,14},{7,15},{8,0},{9,1},... | collective-permute-start | bytes 688136 | tf_op jit(solution)/shard_map/ppermute | solution.py:10
  60.8 6.4 %collective-permute-done.6 = bf16[16,7168]{1,0:T(8,128)(2,1)S(1)} collective-permute-done((bf16[16,7168]{1,0:T(8,128)(2,1)S(1)}, bf16[16,7168]{1,0:T(8,128)(2,1)S(1)}, u32[]{:S(2)}, u32[]{:S(2)}) %collective-permute-start.6) | collective-permute-done | bytes 229408 | tf_op jit(solution)/shard_map/ppermute | solution.py:10
  67.4 1.9 %collective-permute-start.8 = (bf16[4,7168]{1,0:T(4,128)(2,1)S(1)}, bf16[4,7168]{1,0:T(4,128)(2,1)S(1)}, u32[]{:S(2)}, u32[]{:S(2)}) collective-permute-start(bf16[4,7168]{1,0:T(4,128)(2,1)S(1)} %get-tuple-element.7), channel_id=1, source_target_pairs={{0,2},{1,3},{2,0},{3,1},{4,6},{5,7},{6,4},{7,5},{8,10},{9,11},{10,... | collective-permute-start | bytes 172040 | tf_op jit(solution)/shard_map/ppermute | solution.py:10
  69.3 2.5 %collective-permute-start.9 = (bf16[4,7168]{1,0:T(4,128)(2,1)S(1)}, bf16[4,7168]{1,0:T(4,128)(2,1)S(1)}, u32[]{:S(2)}, u32[]{:S(2)}) collective-permute-start(bf16[4,7168]{1,0:T(4,128)(2,1)S(1)} %get-tuple-element.6), channel_id=1, source_target_pairs={{0,3},{1,2},{2,1},{3,0},{4,7},{5,6},{6,5},{7,4},{8,11},{9,10},{10,... | collective-permute-start | bytes 172040 | tf_op jit(solution)/shard_map/ppermute | solution.py:10
  71.8 2.9 %collective-permute-done.8 = bf16[4,7168]{1,0:T(4,128)(2,1)S(1)} collective-permute-done((bf16[4,7168]{1,0:T(4,128)(2,1)S(1)}, bf16[4,7168]{1,0:T(4,128)(2,1)S(1)}, u32[]{:S(2)}, u32[]{:S(2)}) %collective-permute-start.8) | collective-permute-done | bytes 57376 | tf_op jit(solution)/shard_map/ppermute | solution.py:10
  74.7 0.6 collective-permute-done.9
  75.3 0.7 add_convert_fusion.2
  (15 shorter events, 0.5 us)
Async XLA Ops:
  4.9 5.7 %collective-permute-start = (bf16[4,7296]{1,0:T(4,128)(2,1)S(1)}, bf16[4,7296]{1,0:T(4,128)(2,1)S(1)}, u32[]{:S(2)}, u32[]{:S(2)}) collective-permute-start(bf16[4,7296]{1,0:T(4,128)(2,1)S(1)} %copy.37), channel_id=1, source_target_pairs={{0,1},{1,0},{2,3},{3,2},{4,5},{5,4},{6,7},{7,6},{8,9},{9,8},{10,11... | collective-permute-start | bytes 175112 | tf_op jit(solution)/shard_map/ppermute | solution.py:10
  7.9 6.2 %collective-permute-start.1 = (bf16[4,7296]{1,0:T(4,128)(2,1)S(1)}, bf16[4,7296]{1,0:T(4,128)(2,1)S(1)}, u32[]{:S(2)}, u32[]{:S(2)}) collective-permute-start(bf16[4,7296]{1,0:T(4,128)(2,1)S(1)} %copy.37), channel_id=1, source_target_pairs={{0,2},{1,3},{2,0},{3,1},{4,6},{5,7},{6,4},{7,5},{8,10},{9,11},{10,... | collective-permute-start | bytes 175112 | tf_op jit(solution)/shard_map/ppermute | solution.py:10
  10.5 6.0 %collective-permute-start.2 = (bf16[4,7296]{1,0:T(4,128)(2,1)S(1)}, bf16[4,7296]{1,0:T(4,128)(2,1)S(1)}, u32[]{:S(2)}, u32[]{:S(2)}) collective-permute-start(bf16[4,7296]{1,0:T(4,128)(2,1)S(1)} %copy.37), channel_id=1, source_target_pairs={{0,3},{1,2},{2,1},{3,0},{4,7},{5,6},{6,5},{7,4},{8,11},{9,10},{10,... | collective-permute-start | bytes 175112 | tf_op jit(solution)/shard_map/ppermute | solution.py:10
  16.7 6.1 %collective-permute-start.3 = (bf16[16,7296]{1,0:T(8,128)(2,1)S(1)}, bf16[16,7296]{1,0:T(8,128)(2,1)S(1)}, u32[]{:S(2)}, u32[]{:S(2)}) collective-permute-start(bf16[16,7296]{1,0:T(8,128)(2,1)S(1)} %pad_maximum_fusion), channel_id=1, source_target_pairs={{0,8},{1,9},{2,10},{3,11},{4,12},{5,13},{6,14},{7,15},{8,0},{9,1},... | collective-permute-start | bytes 700424 | tf_op jit(solution)/shard_map/ppermute | solution.py:10
  23.1 7.5 %collective-permute-start.4 = (bf16[32,7296]{1,0:T(8,128)(2,1)S(1)}, bf16[32,7296]{1,0:T(8,128)(2,1)S(1)}, u32[]{:S(2)}, u32[]{:S(2)}) collective-permute-start(bf16[32,7296]{1,0:T(8,128)(2,1)S(1)} %concatenate.16), channel_id=1, source_target_pairs={{0,4},{1,5},{2,6},{3,7},{4,0},{5,1},{6,2},{7,3},{8,12},{9,13},{10,... | collective-permute-start | bytes 1400840 | tf_op jit(solution)/shard_map/ppermute | solution.py:10
  44.2 8.3 %slice-start = ((bf16[64,7296]{0,1:T(8,128)(2,1)}), bf16[64,8]{0,1:T(8,128)(2,1)S(1)}, s32[]{:S(2)}) async-start(bf16[64,7296]{0,1:T(8,128)(2,1)} %concatenate.17), calls=%async_computation | async-start | bytes 4096 | tf_op jit(solution)/shard_map/slice | solution.py:43
  57.1 2.0 %collective-permute-start.5 = (bf16[32,7168]{1,0:T(8,128)(2,1)S(1)}, bf16[32,7168]{1,0:T(8,128)(2,1)S(1)}, u32[]{:S(2)}, u32[]{:S(2)}) collective-permute-start(bf16[32,7168]{1,0:T(8,128)(2,1)S(1)} %slice.53), channel_id=1, source_target_pairs={{0,4},{1,5},{2,6},{3,7},{4,0},{5,1},{6,2},{7,3},{8,12},{9,13},{10,... | collective-permute-start | bytes 1376264 | tf_op jit(solution)/shard_map/ppermute | solution.py:10
  59.2 7.9 %collective-permute-start.6 = (bf16[16,7168]{1,0:T(8,128)(2,1)S(1)}, bf16[16,7168]{1,0:T(8,128)(2,1)S(1)}, u32[]{:S(2)}, u32[]{:S(2)}) collective-permute-start(bf16[16,7168]{1,0:T(8,128)(2,1)S(1)} %slice.55), channel_id=1, source_target_pairs={{0,8},{1,9},{2,10},{3,11},{4,12},{5,13},{6,14},{7,15},{8,0},{9,1},... | collective-permute-start | bytes 688136 | tf_op jit(solution)/shard_map/ppermute | solution.py:10
  67.3 4.5 %collective-permute-start.7 = (bf16[4,7168]{1,0:T(4,128)(2,1)S(1)}, bf16[4,7168]{1,0:T(4,128)(2,1)S(1)}, u32[]{:S(2)}, u32[]{:S(2)}) collective-permute-start(bf16[4,7168]{1,0:T(4,128)(2,1)S(1)} %get-tuple-element.5), channel_id=1, source_target_pairs={{0,1},{1,0},{2,3},{3,2},{4,5},{5,4},{6,7},{7,6},{8,9},{9,8},{10,11... | collective-permute-start | bytes 172040 | tf_op jit(solution)/shard_map/ppermute | solution.py:10
  67.4 7.3 %collective-permute-start.8 = (bf16[4,7168]{1,0:T(4,128)(2,1)S(1)}, bf16[4,7168]{1,0:T(4,128)(2,1)S(1)}, u32[]{:S(2)}, u32[]{:S(2)}) collective-permute-start(bf16[4,7168]{1,0:T(4,128)(2,1)S(1)} %get-tuple-element.7), channel_id=1, source_target_pairs={{0,2},{1,3},{2,0},{3,1},{4,6},{5,7},{6,4},{7,5},{8,10},{9,11},{10,... | collective-permute-start | bytes 172040 | tf_op jit(solution)/shard_map/ppermute | solution.py:10
  69.3 6.1 %collective-permute-start.9 = (bf16[4,7168]{1,0:T(4,128)(2,1)S(1)}, bf16[4,7168]{1,0:T(4,128)(2,1)S(1)}, u32[]{:S(2)}, u32[]{:S(2)}) collective-permute-start(bf16[4,7168]{1,0:T(4,128)(2,1)S(1)} %get-tuple-element.6), channel_id=1, source_target_pairs={{0,3},{1,2},{2,1},{3,0},{4,7},{5,6},{6,5},{7,4},{8,11},{9,10},{10,... | collective-permute-start | bytes 172040 | tf_op jit(solution)/shard_map/ppermute | solution.py:10

commit v2 on v1

v2 whole, which is shorter than its diff:
```python
import functools

import jax
import jax.numpy as jnp
from jax import lax
from jax.experimental import pallas as pl
from jax.experimental.pallas import tpu as pltpu
from jax.sharding import PartitionSpec as P

AXES = ("node", "local")
VMEM = pltpu.VMEM
LANES = 128
BUFFERS = 3


def swap(value, mask, count):
    return lax.ppermute(value, AXES, [(i, i ^ mask) for i in range(count)])


def in_vmem(count):
    return [pl.BlockSpec(memory_space=VMEM)] * count


def pack_kernel(tokens, gates, nodes, out):
    rows, width = tokens.shape
    chosen = gates.shape[1]
    slots = nodes.shape[0]
    out[:, :width] = tokens[...]
    tail = jnp.concatenate(
        [gates[...].astype(jnp.float32), jnp.zeros((rows, LANES - chosen), jnp.float32)], axis=1
    )
    row = lax.broadcasted_iota(jnp.int32, (rows, LANES), 0)
    lane = lax.broadcasted_iota(jnp.int32, (rows, LANES), 1)
    for r in range(rows):
        for j in range(slots):
            tail = jnp.where(
                (row == r) & (lane == chosen + j), nodes[j, r].astype(jnp.float32), tail
            )
    out[:, width:] = tail.astype(jnp.bfloat16)


def pack(tokens, gates, node_list):
    rows, width = tokens.shape
    return pl.pallas_call(
        pack_kernel,
        out_shape=jax.ShapeDtypeStruct((rows, width + LANES), jnp.bfloat16),
        in_specs=in_vmem(2) + [pl.BlockSpec(memory_space=pltpu.SMEM)],
        out_specs=pl.BlockSpec(memory_space=VMEM),
    )(tokens, gates, node_list.T)


def sort_kernel(chunk, kinds, source, out, buffer, wide, sem):
    pair, total, _ = source.shape
    steps = total // chunk
    depth = chunk // kinds
    count = pair * steps

    def fetch(i, slot):
        start = pl.multiple_of(lax.rem(i, steps) * chunk, chunk)
        return pltpu.make_async_copy(
            source.at[i // steps, pl.ds(start, chunk)], buffer.at[slot], sem.at[slot]
        )

    for i in range(BUFFERS - 1):
        fetch(i, i).start()

    @pl.loop(0, count)
    def _(i):
        slot = lax.rem(i, BUFFERS)

        @pl.when(i + BUFFERS - 1 < count)
        def _():
            fetch(i + BUFFERS - 1, lax.rem(i + BUFFERS - 1, BUFFERS)).start()

        fetch(i, slot).wait()
        wide[...] = buffer[slot].astype(jnp.float32)
        at = pl.multiple_of(lax.rem(i, steps) * depth, depth)
        for k in range(kinds):
            column = (k % 2) * (kinds // 2) + k // 2
            out[i // steps, pl.ds(at, depth), column * LANES : (column + 1) * LANES] = wide[
                pl.ds(k, depth, stride=kinds), :
            ].astype(jnp.bfloat16)


def sort_weights(weight):
    pair, depth, two, units = weight.shape
    blocks = units // LANES
    kinds = two * blocks
    view = (
        weight.reshape(pair, depth, two, blocks, LANES)
        .transpose(0, 1, 3, 2, 4)
        .reshape(pair, depth * kinds, LANES)
    )
    chunk = 1024 * kinds
    return pl.pallas_call(
        functools.partial(sort_kernel, chunk, kinds),
        out_shape=VMEM((pair, depth, two * units), jnp.bfloat16),
        in_specs=[pl.BlockSpec(memory_space=pl.ANY)],
        out_specs=pl.BlockSpec(memory_space=VMEM),
        scratch_shapes=[
            VMEM((BUFFERS, chunk, LANES), jnp.bfloat16),
            VMEM((chunk, LANES), jnp.float32),
            pltpu.SemaphoreType.DMA((BUFFERS,)),
        ],
        compiler_params=pltpu.CompilerParams(vmem_limit_bytes=12 << 20),
        cost_estimate=pl.CostEstimate(flops=0, bytes_accessed=weight.size * 4, transcendentals=0),
    )(view)


def expert_kernel(chosen, near, far, weight_in, weight_out, out, held, hidden):
    half = near.shape[0]
    pair, depth, columns = weight_in.shape
    units = columns // 2
    slots = chosen // pair
    held[:half] = near[...]
    held[half:] = far[...]
    rows = held[:, :depth]
    tail = held[:, depth:].astype(jnp.float32)
    node = lax.axis_index("node").astype(jnp.float32)
    for e in range(pair):
        gate = jnp.zeros((2 * half, 1), jnp.float32)
        for j in range(slots):
            listed = tail[:, chosen + j : chosen + j + 1] == node
            gate = gate + jnp.where(listed, tail[:, pair * j + e : pair * j + e + 1], 0.0)
        first = jnp.dot(rows, weight_in[e, :, :units], preferred_element_type=jnp.float32)
        second = jnp.dot(rows, weight_in[e, :, units:], preferred_element_type=jnp.float32)
        active = first / (1.0 + jnp.exp(-first)) * second * gate
        hidden[:, e * units : (e + 1) * units] = active.astype(jnp.bfloat16)
    tile = 512

    @pl.loop(0, depth // tile)
    def _(i):
        at = pl.multiple_of(i * tile, tile)
        out[:, pl.ds(at, tile)] = jnp.dot(
            hidden[...], weight_out[:, pl.ds(at, tile)], preferred_element_type=jnp.float32
        ).astype(jnp.bfloat16)


def experts(chosen, near, far, weight_in, weight_out):
    half = near.shape[0]
    pair, depth, columns = weight_in.shape
    weight_out = weight_out.reshape(-1, depth)
    held = [pltpu.with_memory_space_constraint(a, VMEM) for a in (near, far, weight_in, weight_out)]
    return pl.pallas_call(
        functools.partial(expert_kernel, chosen),
        out_shape=VMEM((2 * half, depth), jnp.bfloat16),
        in_specs=in_vmem(4),
        out_specs=pl.BlockSpec(memory_space=VMEM),
        scratch_shapes=[
            VMEM((2 * half, near.shape[1]), jnp.bfloat16),
            VMEM((2 * half, weight_out.shape[0]), jnp.bfloat16),
        ],
        compiler_params=pltpu.CompilerParams(vmem_limit_bytes=16 << 20),
        cost_estimate=pl.CostEstimate(
            flops=6 * half * weight_in.size, bytes_accessed=1 << 20, transcendentals=0
        ),
    )(*held)


def finish_kernel(count, source, *refs):
    out = refs[count]
    total = sum(r[...].astype(jnp.float32) for r in refs[:count])
    rows = total.shape[0]
    picked = []
    for r in range(rows):
        line = total[0:1]
        for k in range(1, rows):
            line = jnp.where(source[0, r] == k, total[k : k + 1], line)
        picked.append(line)
    out[...] = jnp.concatenate(picked, axis=0).astype(jnp.bfloat16)


def finish(row_source, parts):
    return pl.pallas_call(
        functools.partial(finish_kernel, len(parts)),
        out_shape=jax.ShapeDtypeStruct(parts[0].shape, jnp.bfloat16),
        in_specs=[pl.BlockSpec(memory_space=pltpu.SMEM)] + in_vmem(len(parts)),
        out_specs=pl.BlockSpec(memory_space=VMEM),
    )(row_source, *parts)


def shards(tokens, node_list, gates, row_source, expert_in, expert_out):
    rows, width = tokens.shape
    nodes = lax.axis_size("node")
    locals_ = lax.axis_size("local")
    count = nodes * locals_
    weight_in = sort_weights(expert_in)
    message = pack(tokens, gates, node_list)
    along = jnp.concatenate(
        [message] + [swap(message, k, count) for k in range(1, locals_)], axis=0
    )
    across = jnp.concatenate(
        [along] + [swap(along, k * 2 * locals_, count) for k in range(1, nodes // 2)], axis=0
    )
    out = experts(gates.shape[1], across, swap(across, locals_, count), weight_in, expert_out)
    half = across.shape[0]
    out = (
        out[:half].astype(jnp.float32) + swap(out[half:], locals_, count).astype(jnp.float32)
    ).astype(jnp.bfloat16)
    step = rows * locals_
    parts = [out[:step]] + [
        swap(out[k * step : (k + 1) * step], k * 2 * locals_, count) for k in range(1, nodes // 2)
    ]
    out = sum(p.astype(jnp.float32) for p in parts).astype(jnp.bfloat16)
    parts = [out[:rows]] + [
        swap(out[k * rows : (k + 1) * rows], k, count) for k in range(1, locals_)
    ]
    return finish(row_source, parts)


def solution(mesh):
    spec = P(("groups", "node", "local"), None)
    return jax.shard_map(
        shards,
        mesh=mesh,
        in_specs=(spec, spec, spec, spec, P("node", None, None, "local"), P("node", "local", None)),
        out_specs=spec,
        check_vma=False,
    )
```

time: 76.5 us -> 59.2 us (0.77)
  local copies, waits for them, and re-layouts: 23.7 us -> 7.63 us
  Pallas kernels: 0 us -> 14.8 us
  matrix products: 14.5 us -> 0 us
  other arithmetic: 1.92 us -> 1.13 us
    pallas_call x0 -> x4, Pallas kernels: none -> 14.8 us  [the longest x1 6.04 us: sort_weights(): pl.pallas_call(functools.partial(sort_kernel, chunk, kinds), out_shape=VM...]
    dot_general x3 -> x0, matrix products: 14.5 us -> none  [the longest x1 8.29 us: shards(): jnp.einsum('rd,edgf->regf', everything[:, :width], expert_in, preferred_e...]
    concatenate x1 -> x0, local copies, waits for them, and re-layouts: 11.7 us -> none  [shards(): everything = jnp.concatenate([across, swap(across, locals_, count)], axis=0)]
    ppermute x5 -> x0, local copies, waits for them, and re-layouts: 9.33 us -> none  [swap(): return lax.ppermute(value, AXES, [(i, i ^ mask) for i in range(count)])]
    unnamed x1 -> x10, local copies, waits for them, and re-layouts: 0.1 us -> 5.82 us
    convert_element_type x2 -> x0, local copies, waits for them, and re-layouts: 2.09 us -> none  [the longest x1 1.32 us: shards(): jnp.dot(pick, message, preferred_element_type=jnp.float32)]
    convert_element_type x3 -> x0, other arithmetic: 1.44 us -> none  [the longest x1 0.75 us: shards(): (node_list[:, :, None] == jnp.arange(nodes, dtype=jnp.int32)).astype(jnp....]
    concatenate x1, other arithmetic: 0.14 us -> 0.96 us  [shards(): jnp.concatenate([message] + [swap(message, k, count) for k in range(1, lo...]
  transfers between devices with their start and end apart: 10 -> 10, of which waited for: 7 -> 7; matrix products, arithmetic and copies ran while one was open for 10% -> 0% of each run, Pallas kernels for 0% -> 10%
where the time goes in v2:
time: 59.2 us; the launch traced here: 58.9 us
  waiting for transfers between devices  21.3 us (36%)
  Pallas kernels  14.8 us (25%)
  starting transfers between devices  13.9 us (23%)
  local copies, waits for them, and re-layouts  7.63 us (13%)
  other arithmetic  1.13 us (2%)
    ppermute x10, waiting for transfers between devices, swap(): return lax.ppermute(value, AXES, [(i, i ^ mask) for i in range(count)])  21.3 us
    ppermute x10, starting transfers between devices, swap(): return lax.ppermute(value, AXES, [(i, i ^ mask) for i in range(count)])  13.9 us
    pallas_call x1, Pallas kernels, sort_weights(): pl.pallas_call(functools.partial(sort_kernel, chunk, kinds), out_shape=VM...  6.04 us
    unnamed x10, local copies, waits for them, and re-layouts  5.82 us
    pallas_call x1, Pallas kernels, experts(): pl.pallas_call(functools.partial(expert_kernel, chosen), out_shape=VMEM((...  5.61 us
    pallas_call x1, Pallas kernels, finish(): pl.pallas_call(functools.partial(finish_kernel, len(parts)), out_shape=ja...  1.71 us
    pallas_call x1, Pallas kernels, pack(): pl.pallas_call(pack_kernel, out_shape=jax.ShapeDtypeStruct((rows, width +...  1.46 us
  transfers between devices with their start and end apart: 10, of which 7 were waited for; matrix products, arithmetic and copies ran while one was open for 0% of the time, Pallas kernels for 10%

profile of v2, /device:TPU:0, one launch (start us, length us, event | category | flops | bytes accessed | tf_op | source)
XLA Modules:
  0.0 58.9 jit_solution(7034805556461362420)
XLA Ops:
  0.0 1.5 %shard_map.64 = bf16[4,7296]{1,0:T(4,128)(2,1)} custom-call(bf16[4,7168]{1,0:T(4,128)(2,1)} %tokens.1, bf16[4,4]{1,0:T(4,128)(2,1)} %gates.1, s32[2,4]{1,0:T(2,128)} %bitcast.9), custom_call_target="tpu_custom_call" | custom-call | tf_op jit(solution)/shard_map/pallas_call | solution.py:44
  1.5 5.0 %collective-permute-start.2 = (bf16[4,7296]{1,0:T(4,128)(2,1)}, bf16[4,7296]{1,0:T(4,128)(2,1)S(1)}, u32[]{:S(2)}, u32[]{:S(2)}) collective-permute-start(bf16[4,7296]{1,0:T(4,128)(2,1)} %shard_map.64), channel_id=1, source_target_pairs={{0,3},{1,2},{2,1},{3,0},{4,7},{5,6},{6,5},{7,4},{8,11},{9,10},{10,... | collective-permute-start | bytes 175112 | tf_op jit(solution)/shard_map/ppermute | solution.py:17
  6.5 0.0 collective-permute-start.1
  6.5 0.6 collective-permute-start
  7.1 2.1 %collective-permute-done.2 = bf16[4,7296]{1,0:T(4,128)(2,1)S(1)} collective-permute-done((bf16[4,7296]{1,0:T(4,128)(2,1)}, bf16[4,7296]{1,0:T(4,128)(2,1)S(1)}, u32[]{:S(2)}, u32[]{:S(2)}) %collective-permute-start.2) | collective-permute-done | bytes 58400 | tf_op jit(solution)/shard_map/ppermute | solution.py:17
  9.2 2.6 %collective-permute-done.1 = bf16[4,7296]{1,0:T(4,128)(2,1)S(1)} collective-permute-done((bf16[4,7296]{1,0:T(4,128)(2,1)}, bf16[4,7296]{1,0:T(4,128)(2,1)S(1)}, u32[]{:S(2)}, u32[]{:S(2)}) %collective-permute-start.1) | collective-permute-done | bytes 58400 | tf_op jit(solution)/shard_map/ppermute | solution.py:17
  11.8 0.0 collective-permute-done
  11.8 1.0 %pad_maximum_fusion = bf16[16,7296]{1,0:T(8,128)(2,1)S(1)} fusion(bf16[4,7296]{1,0:T(4,128)(2,1)S(1)} %collective-permute-done.2, bf16[4,7296]{1,0:T(4,128)(2,1)S(1)} %collective-permute-done.1, bf16[4,7296]{1,0:T(4,128)(2,1)S(1)} %collective-permute-done, bf16[4,7296]{1,0:T(4,128)(2,1)} %shard_map.64), kind=kLoop, calls=%fused_computation.2 | loop fusion | flops 933888 | bytes 466944 | tf_op jit(solution)/shard_map/concatenate | solution.py:189
  12.8 1.6 %collective-permute-start.3 = (bf16[16,7296]{1,0:T(8,128)(2,1)S(1)}, bf16[16,7296]{1,0:T(8,128)(2,1)S(1)}, u32[]{:S(2)}, u32[]{:S(2)}) collective-permute-start(bf16[16,7296]{1,0:T(8,128)(2,1)S(1)} %pad_maximum_fusion), channel_id=1, source_target_pairs={{0,8},{1,9},{2,10},{3,11},{4,12},{5,13},{6,14},{7,15},{8,0},{9,1},... | collective-permute-start | bytes 700424 | tf_op jit(solution)/shard_map/ppermute | solution.py:17
  14.4 5.2 %collective-permute-done.3 = bf16[16,7296]{1,0:T(8,128)(2,1)S(1)} collective-permute-done((bf16[16,7296]{1,0:T(8,128)(2,1)S(1)}, bf16[16,7296]{1,0:T(8,128)(2,1)S(1)}, u32[]{:S(2)}, u32[]{:S(2)}) %collective-permute-start.3) | collective-permute-done | bytes 233504 | tf_op jit(solution)/shard_map/ppermute | solution.py:17
  19.6 1.1 %concatenate.8.near = bf16[32,7296]{1,0:T(8,128)(2,1)S(1)} concatenate(bf16[4,7296]{1,0:T(4,128)(2,1)} %shard_map.64, bf16[4,7296]{1,0:T(4,128)(2,1)S(1)} %collective-permute-done, bf16[4,7296]{1,0:T(4,128)(2,1)S(1)} %collective-permute-done.1, bf16[4,7296]{1,0:T(4,128)(2,1)S(1)} %collective-permute-done.2, bf16[16,7296]{1,0:T(8,128)(2,1)S(1)} %collective-permute-done.3), dimensions={0} | concatenate | bytes 933888 | tf_op jit(solution)/shard_map/concatenate | solution.py:192
  20.7 0.1 collective-permute-start.4
  20.8 0.0 copy-start
  20.8 5.2 %copy-done = bf16[2,7168,2,256]{3,2,1,0:T(2,128)(2,1)S(1)} copy-done((bf16[2,7168,2,256]{3,2,1,0:T(2,128)(2,1)S(1)}, bf16[2,7168,2,256]{3,2,1,0:T(2,128)(2,1)}, u32[]{:S(2)}) %copy-start) | copy-done | bytes 14680088
  26.0 6.0 %shard_map.65.weight_in = bf16[2,7168,512]{2,1,0:T(8,128)(2,1)S(1)} custom-call(bf16[2,28672,128]{2,1,0:T(8,128)(2,1)S(1)} %bitcast.7), custom_call_target="tpu_custom_call" | custom-call | bytes 29360128 | tf_op jit(solution)/shard_map/pallas_call | solution.py:95
  32.0 0.0 collective-permute-done.4.far
  32.0 5.6 %shard_map.66 = bf16[64,7168]{1,0:T(8,128)(2,1)S(1)} custom-call(bf16[32,7296]{1,0:T(8,128)(2,1)S(1)} %concatenate.8.near, bf16[32,7296]{1,0:T(8,128)(2,1)S(1)} %collective-permute-done.4.far, bf16[2,7168,512]{2,1,0:T(8,128)(2,1)S(1)} %shard_map.65.weight_in, bf16[512,7168]{1,0:T(8,128)(2,1)S(1)} %bitcast.8), custom_call_target="tpu_custom_call" | custom-call | flops 1409286144 | bytes 1048576 | tf_op jit(solution)/shard_map/pallas_call | solution.py:144
  37.7 0.6 collective-permute-start.5
  38.3 1.4 %collective-permute-done.5 = bf16[32,7168]{1,0:T(8,128)(2,1)S(1)} collective-permute-done((bf16[32,7168]{1,0:T(8,128)(2,1)S(1)}, bf16[32,7168]{1,0:T(8,128)(2,1)S(1)}, u32[]{:S(2)}, u32[]{:S(2)}) %collective-permute-start.5) | collective-permute-done | bytes 458784 | tf_op jit(solution)/shard_map/ppermute | solution.py:17
  39.7 0.1 add_convert_fusion
  39.8 1.7 %collective-permute-start.6 = (bf16[16,7168]{1,0:T(8,128)(2,1)S(1)}, bf16[16,7168]{1,0:T(8,128)(2,1)S(1)}, u32[]{:S(2)}, u32[]{:S(2)}) collective-permute-start(bf16[16,7168]{1,0:T(8,128)(2,1)S(1)} %slice.35), channel_id=1, source_target_pairs={{0,8},{1,9},{2,10},{3,11},{4,12},{5,13},{6,14},{7,15},{8,0},{9,1},... | collective-permute-start | bytes 688136 | tf_op jit(solution)/shard_map/ppermute | solution.py:17
  41.5 6.3 %collective-permute-done.6 = bf16[16,7168]{1,0:T(8,128)(2,1)S(1)} collective-permute-done((bf16[16,7168]{1,0:T(8,128)(2,1)S(1)}, bf16[16,7168]{1,0:T(8,128)(2,1)S(1)}, u32[]{:S(2)}, u32[]{:S(2)}) %collective-permute-start.6) | collective-permute-done | bytes 229408 | tf_op jit(solution)/shard_map/ppermute | solution.py:17
  47.8 0.1 add_convert_fusion.1
  47.8 0.7 %fusion = (bf16[4,7168]{1,0:T(4,128)(2,1)S(1)}, bf16[4,7168]{1,0:T(4,128)(2,1)S(1)}, bf16[4,7168]{1,0:T(4,128)(2,1)S(1)}, bf16[4,7168]{1,0:T(4,128)(2,1)}) fusion(bf16[16,7168]{1,0:T(8,128)(2,1)S(1)} %add_convert_fusion.1), kind=kLoop, calls=%fused_computation.3 | loop fusion | bytes 458752 | tf_op jit(solution)/shard_map/slice | solution.py:206
  48.5 1.9 %collective-permute-start.9 = (bf16[4,7168]{1,0:T(4,128)(2,1)S(1)}, bf16[4,7168]{1,0:T(4,128)(2,1)S(1)}, u32[]{:S(2)}, u32[]{:S(2)}) collective-permute-start(bf16[4,7168]{1,0:T(4,128)(2,1)S(1)} %get-tuple-element.5), channel_id=1, source_target_pairs={{0,3},{1,2},{2,1},{3,0},{4,7},{5,6},{6,5},{7,4},{8,11},{9,10},{10,... | collective-permute-start | bytes 172040 | tf_op jit(solution)/shard_map/ppermute | solution.py:17
  50.4 0.2 collective-permute-start.8
  50.7 2.3 %collective-permute-start.7 = (bf16[4,7168]{1,0:T(4,128)(2,1)S(1)}, bf16[4,7168]{1,0:T(4,128)(2,1)S(1)}, u32[]{:S(2)}, u32[]{:S(2)}) collective-permute-start(bf16[4,7168]{1,0:T(4,128)(2,1)S(1)} %get-tuple-element.7), channel_id=1, source_target_pairs={{0,1},{1,0},{2,3},{3,2},{4,5},{5,4},{6,7},{7,6},{8,9},{9,8},{10,11... | collective-permute-start | bytes 172040 | tf_op jit(solution)/shard_map/ppermute | solution.py:17
  52.9 1.8 %collective-permute-done.9.refs_3_ = bf16[4,7168]{1,0:T(4,128)(2,1)S(1)} collective-permute-done((bf16[4,7168]{1,0:T(4,128)(2,1)S(1)}, bf16[4,7168]{1,0:T(4,128)(2,1)S(1)}, u32[]{:S(2)}, u32[]{:S(2)}) %collective-permute-start.9) | collective-permute-done | bytes 57376 | tf_op jit(solution)/shard_map/ppermute | solution.py:17
  54.8 1.7 %collective-permute-done.8.refs_2_ = bf16[4,7168]{1,0:T(4,128)(2,1)S(1)} collective-permute-done((bf16[4,7168]{1,0:T(4,128)(2,1)S(1)}, bf16[4,7168]{1,0:T(4,128)(2,1)S(1)}, u32[]{:S(2)}, u32[]{:S(2)}) %collective-permute-start.8) | collective-permute-done | bytes 57376 | tf_op jit(solution)/shard_map/ppermute | solution.py:17
  56.5 0.6 %copy-done.3 = bf16[4,7168]{1,0:T(4,128)(2,1)} copy-done((bf16[4,7168]{1,0:T(4,128)(2,1)}, bf16[4,7168]{1,0:T(4,128)(2,1)S(1)}, u32[]{:S(2)}) %copy-start.3) | copy-done | bytes 57368
  57.1 0.0 copy-done.4
  57.2 1.7 %shard_map.67 = bf16[4,7168]{1,0:T(4,128)(2,1)} custom-call(s32[1,4]{1,0:T(1,128)} %source.1, bf16[4,7168]{1,0:T(4,128)(2,1)} %get-tuple-element.8.refs_0_, bf16[4,7168]{1,0:T(4,128)(2,1)} %copy-done.4, bf16[4,7168]{1,0:T(4,128)(2,1)} %copy-done.3, bf16[4,7168]{1,0:T(4,128)(2,1)} %copy-done.2), custom_call_target="tpu_custom_call" | custom-call | tf_op jit(solution)/shard_map/pallas_call | solution.py:174
  (9 shorter events, 0.1 us)
Async XLA Ops:
  1.5 7.7 %collective-permute-start.2 = (bf16[4,7296]{1,0:T(4,128)(2,1)}, bf16[4,7296]{1,0:T(4,128)(2,1)S(1)}, u32[]{:S(2)}, u32[]{:S(2)}) collective-permute-start(bf16[4,7296]{1,0:T(4,128)(2,1)} %shard_map.64), channel_id=1, source_target_pairs={{0,3},{1,2},{2,1},{3,0},{4,7},{5,6},{6,5},{7,4},{8,11},{9,10},{10,... | collective-permute-start | bytes 175112 | tf_op jit(solution)/shard_map/ppermute | solution.py:17
  6.5 5.3 %collective-permute-start.1 = (bf16[4,7296]{1,0:T(4,128)(2,1)}, bf16[4,7296]{1,0:T(4,128)(2,1)S(1)}, u32[]{:S(2)}, u32[]{:S(2)}) collective-permute-start(bf16[4,7296]{1,0:T(4,128)(2,1)} %shard_map.64), channel_id=1, source_target_pairs={{0,2},{1,3},{2,0},{3,1},{4,6},{5,7},{6,4},{7,5},{8,10},{9,11},{10,... | collective-permute-start | bytes 175112 | tf_op jit(solution)/shard_map/ppermute | solution.py:17
  6.5 5.3 %collective-permute-start = (bf16[4,7296]{1,0:T(4,128)(2,1)}, bf16[4,7296]{1,0:T(4,128)(2,1)S(1)}, u32[]{:S(2)}, u32[]{:S(2)}) collective-permute-start(bf16[4,7296]{1,0:T(4,128)(2,1)} %shard_map.64), channel_id=1, source_target_pairs={{0,1},{1,0},{2,3},{3,2},{4,5},{5,4},{6,7},{7,6},{8,9},{9,8},{10,11... | collective-permute-start | bytes 175112 | tf_op jit(solution)/shard_map/ppermute | solution.py:17
  12.8 6.8 %collective-permute-start.3 = (bf16[16,7296]{1,0:T(8,128)(2,1)S(1)}, bf16[16,7296]{1,0:T(8,128)(2,1)S(1)}, u32[]{:S(2)}, u32[]{:S(2)}) collective-permute-start(bf16[16,7296]{1,0:T(8,128)(2,1)S(1)} %pad_maximum_fusion), channel_id=1, source_target_pairs={{0,8},{1,9},{2,10},{3,11},{4,12},{5,13},{6,14},{7,15},{8,0},{9,1},... | collective-permute-start | bytes 700424 | tf_op jit(solution)/shard_map/ppermute | solution.py:17
  20.7 11.3 %collective-permute-start.4 = (bf16[32,7296]{1,0:T(8,128)(2,1)S(1)}, bf16[32,7296]{1,0:T(8,128)(2,1)S(1)}, u32[]{:S(2)}, u32[]{:S(2)}) collective-permute-start(bf16[32,7296]{1,0:T(8,128)(2,1)S(1)} %concatenate.8.near), channel_id=1, source_target_pairs={{0,4},{1,5},{2,6},{3,7},{4,0},{5,1},{6,2},{7,3},{8,12},{9,13},{10,... | collective-permute-start | bytes 1400840 | tf_op jit(solution)/shard_map/ppermute | solution.py:17
  20.8 5.2 %copy-start = (bf16[2,7168,2,256]{3,2,1,0:T(2,128)(2,1)S(1)}, bf16[2,7168,2,256]{3,2,1,0:T(2,128)(2,1)}, u32[]{:S(2)}) copy-start(bf16[2,7168,2,256]{3,2,1,0:T(2,128)(2,1)} %param.10) | copy-start | bytes 44040196
  26.0 6.1 %copy-start.1 = (bf16[2,256,7168]{2,1,0:T(8,128)(2,1)S(1)}, bf16[2,256,7168]{2,1,0:T(8,128)(2,1)}, u32[]{:S(2)}) copy-start(bf16[2,256,7168]{2,1,0:T(8,128)(2,1)} %param.11) | copy-start | bytes 22020100
  37.7 2.0 %collective-permute-start.5 = (bf16[32,7168]{1,0:T(8,128)(2,1)S(1)}, bf16[32,7168]{1,0:T(8,128)(2,1)S(1)}, u32[]{:S(2)}, u32[]{:S(2)}) collective-permute-start(bf16[32,7168]{1,0:T(8,128)(2,1)S(1)} %slice.33), channel_id=1, source_target_pairs={{0,4},{1,5},{2,6},{3,7},{4,0},{5,1},{6,2},{7,3},{8,12},{9,13},{10,... | collective-permute-start | bytes 1376264 | tf_op jit(solution)/shard_map/ppermute | solution.py:17
  39.8 7.9 %collective-permute-start.6 = (bf16[16,7168]{1,0:T(8,128)(2,1)S(1)}, bf16[16,7168]{1,0:T(8,128)(2,1)S(1)}, u32[]{:S(2)}, u32[]{:S(2)}) collective-permute-start(bf16[16,7168]{1,0:T(8,128)(2,1)S(1)} %slice.35), channel_id=1, source_target_pairs={{0,8},{1,9},{2,10},{3,11},{4,12},{5,13},{6,14},{7,15},{8,0},{9,1},... | collective-permute-start | bytes 688136 | tf_op jit(solution)/shard_map/ppermute | solution.py:17
  48.5 6.2 %collective-permute-start.9 = (bf16[4,7168]{1,0:T(4,128)(2,1)S(1)}, bf16[4,7168]{1,0:T(4,128)(2,1)S(1)}, u32[]{:S(2)}, u32[]{:S(2)}) collective-permute-start(bf16[4,7168]{1,0:T(4,128)(2,1)S(1)} %get-tuple-element.5), channel_id=1, source_target_pairs={{0,3},{1,2},{2,1},{3,0},{4,7},{5,6},{6,5},{7,4},{8,11},{9,10},{10,... | collective-permute-start | bytes 172040 | tf_op jit(solution)/shard_map/ppermute | solution.py:17
  50.4 6.1 %collective-permute-start.8 = (bf16[4,7168]{1,0:T(4,128)(2,1)S(1)}, bf16[4,7168]{1,0:T(4,128)(2,1)S(1)}, u32[]{:S(2)}, u32[]{:S(2)}) collective-permute-start(bf16[4,7168]{1,0:T(4,128)(2,1)S(1)} %get-tuple-element.6), channel_id=1, source_target_pairs={{0,2},{1,3},{2,0},{3,1},{4,6},{5,7},{6,4},{7,5},{8,10},{9,11},{10,... | collective-permute-start | bytes 172040 | tf_op jit(solution)/shard_map/ppermute | solution.py:17
  50.7 5.8 %collective-permute-start.7 = (bf16[4,7168]{1,0:T(4,128)(2,1)S(1)}, bf16[4,7168]{1,0:T(4,128)(2,1)S(1)}, u32[]{:S(2)}, u32[]{:S(2)}) collective-permute-start(bf16[4,7168]{1,0:T(4,128)(2,1)S(1)} %get-tuple-element.7), channel_id=1, source_target_pairs={{0,1},{1,0},{2,3},{3,2},{4,5},{5,4},{6,7},{7,6},{8,9},{9,8},{10,11... | collective-permute-start | bytes 172040 | tf_op jit(solution)/shard_map/ppermute | solution.py:17
  54.8 1.8 %copy-start.2 = (bf16[4,7168]{1,0:T(4,128)(2,1)}, bf16[4,7168]{1,0:T(4,128)(2,1)S(1)}, u32[]{:S(2)}) copy-start(bf16[4,7168]{1,0:T(4,128)(2,1)S(1)} %collective-permute-done.9.refs_3_) | copy-start | bytes 172036
  56.5 0.6 %copy-start.3 = (bf16[4,7168]{1,0:T(4,128)(2,1)}, bf16[4,7168]{1,0:T(4,128)(2,1)S(1)}, u32[]{:S(2)}) copy-start(bf16[4,7168]{1,0:T(4,128)(2,1)S(1)} %collective-permute-done.8.refs_2_) | copy-start | bytes 172036
  56.5 0.6 %copy-start.4 = (bf16[4,7168]{1,0:T(4,128)(2,1)}, bf16[4,7168]{1,0:T(4,128)(2,1)S(1)}, u32[]{:S(2)}) copy-start(bf16[4,7168]{1,0:T(4,128)(2,1)S(1)} %collective-permute-done.7.refs_1_) | copy-start | bytes 172036

commit v3 on v2

v3 whole, which is shorter than its diff:
```python
import functools

import jax
import jax.numpy as jnp
from jax import lax
from jax.experimental import pallas as pl
from jax.experimental.pallas import tpu as pltpu
from jax.sharding import PartitionSpec as P

AXES = ("node", "local")
VMEM = pltpu.VMEM
LANES = 128
BUFFERS = 8
PIECE = 1024
SMALL = pltpu.CompilerParams(vmem_limit_bytes=4 << 20)


def swap(value, mask, count):
    return lax.ppermute(value, AXES, [(i, i ^ mask) for i in range(count)])


def in_vmem(count):
    return [pl.BlockSpec(memory_space=VMEM)] * count


def hold(*arrays):
    return [pltpu.with_memory_space_constraint(a, VMEM) for a in arrays]


def local_call(kernel, shapes, operands):
    return pl.pallas_call(
        kernel,
        out_shape=tuple(VMEM(s, jnp.bfloat16) for s in shapes),
        in_specs=in_vmem(len(operands)),
        out_specs=tuple(in_vmem(len(shapes))),
        compiler_params=SMALL,
    )(*hold(*operands))


def pack_kernel(tokens, gates, nodes, source, out):
    rows, width = tokens.shape
    chosen = gates.shape[1]
    slots = nodes.shape[0]
    out[:, :width] = tokens[...]
    tail = jnp.concatenate(
        [gates[...].astype(jnp.float32), jnp.zeros((rows, LANES - chosen), jnp.float32)], axis=1
    )
    row = lax.broadcasted_iota(jnp.int32, (rows, LANES), 0)
    lane = lax.broadcasted_iota(jnp.int32, (rows, LANES), 1)
    for r in range(rows):
        numbers = [nodes[j, r] for j in range(slots)] + [source[0, r]]
        for j, number in enumerate(numbers):
            tail = jnp.where((row == r) & (lane == chosen + j), number.astype(jnp.float32), tail)
    out[:, width:] = tail.astype(jnp.bfloat16)


def pack(tokens, gates, node_list, row_source):
    rows, width = tokens.shape
    return pl.pallas_call(
        pack_kernel,
        out_shape=VMEM((rows, width + LANES), jnp.bfloat16),
        in_specs=in_vmem(2) + [pl.BlockSpec(memory_space=pltpu.SMEM)] * 2,
        out_specs=pl.BlockSpec(memory_space=VMEM),
    )(tokens, gates, node_list.T, row_source)


def sort_kernel(chunk, kinds, expert, source, out, token, buffer, wide, sem):
    _, total, _ = source.shape
    count = total // chunk
    depth = chunk // kinds

    def fetch(i, slot):
        start = pl.multiple_of(i * chunk, chunk)
        return pltpu.make_async_copy(
            source.at[expert, pl.ds(start, chunk)], buffer.at[slot], sem.at[slot]
        )

    for i in range(BUFFERS - 1):
        fetch(i, i).start()

    @pl.loop(0, count)
    def _(i):
        slot = lax.rem(i, BUFFERS)

        @pl.when(i + BUFFERS - 1 < count)
        def _():
            fetch(i + BUFFERS - 1, lax.rem(i + BUFFERS - 1, BUFFERS)).start()

        fetch(i, slot).wait()
        wide[...] = buffer[slot].astype(jnp.float32)
        at = pl.multiple_of(i * depth, depth)
        for k in range(kinds):
            column = (k % 2) * (kinds // 2) + k // 2
            out[pl.ds(at, depth), column * LANES : (column + 1) * LANES] = wide[
                pl.ds(k, depth, stride=kinds), :
            ].astype(jnp.bfloat16)

    token[...] = jnp.zeros_like(token)


def sort_weights(weight):
    pair, depth, two, units = weight.shape
    blocks = units // LANES
    kinds = two * blocks
    view = (
        weight.reshape(pair, depth, two, blocks, LANES)
        .transpose(0, 1, 3, 2, 4)
        .reshape(pair, depth * kinds, LANES)
    )
    chunk = 512 * kinds
    return [
        pl.pallas_call(
            functools.partial(sort_kernel, chunk, kinds, expert),
            out_shape=(VMEM((depth, two * units), jnp.bfloat16), VMEM((16, LANES), jnp.bfloat16)),
            in_specs=[pl.BlockSpec(memory_space=pltpu.HBM)],
            out_specs=tuple(in_vmem(2)),
            scratch_shapes=[
                VMEM((BUFFERS, chunk, LANES), jnp.bfloat16),
                VMEM((chunk, LANES), jnp.float32),
                pltpu.SemaphoreType.DMA((BUFFERS,)),
            ],
            compiler_params=pltpu.CompilerParams(vmem_limit_bytes=8 << 20),
            cost_estimate=pl.CostEstimate(
                flops=0, bytes_accessed=2 * weight.size, transcendentals=0
            ),
        )(pltpu.with_memory_space_constraint(view, pltpu.HBM))
        for expert in range(pair)
    ]


def expert_kernel(chosen, pair, rows, near, far, *refs):
    weight_in, weight_out = refs[:pair], refs[pair]
    near_out, far_out, held, hidden, down, sem = refs[pair + 1 :]
    half = near.shape[0]
    depth, columns = weight_in[0].shape
    units = columns // 2
    slots = chosen // pair
    total = 2 * half
    pieces = range(0, depth, PIECE)
    copies = [
        pltpu.make_async_copy(
            weight_out.at[:, pl.ds(at, PIECE)], down.at[:, pl.ds(at, PIECE)], sem.at[i]
        )
        for i, at in enumerate(pieces)
    ]
    for copy in copies:
        copy.start()
    held[:half] = near[...]
    held[half:] = far[...]
    tail = held[:, depth:].astype(jnp.float32)
    node = lax.axis_index("node").astype(jnp.float32)
    active = []
    for e in range(pair):
        gate = jnp.zeros((total, 1), jnp.float32)
        for j in range(slots):
            listed = tail[:, chosen + j : chosen + j + 1] == node
            gate = gate + jnp.where(listed, tail[:, pair * j + e : pair * j + e + 1], 0.0)
        first = jnp.dot(held[:, :depth], weight_in[e][:, :units], preferred_element_type=jnp.float32)
        second = jnp.dot(
            held[:, :depth], weight_in[e][:, units:], preferred_element_type=jnp.float32
        )
        active.append((first / (1.0 + jnp.exp(-first)) * second * gate).astype(jnp.bfloat16))
    row = lax.broadcasted_iota(jnp.int32, (total, total), 0)
    column = lax.broadcasted_iota(jnp.int32, (total, total), 1)
    source = tail[:, chosen + slots : chosen + slots + 1].astype(jnp.int32)
    order = (column == row - lax.rem(row, rows) + source).astype(jnp.bfloat16)
    hidden[...] = jnp.dot(
        order, jnp.concatenate(active, axis=1), preferred_element_type=jnp.float32
    ).astype(jnp.bfloat16)
    for copy, at in zip(copies, pieces):
        copy.wait()
        result = jnp.dot(
            hidden[...], down[:, at : at + PIECE], preferred_element_type=jnp.float32
        ).astype(jnp.bfloat16)
        near_out[:, at : at + PIECE] = result[:half]
        far_out[:, at : at + PIECE] = result[half:]


def experts(chosen, rows, near, far, weight_in, weight_out):
    half = near.shape[0]
    pair = len(weight_in)
    depth, columns = weight_in[0].shape
    weight_out = pltpu.with_memory_space_constraint(weight_out.reshape(-1, depth), pltpu.HBM)
    return pl.pallas_call(
        functools.partial(expert_kernel, chosen, pair, rows),
        out_shape=(VMEM((half, depth), jnp.bfloat16),) * 2,
        in_specs=in_vmem(2 + pair) + [pl.BlockSpec(memory_space=pltpu.HBM)],
        out_specs=tuple(in_vmem(2)),
        scratch_shapes=[
            VMEM((2 * half, near.shape[1]), jnp.bfloat16),
            VMEM((2 * half, weight_out.shape[0]), jnp.bfloat16),
            VMEM(weight_out.shape, jnp.bfloat16),
            pltpu.SemaphoreType.DMA((depth // PIECE,)),
        ],
        compiler_params=pltpu.CompilerParams(vmem_limit_bytes=24 << 20),
        cost_estimate=pl.CostEstimate(
            flops=6 * half * pair * weight_in[0].size, bytes_accessed=8 << 20, transcendentals=0
        ),
    )(*hold(near, far, *weight_in), weight_out)


def join(operands, *after):
    count = len(operands)

    def kernel(*refs):
        refs[-1][...] = jnp.concatenate([r[...] for r in refs[:count]], axis=0)

    shape = (sum(a.shape[0] for a in operands), operands[0].shape[1])
    return local_call(kernel, [shape], [*operands, *after])[0]


def fold_kernel(near, far, *outs):
    total = near[...].astype(jnp.float32) + far[...].astype(jnp.float32)
    at = 0
    for out in outs:
        out[...] = total[at : at + out.shape[0]].astype(jnp.bfloat16)
        at += out.shape[0]


def split_kernel(count, rows, head, head_got, *refs):
    top = head[...].astype(jnp.float32) + head_got[...].astype(jnp.float32)
    low = sum(r[...].astype(jnp.float32) for r in refs[:count])
    both = jnp.concatenate([top, low], axis=0)
    for i, out in enumerate(refs[count:]):
        out[...] = both[i * rows : (i + 1) * rows].astype(jnp.bfloat16)


def shards(tokens, node_list, gates, row_source, expert_in, expert_out):
    rows, width = tokens.shape
    nodes = lax.axis_size("node")
    locals_ = lax.axis_size("local")
    count = nodes * locals_
    step = 2 * locals_
    across = range(1, nodes // 2)
    beyond = range(2, locals_)
    message = pack(tokens, gates, node_list, row_source)
    (first, first_done), *later = sort_weights(expert_in)
    tail = [swap(message, k, count) for k in beyond]
    head = [message] + [swap(message, a * step, count) for a in across]
    head, tail = join(head, first_done), join(tail, first_done)
    near = [head, tail, swap(head, 1, count)] + [swap(tail, a * step, count) for a in across]
    near = join(near, *[done for _, done in later])
    near_out, far_out = experts(
        gates.shape[1],
        rows,
        near,
        swap(near, locals_, count),
        [first] + [w for w, _ in later],
        expert_out,
    )
    sizes = [head.shape[0], tail.shape[0], head.shape[0]] + [tail.shape[0]] * len(across)
    head, tail, side, *sides = local_call(
        fold_kernel, [(s, width) for s in sizes], [near_out, swap(far_out, locals_, count)]
    )
    head_got = swap(side, 1, count)
    tail_got = [swap(v, a * step, count) for a, v in zip(across, sides)]
    own, *others = local_call(
        functools.partial(split_kernel, 1 + len(across), rows),
        [(rows, width)] * (1 + len(across) + len(beyond)),
        [head, head_got, tail, *tail_got],
    )
    masks = [a * step for a in across] + list(beyond)
    got = [swap(v, m, count) for m, v in reversed(list(zip(masks, others)))]
    return sum(v.astype(jnp.float32) for v in [own, *got]).astype(jnp.bfloat16)


def solution(mesh):
    spec = P(("groups", "node", "local"), None)
    return jax.shard_map(
        shards,
        mesh=mesh,
        in_specs=(spec, spec, spec, spec, P("node", None, None, "local"), P("node", "local", None)),
        out_specs=spec,
        check_vma=False,
    )
```

time: 59.2 us -> 42.5 us (0.72)
  waiting for transfers between devices: 21.3 us -> 13.4 us
  local copies, waits for them, and re-layouts: 7.63 us -> 0 us
    ppermute x10 -> x12, waiting for transfers between devices: 21.3 us -> 13.4 us  [swap(): return lax.ppermute(value, AXES, [(i, i ^ mask) for i in range(count)])]
    unnamed x10 -> x0, local copies, waits for them, and re-layouts: 5.82 us -> none
    concatenate x1 -> x0, local copies, waits for them, and re-layouts: 1.07 us -> none  [shards(): jnp.concatenate([along] + [swap(along, k * 2 * locals_, count) for k in r...]
    concatenate x1 -> x0, other arithmetic: 0.96 us -> none  [shards(): jnp.concatenate([message] + [swap(message, k, count) for k in range(1, lo...]
    slice x3 -> x0, local copies, waits for them, and re-layouts: 0.74 us -> none  [the longest x1 0.69 us: shards(): out[k * rows:(k + 1) * rows]]
    pallas_call x4 -> x9, Pallas kernels: 14.8 us -> 14.3 us  [the longest x2 7.17 us: sort_weights(): pl.pallas_call(functools.partial(sort_kernel, chunk, kinds, expert), out_...]
    ppermute x10 -> x12, starting transfers between devices: 13.9 us -> 13.8 us  [swap(): return lax.ppermute(value, AXES, [(i, i ^ mask) for i in range(count)])]
  transfers between devices with their start and end apart: 10 -> 12, of which waited for: 7 -> 8; matrix products, arithmetic and copies ran while one was open for 0% -> 0% of each run, Pallas kernels for 10% -> 17%
where the time goes in v3:
time: 42.5 us; the launch traced here: 42.3 us
  Pallas kernels  14.3 us (34%)
  starting transfers between devices  13.8 us (32%)
  waiting for transfers between devices  13.4 us (32%)
  other arithmetic  0.69 us (2%)
    ppermute x12, starting transfers between devices, swap(): return lax.ppermute(value, AXES, [(i, i ^ mask) for i in range(count)])  13.8 us
    ppermute x12, waiting for transfers between devices, swap(): return lax.ppermute(value, AXES, [(i, i ^ mask) for i in range(count)])  13.4 us
    pallas_call x2, Pallas kernels, sort_weights(): pl.pallas_call(functools.partial(sort_kernel, chunk, kinds, expert), out_...  7.17 us
    pallas_call x1, Pallas kernels, experts(): pl.pallas_call(functools.partial(expert_kernel, chosen, pair, rows), out_...  5.98 us
    pallas_call x1, Pallas kernels, pack(): pl.pallas_call(pack_kernel, out_shape=VMEM((rows, width + LANES), jnp.bfl...  0.85 us
  transfers between devices with their start and end apart: 12, of which 8 were waited for; matrix products, arithmetic and copies ran while one was open for 0% of the time, Pallas kernels for 17%

profile of v3, /device:TPU:0, one launch (start us, length us, event | category | flops | bytes accessed | tf_op | source)
XLA Modules:
  0.0 42.3 jit_solution(17181023879985553177)
XLA Ops:
  0.0 0.9 %shard_map.64.refs_0_ = bf16[4,7296]{1,0:T(4,128)(2,1)S(1)} custom-call(bf16[4,7168]{1,0:T(4,128)(2,1)} %tokens.1, bf16[4,4]{1,0:T(4,128)(2,1)} %gates.1, s32[2,4]{1,0:T(2,128)} %bitcast.10, s32[1,4]{1,0:T(1,128)} %source.1), custom_call_target="tpu_custom_call" | custom-call | tf_op jit(solution)/shard_map/pallas_call | solution.py:59
  0.9 3.0 %collective-permute-start = (bf16[4,7296]{1,0:T(4,128)(2,1)S(1)}, bf16[4,7296]{1,0:T(4,128)(2,1)S(1)}, u32[]{:S(2)}, u32[]{:S(2)}) collective-permute-start(bf16[4,7296]{1,0:T(4,128)(2,1)S(1)} %shard_map.64.refs_0_), channel_id=1, source_target_pairs={{0,8},{1,9},{2,10},{3,11},{4,12},{5,13},{6,14},{7,15},{8,0},{9,1},... | collective-permute-start | bytes 175112 | tf_op jit(solution)/shard_map/ppermute | solution.py:19
  3.9 3.6 %collective-permute-start.2 = (bf16[4,7296]{1,0:T(4,128)(2,1)S(1)}, bf16[4,7296]{1,0:T(4,128)(2,1)S(1)}, u32[]{:S(2)}, u32[]{:S(2)}) collective-permute-start(bf16[4,7296]{1,0:T(4,128)(2,1)S(1)} %shard_map.64.refs_0_), channel_id=1, source_target_pairs={{0,3},{1,2},{2,1},{3,0},{4,7},{5,6},{6,5},{7,4},{8,11},{9,10},{10,... | collective-permute-start | bytes 175112 | tf_op jit(solution)/shard_map/ppermute | solution.py:19
  7.5 0.0 collective-permute-start.1
  7.5 3.6 %shard_map.65 = (bf16[7168,512]{1,0:T(8,128)(2,1)S(1)}, bf16[16,128]{1,0:T(8,128)(2,1)S(1)}) custom-call(bf16[2,28672,128]{2,1,0:T(8,128)(2,1)} %bitcast.7), custom_call_target="tpu_custom_call" | custom-call | bytes 14680064 | tf_op jit(solution)/shard_map/pallas_call | solution.py:112
  11.1 0.0 collective-permute-done.refs_1_
  11.1 0.8 %collective-permute-start.3 = (bf16[8,7296]{1,0:T(8,128)(2,1)S(1)}, bf16[8,7296]{1,0:T(8,128)(2,1)S(1)}, u32[]{:S(2)}, u32[]{:S(2)}) collective-permute-start(bf16[8,7296]{1,0:T(8,128)(2,1)S(1)} %shard_map.66.refs_0_), channel_id=1, source_target_pairs={{0,1},{1,0},{2,3},{3,2},{4,5},{5,4},{6,7},{7,6},{8,9},{9,8},{10,11... | collective-permute-start | bytes 350216 | tf_op jit(solution)/shard_map/ppermute | solution.py:19
  12.0 0.0 collective-permute-done.2.refs_1_
  12.0 0.6 %collective-permute-done.1.refs_0_ = bf16[4,7296]{1,0:T(4,128)(2,1)S(1)} collective-permute-done((bf16[4,7296]{1,0:T(4,128)(2,1)S(1)}, bf16[4,7296]{1,0:T(4,128)(2,1)S(1)}, u32[]{:S(2)}, u32[]{:S(2)}) %collective-permute-start.1) | collective-permute-done | bytes 58400 | tf_op jit(solution)/shard_map/ppermute | solution.py:19
  12.6 0.6 %collective-permute-start.4 = (bf16[8,7296]{1,0:T(8,128)(2,1)S(1)}, bf16[8,7296]{1,0:T(8,128)(2,1)S(1)}, u32[]{:S(2)}, u32[]{:S(2)}) collective-permute-start(bf16[8,7296]{1,0:T(8,128)(2,1)S(1)} %shard_map.67.refs_1_), channel_id=1, source_target_pairs={{0,8},{1,9},{2,10},{3,11},{4,12},{5,13},{6,14},{7,15},{8,0},{9,1},... | collective-permute-start | bytes 350216 | tf_op jit(solution)/shard_map/ppermute | solution.py:19
  13.2 3.6 %shard_map.68 = (bf16[7168,512]{1,0:T(8,128)(2,1)S(1)}, bf16[16,128]{1,0:T(8,128)(2,1)S(1)}) custom-call(bf16[2,28672,128]{2,1,0:T(8,128)(2,1)} %bitcast.8), custom_call_target="tpu_custom_call" | custom-call | bytes 14680064 | tf_op jit(solution)/shard_map/pallas_call | solution.py:112
  16.8 0.0 collective-permute-done.3.refs_2_
  16.8 0.7 %collective-permute-done.4.refs_3_ = bf16[8,7296]{1,0:T(8,128)(2,1)S(1)} collective-permute-done((bf16[8,7296]{1,0:T(8,128)(2,1)S(1)}, bf16[8,7296]{1,0:T(8,128)(2,1)S(1)}, u32[]{:S(2)}, u32[]{:S(2)}) %collective-permute-start.4) | collective-permute-done | bytes 116768 | tf_op jit(solution)/shard_map/ppermute | solution.py:19
  17.5 0.1 shard_map.69.near
  17.6 0.1 collective-permute-start.5
  17.6 1.8 %collective-permute-done.5.far = bf16[32,7296]{1,0:T(8,128)(2,1)S(1)} collective-permute-done((bf16[32,7296]{1,0:T(8,128)(2,1)S(1)}, bf16[32,7296]{1,0:T(8,128)(2,1)S(1)}, u32[]{:S(2)}, u32[]{:S(2)}) %collective-permute-start.5) | collective-permute-done | bytes 466976 | tf_op jit(solution)/shard_map/ppermute | solution.py:19
  19.4 6.0 %shard_map.70 = (bf16[32,7168]{1,0:T(8,128)(2,1)S(1)}, bf16[32,7168]{1,0:T(8,128)(2,1)S(1)}) custom-call(bf16[32,7296]{1,0:T(8,128)(2,1)S(1)} %shard_map.69.near, bf16[32,7296]{1,0:T(8,128)(2,1)S(1)} %collective-permute-done.5.far, bf16[7168,512]{1,0:T(8,128)(2,1)S(1)} %get-tuple-element.21.refs_0_, bf16[7168,512]{1,0:T(8,128)(2,1)S(1)} %get-tuple-element.22.refs_1_, ...), custom_call_target="tpu_custom_call" | custom-call | flops 1409286144 | bytes 8388608 | tf_op jit(solution)/shard_map/pallas_call | solution.py:184
  25.4 0.2 collective-permute-start.6
  25.6 1.7 %collective-permute-done.6.far = bf16[32,7168]{1,0:T(8,128)(2,1)S(1)} collective-permute-done((bf16[32,7168]{1,0:T(8,128)(2,1)S(1)}, bf16[32,7168]{1,0:T(8,128)(2,1)S(1)}, u32[]{:S(2)}, u32[]{:S(2)}) %collective-permute-start.6) | collective-permute-done | bytes 458784 | tf_op jit(solution)/shard_map/ppermute | solution.py:19
  27.3 0.1 shard_map.71
  27.4 0.7 %collective-permute-start.7 = (bf16[8,7168]{1,0:T(8,128)(2,1)S(1)}, bf16[8,7168]{1,0:T(8,128)(2,1)S(1)}, u32[]{:S(2)}, u32[]{:S(2)}) collective-permute-start(bf16[8,7168]{1,0:T(8,128)(2,1)S(1)} %get-tuple-element.26), channel_id=1, source_target_pairs={{0,1},{1,0},{2,3},{3,2},{4,5},{5,4},{6,7},{7,6},{8,9},{9,8},{10,11... | collective-permute-start | bytes 344072 | tf_op jit(solution)/shard_map/ppermute | solution.py:19
  28.1 0.8 %collective-permute-start.8 = (bf16[8,7168]{1,0:T(8,128)(2,1)S(1)}, bf16[8,7168]{1,0:T(8,128)(2,1)S(1)}, u32[]{:S(2)}, u32[]{:S(2)}) collective-permute-start(bf16[8,7168]{1,0:T(8,128)(2,1)S(1)} %get-tuple-element.28), channel_id=1, source_target_pairs={{0,8},{1,9},{2,10},{3,11},{4,12},{5,13},{6,14},{7,15},{8,0},{9,1},... | collective-permute-start | bytes 344072 | tf_op jit(solution)/shard_map/ppermute | solution.py:19
  29.0 3.7 %collective-permute-done.7.head_got = bf16[8,7168]{1,0:T(8,128)(2,1)S(1)} collective-permute-done((bf16[8,7168]{1,0:T(8,128)(2,1)S(1)}, bf16[8,7168]{1,0:T(8,128)(2,1)S(1)}, u32[]{:S(2)}, u32[]{:S(2)}) %collective-permute-start.7) | collective-permute-done | bytes 114720 | tf_op jit(solution)/shard_map/ppermute | solution.py:19
  32.7 0.4 collective-permute-done.8.refs_1_
  33.1 0.1 shard_map.72
  33.1 2.8 %collective-permute-start.9 = (bf16[4,7168]{1,0:T(4,128)(2,1)S(1)}, bf16[4,7168]{1,0:T(4,128)(2,1)S(1)}, u32[]{:S(2)}, u32[]{:S(2)}) collective-permute-start(bf16[4,7168]{1,0:T(4,128)(2,1)S(1)} %get-tuple-element.30), channel_id=1, source_target_pairs={{0,3},{1,2},{2,1},{3,0},{4,7},{5,6},{6,5},{7,4},{8,11},{9,10},{10,... | collective-permute-start | bytes 172040 | tf_op jit(solution)/shard_map/ppermute | solution.py:19
  35.9 0.3 collective-permute-start.10
  36.2 0.8 %collective-permute-start.11 = (bf16[4,7168]{1,0:T(4,128)(2,1)S(1)}, bf16[4,7168]{1,0:T(4,128)(2,1)S(1)}, u32[]{:S(2)}, u32[]{:S(2)}) collective-permute-start(bf16[4,7168]{1,0:T(4,128)(2,1)S(1)} %get-tuple-element.32), channel_id=1, source_target_pairs={{0,8},{1,9},{2,10},{3,11},{4,12},{5,13},{6,14},{7,15},{8,0},{9,1},... | collective-permute-start | bytes 172040 | tf_op jit(solution)/shard_map/ppermute | solution.py:19
  37.0 2.6 %collective-permute-done.9 = bf16[4,7168]{1,0:T(4,128)(2,1)S(1)} collective-permute-done((bf16[4,7168]{1,0:T(4,128)(2,1)S(1)}, bf16[4,7168]{1,0:T(4,128)(2,1)S(1)}, u32[]{:S(2)}, u32[]{:S(2)}) %collective-permute-start.9) | collective-permute-done | bytes 57376 | tf_op jit(solution)/shard_map/ppermute | solution.py:19
  39.7 2.0 %collective-permute-done.10 = bf16[4,7168]{1,0:T(4,128)(2,1)S(1)} collective-permute-done((bf16[4,7168]{1,0:T(4,128)(2,1)S(1)}, bf16[4,7168]{1,0:T(4,128)(2,1)S(1)}, u32[]{:S(2)}, u32[]{:S(2)}) %collective-permute-start.10) | collective-permute-done | bytes 57376 | tf_op jit(solution)/shard_map/ppermute | solution.py:19
  41.6 0.0 collective-permute-done.11
  41.6 0.7 %add_convert_fusion = bf16[4,7168]{1,0:T(4,128)(2,1)} fusion(bf16[4,7168]{1,0:T(4,128)(2,1)S(1)} %collective-permute-done.11, bf16[4,7168]{1,0:T(4,128)(2,1)S(1)} %collective-permute-done.10, bf16[4,7168]{1,0:T(4,128)(2,1)S(1)} %collective-permute-done.9, bf16[4,7168]{1,0:T(4,128)(2,1)S(1)} %get-tuple-element.29), kind=kLoop, calls=%fused_computation | loop fusion | flops 229376 | bytes 286720 | tf_op jit(solution)/shard_map/convert_element_type | solution.py:264
  (2 shorter events, 0.1 us)
Async XLA Ops:
  0.9 10.2 %collective-permute-start = (bf16[4,7296]{1,0:T(4,128)(2,1)S(1)}, bf16[4,7296]{1,0:T(4,128)(2,1)S(1)}, u32[]{:S(2)}, u32[]{:S(2)}) collective-permute-start(bf16[4,7296]{1,0:T(4,128)(2,1)S(1)} %shard_map.64.refs_0_), channel_id=1, source_target_pairs={{0,8},{1,9},{2,10},{3,11},{4,12},{5,13},{6,14},{7,15},{8,0},{9,1},... | collective-permute-start | bytes 175112 | tf_op jit(solution)/shard_map/ppermute | solution.py:19
  3.9 8.1 %collective-permute-start.2 = (bf16[4,7296]{1,0:T(4,128)(2,1)S(1)}, bf16[4,7296]{1,0:T(4,128)(2,1)S(1)}, u32[]{:S(2)}, u32[]{:S(2)}) collective-permute-start(bf16[4,7296]{1,0:T(4,128)(2,1)S(1)} %shard_map.64.refs_0_), channel_id=1, source_target_pairs={{0,3},{1,2},{2,1},{3,0},{4,7},{5,6},{6,5},{7,4},{8,11},{9,10},{10,... | collective-permute-start | bytes 175112 | tf_op jit(solution)/shard_map/ppermute | solution.py:19
  7.5 5.1 %collective-permute-start.1 = (bf16[4,7296]{1,0:T(4,128)(2,1)S(1)}, bf16[4,7296]{1,0:T(4,128)(2,1)S(1)}, u32[]{:S(2)}, u32[]{:S(2)}) collective-permute-start(bf16[4,7296]{1,0:T(4,128)(2,1)S(1)} %shard_map.64.refs_0_), channel_id=1, source_target_pairs={{0,2},{1,3},{2,0},{3,1},{4,6},{5,7},{6,4},{7,5},{8,10},{9,11},{10,... | collective-permute-start | bytes 175112 | tf_op jit(solution)/shard_map/ppermute | solution.py:19
  11.1 5.7 %collective-permute-start.3 = (bf16[8,7296]{1,0:T(8,128)(2,1)S(1)}, bf16[8,7296]{1,0:T(8,128)(2,1)S(1)}, u32[]{:S(2)}, u32[]{:S(2)}) collective-permute-start(bf16[8,7296]{1,0:T(8,128)(2,1)S(1)} %shard_map.66.refs_0_), channel_id=1, source_target_pairs={{0,1},{1,0},{2,3},{3,2},{4,5},{5,4},{6,7},{7,6},{8,9},{9,8},{10,11... | collective-permute-start | bytes 350216 | tf_op jit(solution)/shard_map/ppermute | solution.py:19
  12.6 4.9 %collective-permute-start.4 = (bf16[8,7296]{1,0:T(8,128)(2,1)S(1)}, bf16[8,7296]{1,0:T(8,128)(2,1)S(1)}, u32[]{:S(2)}, u32[]{:S(2)}) collective-permute-start(bf16[8,7296]{1,0:T(8,128)(2,1)S(1)} %shard_map.67.refs_1_), channel_id=1, source_target_pairs={{0,8},{1,9},{2,10},{3,11},{4,12},{5,13},{6,14},{7,15},{8,0},{9,1},... | collective-permute-start | bytes 350216 | tf_op jit(solution)/shard_map/ppermute | solution.py:19
  17.6 1.9 %collective-permute-start.5 = (bf16[32,7296]{1,0:T(8,128)(2,1)S(1)}, bf16[32,7296]{1,0:T(8,128)(2,1)S(1)}, u32[]{:S(2)}, u32[]{:S(2)}) collective-permute-start(bf16[32,7296]{1,0:T(8,128)(2,1)S(1)} %shard_map.69.near), channel_id=1, source_target_pairs={{0,4},{1,5},{2,6},{3,7},{4,0},{5,1},{6,2},{7,3},{8,12},{9,13},{10,... | collective-permute-start | bytes 1400840 | tf_op jit(solution)/shard_map/ppermute | solution.py:19
  25.4 1.9 %collective-permute-start.6 = (bf16[32,7168]{1,0:T(8,128)(2,1)S(1)}, bf16[32,7168]{1,0:T(8,128)(2,1)S(1)}, u32[]{:S(2)}, u32[]{:S(2)}) collective-permute-start(bf16[32,7168]{1,0:T(8,128)(2,1)S(1)} %get-tuple-element.24), channel_id=1, source_target_pairs={{0,4},{1,5},{2,6},{3,7},{4,0},{5,1},{6,2},{7,3},{8,12},{9,13},{10,... | collective-permute-start | bytes 1376264 | tf_op jit(solution)/shard_map/ppermute | solution.py:19
  27.4 5.3 %collective-permute-start.7 = (bf16[8,7168]{1,0:T(8,128)(2,1)S(1)}, bf16[8,7168]{1,0:T(8,128)(2,1)S(1)}, u32[]{:S(2)}, u32[]{:S(2)}) collective-permute-start(bf16[8,7168]{1,0:T(8,128)(2,1)S(1)} %get-tuple-element.26), channel_id=1, source_target_pairs={{0,1},{1,0},{2,3},{3,2},{4,5},{5,4},{6,7},{7,6},{8,9},{9,8},{10,11... | collective-permute-start | bytes 344072 | tf_op jit(solution)/shard_map/ppermute | solution.py:19
  28.1 4.9 %collective-permute-start.8 = (bf16[8,7168]{1,0:T(8,128)(2,1)S(1)}, bf16[8,7168]{1,0:T(8,128)(2,1)S(1)}, u32[]{:S(2)}, u32[]{:S(2)}) collective-permute-start(bf16[8,7168]{1,0:T(8,128)(2,1)S(1)} %get-tuple-element.28), channel_id=1, source_target_pairs={{0,8},{1,9},{2,10},{3,11},{4,12},{5,13},{6,14},{7,15},{8,0},{9,1},... | collective-permute-start | bytes 344072 | tf_op jit(solution)/shard_map/ppermute | solution.py:19
  33.1 6.5 %collective-permute-start.9 = (bf16[4,7168]{1,0:T(4,128)(2,1)S(1)}, bf16[4,7168]{1,0:T(4,128)(2,1)S(1)}, u32[]{:S(2)}, u32[]{:S(2)}) collective-permute-start(bf16[4,7168]{1,0:T(4,128)(2,1)S(1)} %get-tuple-element.30), channel_id=1, source_target_pairs={{0,3},{1,2},{2,1},{3,0},{4,7},{5,6},{6,5},{7,4},{8,11},{9,10},{10,... | collective-permute-start | bytes 172040 | tf_op jit(solution)/shard_map/ppermute | solution.py:19
  35.9 5.7 %collective-permute-start.10 = (bf16[4,7168]{1,0:T(4,128)(2,1)S(1)}, bf16[4,7168]{1,0:T(4,128)(2,1)S(1)}, u32[]{:S(2)}, u32[]{:S(2)}) collective-permute-start(bf16[4,7168]{1,0:T(4,128)(2,1)S(1)} %get-tuple-element.31), channel_id=1, source_target_pairs={{0,2},{1,3},{2,0},{3,1},{4,6},{5,7},{6,4},{7,5},{8,10},{9,11},{10,... | collective-permute-start | bytes 172040 | tf_op jit(solution)/shard_map/ppermute | solution.py:19
  36.2 5.4 %collective-permute-start.11 = (bf16[4,7168]{1,0:T(4,128)(2,1)S(1)}, bf16[4,7168]{1,0:T(4,128)(2,1)S(1)}, u32[]{:S(2)}, u32[]{:S(2)}) collective-permute-start(bf16[4,7168]{1,0:T(4,128)(2,1)S(1)} %get-tuple-element.32), channel_id=1, source_target_pairs={{0,8},{1,9},{2,10},{3,11},{4,12},{5,13},{6,14},{7,15},{8,0},{9,1},... | collective-permute-start | bytes 172040 | tf_op jit(solution)/shard_map/ppermute | solution.py:19

commit v4 on v3

--- a/solution.py
+++ b/solution.py
@@ -12,6 +12,7 @@
 LANES = 128
 BUFFERS = 8
 PIECE = 1024
+EARLY = (2, 2)
 SMALL = pltpu.CompilerParams(vmem_limit_bytes=4 << 20)
 
 
@@ -64,7 +65,7 @@
     )(tokens, gates, node_list.T, row_source)
 
 
-def sort_kernel(chunk, kinds, expert, source, out, token, buffer, wide, sem):
+def sort_kernel(chunk, kinds, expert, start_at, source, down, out, part, buffer, wide, sem, down_sem):
     _, total, _ = source.shape
     count = total // chunk
     depth = chunk // kinds
@@ -77,6 +78,8 @@
 
     for i in range(BUFFERS - 1):
         fetch(i, i).start()
+    extra = pltpu.make_async_copy(down.at[:, pl.ds(start_at, part.shape[1])], part, down_sem)
+    extra.start()
 
     @pl.loop(0, count)
     def _(i):
@@ -95,10 +98,10 @@
                 pl.ds(k, depth, stride=kinds), :
             ].astype(jnp.bfloat16)
 
-    token[...] = jnp.zeros_like(token)
-
-
-def sort_weights(weight):
+    extra.wait()
+
+
+def sort_weights(weight, down):
     pair, depth, two, units = weight.shape
     blocks = units // LANES
     kinds = two * blocks
@@ -108,43 +111,41 @@
         .reshape(pair, depth * kinds, LANES)
     )
     chunk = 512 * kinds
+    down = down.reshape(-1, depth)
+    ends = [sum(EARLY[:e]) * PIECE for e in range(pair + 1)]
+    source = [pltpu.with_memory_space_constraint(a, pltpu.HBM) for a in (view, down)]
     return [
         pl.pallas_call(
-            functools.partial(sort_kernel, chunk, kinds, expert),
-            out_shape=(VMEM((depth, two * units), jnp.bfloat16), VMEM((16, LANES), jnp.bfloat16)),
-            in_specs=[pl.BlockSpec(memory_space=pltpu.HBM)],
+            functools.partial(sort_kernel, chunk, kinds, expert, ends[expert]),
+            out_shape=(
+                VMEM((depth, two * units), jnp.bfloat16),
+                VMEM((down.shape[0], ends[expert + 1] - ends[expert]), jnp.bfloat16),
+            ),
+            in_specs=[pl.BlockSpec(memory_space=pltpu.HBM)] * 2,
             out_specs=tuple(in_vmem(2)),
             scratch_shapes=[
                 VMEM((BUFFERS, chunk, LANES), jnp.bfloat16),
                 VMEM((chunk, LANES), jnp.float32),
                 pltpu.SemaphoreType.DMA((BUFFERS,)),
+                pltpu.SemaphoreType.DMA,
             ],
             compiler_params=pltpu.CompilerParams(vmem_limit_bytes=8 << 20),
             cost_estimate=pl.CostEstimate(
                 flops=0, bytes_accessed=2 * weight.size, transcendentals=0
             ),
-        )(pltpu.with_memory_space_constraint(view, pltpu.HBM))
+        )(*source)
         for expert in range(pair)
     ]
 
 
 def expert_kernel(chosen, pair, rows, near, far, *refs):
-    weight_in, weight_out = refs[:pair], refs[pair]
-    near_out, far_out, held, hidden, down, sem = refs[pair + 1 :]
+    weight_in, weight_out = refs[:pair], refs[pair:-4]
+    near_out, far_out, held, hidden = refs[-4:]
     half = near.shape[0]
     depth, columns = weight_in[0].shape
     units = columns // 2
     slots = chosen // pair
     total = 2 * half
-    pieces = range(0, depth, PIECE)
-    copies = [
-        pltpu.make_async_copy(
-            weight_out.at[:, pl.ds(at, PIECE)], down.at[:, pl.ds(at, PIECE)], sem.at[i]
-        )
-        for i, at in enumerate(pieces)
-    ]
-    for copy in copies:
-        copy.start()
     held[:half] = near[...]
     held[half:] = far[...]
     tail = held[:, depth:].astype(jnp.float32)
@@ -167,36 +168,61 @@
     hidden[...] = jnp.dot(
         order, jnp.concatenate(active, axis=1), preferred_element_type=jnp.float32
     ).astype(jnp.bfloat16)
-    for copy, at in zip(copies, pieces):
-        copy.wait()
-        result = jnp.dot(
-            hidden[...], down[:, at : at + PIECE], preferred_element_type=jnp.float32
-        ).astype(jnp.bfloat16)
-        near_out[:, at : at + PIECE] = result[:half]
-        far_out[:, at : at + PIECE] = result[half:]
+    at = 0
+    for down in weight_out:
+        for i in range(down.shape[1] // PIECE):
+            result = jnp.dot(
+                hidden[...],
+                down[:, i * PIECE : (i + 1) * PIECE],
+                preferred_element_type=jnp.float32,
+            ).astype(jnp.bfloat16)
+            near_out[:, at : at + PIECE] = result[:half]
+            far_out[:, at : at + PIECE] = result[half:]
+            at += PIECE
+
+
+def load_kernel(begin, source, after, out, sem):
+    copy = pltpu.make_async_copy(source.at[:, pl.ds(begin, out.shape[1])], out, sem)
+    copy.start()
+    copy.wait()
+
+
+def load(weight_out, begin, after):
+    weight_out = pltpu.with_memory_space_constraint(
+        weight_out.reshape(-1, weight_out.shape[-1]), pltpu.HBM
+    )
+    height, depth = weight_out.shape
+    return pl.pallas_call(
+        functools.partial(load_kernel, begin),
+        out_shape=VMEM((height, depth - begin), jnp.bfloat16),
+        in_specs=[pl.BlockSpec(memory_space=pltpu.HBM)] + in_vmem(1),
+        out_specs=pl.BlockSpec(memory_space=VMEM),
+        scratch_shapes=[pltpu.SemaphoreType.DMA],
+        compiler_params=SMALL,
+        cost_estimate=pl.CostEstimate(
+            flops=0, bytes_accessed=2 * height * (depth - begin), transcendentals=0
+        ),
+    )(weight_out, *hold(after))
 
 
 def experts(chosen, rows, near, far, weight_in, weight_out):
     half = near.shape[0]
     pair = len(weight_in)
     depth, columns = weight_in[0].shape
-    weight_out = pltpu.with_memory_space_constraint(weight_out.reshape(-1, depth), pltpu.HBM)
     return pl.pallas_call(
         functools.partial(expert_kernel, chosen, pair, rows),
         out_shape=(VMEM((half, depth), jnp.bfloat16),) * 2,
-        in_specs=in_vmem(2 + pair) + [pl.BlockSpec(memory_space=pltpu.HBM)],
+        in_specs=in_vmem(2 + pair + len(weight_out)),
         out_specs=tuple(in_vmem(2)),
         scratch_shapes=[
             VMEM((2 * half, near.shape[1]), jnp.bfloat16),
-            VMEM((2 * half, weight_out.shape[0]), jnp.bfloat16),
-            VMEM(weight_out.shape, jnp.bfloat16),
-            pltpu.SemaphoreType.DMA((depth // PIECE,)),
+            VMEM((2 * half, weight_out[0].shape[0]), jnp.bfloat16),
         ],
-        compiler_params=pltpu.CompilerParams(vmem_limit_bytes=24 << 20),
+        compiler_params=pltpu.CompilerParams(vmem_limit_bytes=20 << 20),
         cost_estimate=pl.CostEstimate(
             flops=6 * half * pair * weight_in[0].size, bytes_accessed=8 << 20, transcendentals=0
         ),
-    )(*hold(near, far, *weight_in), weight_out)
+    )(*hold(near, far, *weight_in, *weight_out))
 
 
 def join(operands, *after):
@@ -234,19 +260,15 @@
     across = range(1, nodes // 2)
     beyond = range(2, locals_)
     message = pack(tokens, gates, node_list, row_source)
-    (first, first_done), *later = sort_weights(expert_in)
+    weights, early = zip(*sort_weights(expert_in, expert_out))
     tail = [swap(message, k, count) for k in beyond]
     head = [message] + [swap(message, a * step, count) for a in across]
-    head, tail = join(head, first_done), join(tail, first_done)
+    head, tail = join(head, early[0]), join(tail, early[0])
     near = [head, tail, swap(head, 1, count)] + [swap(tail, a * step, count) for a in across]
-    near = join(near, *[done for _, done in later])
+    near = join(near, *early[1:])
+    late = load(expert_out, sum(a.shape[1] for a in early), near)
     near_out, far_out = experts(
-        gates.shape[1],
-        rows,
-        near,
-        swap(near, locals_, count),
-        [first] + [w for w, _ in later],
-        expert_out,
+        gates.shape[1], rows, near, swap(near, locals_, count), weights, (*early, late)
     )
     sizes = [head.shape[0], tail.shape[0], head.shape[0]] + [tail.shape[0]] * len(across)
     head, tail, side, *sides = local_call(

time: 42.5 us -> 41.7 us (0.981)
  waiting for transfers between devices: 13.4 us -> 9.26 us
  starting transfers between devices: 13.8 us -> 15.9 us
  Pallas kernels: 14.3 us -> 15.6 us
    ppermute x12, waiting for transfers between devices: 13.4 us -> 9.26 us  [swap(): return lax.ppermute(value, AXES, [(i, i ^ mask) for i in range(count)])]
    pallas_call x2 -> x3, Pallas kernels: 7.17 us -> 10.3 us  [the longest x2 8.36 us: sort_weights(): pl.pallas_call(functools.partial(sort_kernel, chunk, kinds, expert, ends[...]
    ppermute x12, starting transfers between devices: 13.8 us -> 15.9 us  [swap(): return lax.ppermute(value, AXES, [(i, i ^ mask) for i in range(count)])]
    pallas_call x1, Pallas kernels: 5.98 us -> 4.11 us  [experts(): pl.pallas_call(functools.partial(expert_kernel, chosen, pair, rows), out_...]
  transfers between devices with their start and end apart: 12 -> 12, of which waited for: 8 -> 6; matrix products, arithmetic and copies ran while one was open for 0% -> 0% of each run, Pallas kernels for 17% -> 25%
where the time goes in v4:
time: 41.7 us; the launch traced here: 41.5 us
  starting transfers between devices  15.9 us (38%)
  Pallas kernels  15.6 us (37%)
  waiting for transfers between devices  9.26 us (22%)
  other arithmetic  0.69 us (2%)
    ppermute x12, starting transfers between devices, swap(): return lax.ppermute(value, AXES, [(i, i ^ mask) for i in range(count)])  15.9 us
    ppermute x12, waiting for transfers between devices, swap(): return lax.ppermute(value, AXES, [(i, i ^ mask) for i in range(count)])  9.26 us
    pallas_call x2, Pallas kernels, sort_weights(): pl.pallas_call(functools.partial(sort_kernel, chunk, kinds, expert, ends[...  8.36 us
    pallas_call x1, Pallas kernels, experts(): pl.pallas_call(functools.partial(expert_kernel, chosen, pair, rows), out_...  4.11 us
    pallas_call x1, Pallas kernels, load(): pl.pallas_call(functools.partial(load_kernel, begin), out_shape=VMEM((hei...  1.9 us
    pallas_call x1, Pallas kernels, pack(): pl.pallas_call(pack_kernel, out_shape=VMEM((rows, width + LANES), jnp.bfl...  0.85 us
  transfers between devices with their start and end apart: 12, of which 6 were waited for; matrix products, arithmetic and copies ran while one was open for 0% of the time, Pallas kernels for 25%

profile of v4, /device:TPU:0, one launch (start us, length us, event | category | flops | bytes accessed | tf_op | source)
XLA Modules:
  0.0 41.5 jit_solution(4667601498439761168)
XLA Ops:
  0.0 0.9 %shard_map.64.refs_0_ = bf16[4,7296]{1,0:T(4,128)(2,1)S(1)} custom-call(bf16[4,7168]{1,0:T(4,128)(2,1)} %tokens.1, bf16[4,4]{1,0:T(4,128)(2,1)} %gates.1, s32[2,4]{1,0:T(2,128)} %bitcast.12, s32[1,4]{1,0:T(1,128)} %source.1), custom_call_target="tpu_custom_call" | custom-call | tf_op jit(solution)/shard_map/pallas_call | solution.py:60
  0.9 3.0 %collective-permute-start = (bf16[4,7296]{1,0:T(4,128)(2,1)S(1)}, bf16[4,7296]{1,0:T(4,128)(2,1)S(1)}, u32[]{:S(2)}, u32[]{:S(2)}) collective-permute-start(bf16[4,7296]{1,0:T(4,128)(2,1)S(1)} %shard_map.64.refs_0_), channel_id=1, source_target_pairs={{0,8},{1,9},{2,10},{3,11},{4,12},{5,13},{6,14},{7,15},{8,0},{9,1},... | collective-permute-start | bytes 175112 | tf_op jit(solution)/shard_map/ppermute | solution.py:20
  3.9 3.6 %collective-permute-start.2 = (bf16[4,7296]{1,0:T(4,128)(2,1)S(1)}, bf16[4,7296]{1,0:T(4,128)(2,1)S(1)}, u32[]{:S(2)}, u32[]{:S(2)}) collective-permute-start(bf16[4,7296]{1,0:T(4,128)(2,1)S(1)} %shard_map.64.refs_0_), channel_id=1, source_target_pairs={{0,3},{1,2},{2,1},{3,0},{4,7},{5,6},{6,5},{7,4},{8,11},{9,10},{10,... | collective-permute-start | bytes 175112 | tf_op jit(solution)/shard_map/ppermute | solution.py:20
  7.5 0.0 collective-permute-start.1
  7.5 4.2 %shard_map.65 = (bf16[7168,512]{1,0:T(8,128)(2,1)S(1)}, bf16[512,2048]{1,0:T(8,128)(2,1)S(1)}) custom-call(bf16[2,28672,128]{2,1,0:T(8,128)(2,1)} %bitcast.10, bf16[512,7168]{1,0:T(8,128)(2,1)} %bitcast.7), custom_call_target="tpu_custom_call" | custom-call | bytes 14680064 | tf_op jit(solution)/shard_map/pallas_call | solution.py:118
  11.7 0.0 collective-permute-done.refs_1_
  11.7 0.8 %collective-permute-start.3 = (bf16[8,7296]{1,0:T(8,128)(2,1)S(1)}, bf16[8,7296]{1,0:T(8,128)(2,1)S(1)}, u32[]{:S(2)}, u32[]{:S(2)}) collective-permute-start(bf16[8,7296]{1,0:T(8,128)(2,1)S(1)} %shard_map.66.refs_0_), channel_id=1, source_target_pairs={{0,1},{1,0},{2,3},{3,2},{4,5},{5,4},{6,7},{7,6},{8,9},{9,8},{10,11... | collective-permute-start | bytes 350216 | tf_op jit(solution)/shard_map/ppermute | solution.py:20
  12.6 0.0 collective-permute-done.2.refs_1_
  12.6 0.6 %collective-permute-start.4 = (bf16[8,7296]{1,0:T(8,128)(2,1)S(1)}, bf16[8,7296]{1,0:T(8,128)(2,1)S(1)}, u32[]{:S(2)}, u32[]{:S(2)}) collective-permute-start(bf16[8,7296]{1,0:T(8,128)(2,1)S(1)} %shard_map.67.refs_1_), channel_id=1, source_target_pairs={{0,8},{1,9},{2,10},{3,11},{4,12},{5,13},{6,14},{7,15},{8,0},{9,1},... | collective-permute-start | bytes 350216 | tf_op jit(solution)/shard_map/ppermute | solution.py:20
  13.2 4.2 %shard_map.68 = (bf16[7168,512]{1,0:T(8,128)(2,1)S(1)}, bf16[512,2048]{1,0:T(8,128)(2,1)S(1)}) custom-call(bf16[2,28672,128]{2,1,0:T(8,128)(2,1)} %bitcast.11, bf16[512,7168]{1,0:T(8,128)(2,1)} %bitcast.8), custom_call_target="tpu_custom_call" | custom-call | bytes 14680064 | tf_op jit(solution)/shard_map/pallas_call | solution.py:118
  17.4 0.0 collective-permute-done.3.refs_2_
  17.4 0.1 collective-permute-done.4.refs_3_
  17.5 0.1 shard_map.69.after.near
  17.6 0.1 collective-permute-start.5
  17.6 1.9 %shard_map.70.refs_4_ = bf16[512,3072]{1,0:T(8,128)(2,1)S(1)} custom-call(bf16[512,7168]{1,0:T(8,128)(2,1)} %bitcast.9, bf16[32,7296]{1,0:T(8,128)(2,1)S(1)} %shard_map.69.after.near), custom_call_target="tpu_custom_call" | custom-call | bytes 3145728 | tf_op jit(solution)/shard_map/pallas_call | solution.py:195
  19.6 0.0 collective-permute-done.5.far
  19.6 4.1 %shard_map.71 = (bf16[32,7168]{1,0:T(8,128)(2,1)S(1)}, bf16[32,7168]{1,0:T(8,128)(2,1)S(1)}) custom-call(bf16[32,7296]{1,0:T(8,128)(2,1)S(1)} %shard_map.69.after.near, bf16[32,7296]{1,0:T(8,128)(2,1)S(1)} %collective-permute-done.5.far, bf16[7168,512]{1,0:T(8,128)(2,1)S(1)} %get-tuple-element.21.refs_0_, bf16[7168,512]{1,0:T(8,128)(2,1)S(1)} %get-tuple-element.22.refs_1_, ...), custom_call_target="tpu_custom_call" | custom-call | flops 1409286144 | bytes 8388608 | tf_op jit(solution)/shard_map/pallas_call | solution.py:212
  23.7 0.6 %collective-permute-start.6 = (bf16[32,7168]{1,0:T(8,128)(2,1)S(1)}, bf16[32,7168]{1,0:T(8,128)(2,1)S(1)}, u32[]{:S(2)}, u32[]{:S(2)}) collective-permute-start(bf16[32,7168]{1,0:T(8,128)(2,1)S(1)} %get-tuple-element.24), channel_id=1, source_target_pairs={{0,4},{1,5},{2,6},{3,7},{4,0},{5,1},{6,2},{7,3},{8,12},{9,13},{10,... | collective-permute-start | bytes 1376264 | tf_op jit(solution)/shard_map/ppermute | solution.py:20
  24.2 1.4 %collective-permute-done.6.far = bf16[32,7168]{1,0:T(8,128)(2,1)S(1)} collective-permute-done((bf16[32,7168]{1,0:T(8,128)(2,1)S(1)}, bf16[32,7168]{1,0:T(8,128)(2,1)S(1)}, u32[]{:S(2)}, u32[]{:S(2)}) %collective-permute-start.6) | collective-permute-done | bytes 458784 | tf_op jit(solution)/shard_map/ppermute | solution.py:20
  25.7 0.1 shard_map.72
  25.8 1.3 %collective-permute-start.7 = (bf16[8,7168]{1,0:T(8,128)(2,1)S(1)}, bf16[8,7168]{1,0:T(8,128)(2,1)S(1)}, u32[]{:S(2)}, u32[]{:S(2)}) collective-permute-start(bf16[8,7168]{1,0:T(8,128)(2,1)S(1)} %get-tuple-element.26), channel_id=1, source_target_pairs={{0,1},{1,0},{2,3},{3,2},{4,5},{5,4},{6,7},{7,6},{8,9},{9,8},{10,11... | collective-permute-start | bytes 344072 | tf_op jit(solution)/shard_map/ppermute | solution.py:20
  27.1 1.4 %collective-permute-start.8 = (bf16[8,7168]{1,0:T(8,128)(2,1)S(1)}, bf16[8,7168]{1,0:T(8,128)(2,1)S(1)}, u32[]{:S(2)}, u32[]{:S(2)}) collective-permute-start(bf16[8,7168]{1,0:T(8,128)(2,1)S(1)} %get-tuple-element.28), channel_id=1, source_target_pairs={{0,8},{1,9},{2,10},{3,11},{4,12},{5,13},{6,14},{7,15},{8,0},{9,1},... | collective-permute-start | bytes 344072 | tf_op jit(solution)/shard_map/ppermute | solution.py:20
  28.5 2.7 %collective-permute-done.7.head_got = bf16[8,7168]{1,0:T(8,128)(2,1)S(1)} collective-permute-done((bf16[8,7168]{1,0:T(8,128)(2,1)S(1)}, bf16[8,7168]{1,0:T(8,128)(2,1)S(1)}, u32[]{:S(2)}, u32[]{:S(2)}) %collective-permute-start.7) | collective-permute-done | bytes 114720 | tf_op jit(solution)/shard_map/ppermute | solution.py:20
  31.3 1.0 %collective-permute-done.8.refs_1_ = bf16[8,7168]{1,0:T(8,128)(2,1)S(1)} collective-permute-done((bf16[8,7168]{1,0:T(8,128)(2,1)S(1)}, bf16[8,7168]{1,0:T(8,128)(2,1)S(1)}, u32[]{:S(2)}, u32[]{:S(2)}) %collective-permute-start.8) | collective-permute-done | bytes 114720 | tf_op jit(solution)/shard_map/ppermute | solution.py:20
  32.2 0.1 shard_map.73
  32.3 2.8 %collective-permute-start.9 = (bf16[4,7168]{1,0:T(4,128)(2,1)S(1)}, bf16[4,7168]{1,0:T(4,128)(2,1)S(1)}, u32[]{:S(2)}, u32[]{:S(2)}) collective-permute-start(bf16[4,7168]{1,0:T(4,128)(2,1)S(1)} %get-tuple-element.30), channel_id=1, source_target_pairs={{0,3},{1,2},{2,1},{3,0},{4,7},{5,6},{6,5},{7,4},{8,11},{9,10},{10,... | collective-permute-start | bytes 172040 | tf_op jit(solution)/shard_map/ppermute | solution.py:20
  35.1 0.3 collective-permute-start.10
  35.4 1.4 %collective-permute-start.11 = (bf16[4,7168]{1,0:T(4,128)(2,1)S(1)}, bf16[4,7168]{1,0:T(4,128)(2,1)S(1)}, u32[]{:S(2)}, u32[]{:S(2)}) collective-permute-start(bf16[4,7168]{1,0:T(4,128)(2,1)S(1)} %get-tuple-element.32), channel_id=1, source_target_pairs={{0,8},{1,9},{2,10},{3,11},{4,12},{5,13},{6,14},{7,15},{8,0},{9,1},... | collective-permute-start | bytes 172040 | tf_op jit(solution)/shard_map/ppermute | solution.py:20
  36.8 2.2 %collective-permute-done.9 = bf16[4,7168]{1,0:T(4,128)(2,1)S(1)} collective-permute-done((bf16[4,7168]{1,0:T(4,128)(2,1)S(1)}, bf16[4,7168]{1,0:T(4,128)(2,1)S(1)}, u32[]{:S(2)}, u32[]{:S(2)}) %collective-permute-start.9) | collective-permute-done | bytes 57376 | tf_op jit(solution)/shard_map/ppermute | solution.py:20
  39.1 1.8 %collective-permute-done.10 = bf16[4,7168]{1,0:T(4,128)(2,1)S(1)} collective-permute-done((bf16[4,7168]{1,0:T(4,128)(2,1)S(1)}, bf16[4,7168]{1,0:T(4,128)(2,1)S(1)}, u32[]{:S(2)}, u32[]{:S(2)}) %collective-permute-start.10) | collective-permute-done | bytes 57376 | tf_op jit(solution)/shard_map/ppermute | solution.py:20
  40.8 0.0 collective-permute-done.11
  40.8 0.7 %add_convert_fusion = bf16[4,7168]{1,0:T(4,128)(2,1)} fusion(bf16[4,7168]{1,0:T(4,128)(2,1)S(1)} %collective-permute-done.11, bf16[4,7168]{1,0:T(4,128)(2,1)S(1)} %collective-permute-done.10, bf16[4,7168]{1,0:T(4,128)(2,1)S(1)} %collective-permute-done.9, bf16[4,7168]{1,0:T(4,128)(2,1)S(1)} %get-tuple-element.29), kind=kLoop, calls=%fused_computation | loop fusion | flops 229376 | bytes 286720 | tf_op jit(solution)/shard_map/convert_element_type | solution.py:286
  (3 shorter events, 0.1 us)
Async XLA Ops:
  0.9 10.8 %collective-permute-start = (bf16[4,7296]{1,0:T(4,128)(2,1)S(1)}, bf16[4,7296]{1,0:T(4,128)(2,1)S(1)}, u32[]{:S(2)}, u32[]{:S(2)}) collective-permute-start(bf16[4,7296]{1,0:T(4,128)(2,1)S(1)} %shard_map.64.refs_0_), channel_id=1, source_target_pairs={{0,8},{1,9},{2,10},{3,11},{4,12},{5,13},{6,14},{7,15},{8,0},{9,1},... | collective-permute-start | bytes 175112 | tf_op jit(solution)/shard_map/ppermute | solution.py:20
  3.9 8.7 %collective-permute-start.2 = (bf16[4,7296]{1,0:T(4,128)(2,1)S(1)}, bf16[4,7296]{1,0:T(4,128)(2,1)S(1)}, u32[]{:S(2)}, u32[]{:S(2)}) collective-permute-start(bf16[4,7296]{1,0:T(4,128)(2,1)S(1)} %shard_map.64.refs_0_), channel_id=1, source_target_pairs={{0,3},{1,2},{2,1},{3,0},{4,7},{5,6},{6,5},{7,4},{8,11},{9,10},{10,... | collective-permute-start | bytes 175112 | tf_op jit(solution)/shard_map/ppermute | solution.py:20
  7.5 5.1 %collective-permute-start.1 = (bf16[4,7296]{1,0:T(4,128)(2,1)S(1)}, bf16[4,7296]{1,0:T(4,128)(2,1)S(1)}, u32[]{:S(2)}, u32[]{:S(2)}) collective-permute-start(bf16[4,7296]{1,0:T(4,128)(2,1)S(1)} %shard_map.64.refs_0_), channel_id=1, source_target_pairs={{0,2},{1,3},{2,0},{3,1},{4,6},{5,7},{6,4},{7,5},{8,10},{9,11},{10,... | collective-permute-start | bytes 175112 | tf_op jit(solution)/shard_map/ppermute | solution.py:20
  11.7 5.7 %collective-permute-start.3 = (bf16[8,7296]{1,0:T(8,128)(2,1)S(1)}, bf16[8,7296]{1,0:T(8,128)(2,1)S(1)}, u32[]{:S(2)}, u32[]{:S(2)}) collective-permute-start(bf16[8,7296]{1,0:T(8,128)(2,1)S(1)} %shard_map.66.refs_0_), channel_id=1, source_target_pairs={{0,1},{1,0},{2,3},{3,2},{4,5},{5,4},{6,7},{7,6},{8,9},{9,8},{10,11... | collective-permute-start | bytes 350216 | tf_op jit(solution)/shard_map/ppermute | solution.py:20
  12.6 4.9 %collective-permute-start.4 = (bf16[8,7296]{1,0:T(8,128)(2,1)S(1)}, bf16[8,7296]{1,0:T(8,128)(2,1)S(1)}, u32[]{:S(2)}, u32[]{:S(2)}) collective-permute-start(bf16[8,7296]{1,0:T(8,128)(2,1)S(1)} %shard_map.67.refs_1_), channel_id=1, source_target_pairs={{0,8},{1,9},{2,10},{3,11},{4,12},{5,13},{6,14},{7,15},{8,0},{9,1},... | collective-permute-start | bytes 350216 | tf_op jit(solution)/shard_map/ppermute | solution.py:20
  17.6 2.0 %collective-permute-start.5 = (bf16[32,7296]{1,0:T(8,128)(2,1)S(1)}, bf16[32,7296]{1,0:T(8,128)(2,1)S(1)}, u32[]{:S(2)}, u32[]{:S(2)}) collective-permute-start(bf16[32,7296]{1,0:T(8,128)(2,1)S(1)} %shard_map.69.after.near), channel_id=1, source_target_pairs={{0,4},{1,5},{2,6},{3,7},{4,0},{5,1},{6,2},{7,3},{8,12},{9,13},{10,... | collective-permute-start | bytes 1400840 | tf_op jit(solution)/shard_map/ppermute | solution.py:20
  23.7 2.0 %collective-permute-start.6 = (bf16[32,7168]{1,0:T(8,128)(2,1)S(1)}, bf16[32,7168]{1,0:T(8,128)(2,1)S(1)}, u32[]{:S(2)}, u32[]{:S(2)}) collective-permute-start(bf16[32,7168]{1,0:T(8,128)(2,1)S(1)} %get-tuple-element.24), channel_id=1, source_target_pairs={{0,4},{1,5},{2,6},{3,7},{4,0},{5,1},{6,2},{7,3},{8,12},{9,13},{10,... | collective-permute-start | bytes 1376264 | tf_op jit(solution)/shard_map/ppermute | solution.py:20
  25.8 5.5 %collective-permute-start.7 = (bf16[8,7168]{1,0:T(8,128)(2,1)S(1)}, bf16[8,7168]{1,0:T(8,128)(2,1)S(1)}, u32[]{:S(2)}, u32[]{:S(2)}) collective-permute-start(bf16[8,7168]{1,0:T(8,128)(2,1)S(1)} %get-tuple-element.26), channel_id=1, source_target_pairs={{0,1},{1,0},{2,3},{3,2},{4,5},{5,4},{6,7},{7,6},{8,9},{9,8},{10,11... | collective-permute-start | bytes 344072 | tf_op jit(solution)/shard_map/ppermute | solution.py:20
  27.1 5.1 %collective-permute-start.8 = (bf16[8,7168]{1,0:T(8,128)(2,1)S(1)}, bf16[8,7168]{1,0:T(8,128)(2,1)S(1)}, u32[]{:S(2)}, u32[]{:S(2)}) collective-permute-start(bf16[8,7168]{1,0:T(8,128)(2,1)S(1)} %get-tuple-element.28), channel_id=1, source_target_pairs={{0,8},{1,9},{2,10},{3,11},{4,12},{5,13},{6,14},{7,15},{8,0},{9,1},... | collective-permute-start | bytes 344072 | tf_op jit(solution)/shard_map/ppermute | solution.py:20
  32.3 6.7 %collective-permute-start.9 = (bf16[4,7168]{1,0:T(4,128)(2,1)S(1)}, bf16[4,7168]{1,0:T(4,128)(2,1)S(1)}, u32[]{:S(2)}, u32[]{:S(2)}) collective-permute-start(bf16[4,7168]{1,0:T(4,128)(2,1)S(1)} %get-tuple-element.30), channel_id=1, source_target_pairs={{0,3},{1,2},{2,1},{3,0},{4,7},{5,6},{6,5},{7,4},{8,11},{9,10},{10,... | collective-permute-start | bytes 172040 | tf_op jit(solution)/shard_map/ppermute | solution.py:20
  35.1 5.7 %collective-permute-start.10 = (bf16[4,7168]{1,0:T(4,128)(2,1)S(1)}, bf16[4,7168]{1,0:T(4,128)(2,1)S(1)}, u32[]{:S(2)}, u32[]{:S(2)}) collective-permute-start(bf16[4,7168]{1,0:T(4,128)(2,1)S(1)} %get-tuple-element.31), channel_id=1, source_target_pairs={{0,2},{1,3},{2,0},{3,1},{4,6},{5,7},{6,4},{7,5},{8,10},{9,11},{10,... | collective-permute-start | bytes 172040 | tf_op jit(solution)/shard_map/ppermute | solution.py:20
  35.4 5.4 %collective-permute-start.11 = (bf16[4,7168]{1,0:T(4,128)(2,1)S(1)}, bf16[4,7168]{1,0:T(4,128)(2,1)S(1)}, u32[]{:S(2)}, u32[]{:S(2)}) collective-permute-start(bf16[4,7168]{1,0:T(4,128)(2,1)S(1)} %get-tuple-element.32), channel_id=1, source_target_pairs={{0,8},{1,9},{2,10},{3,11},{4,12},{5,13},{6,14},{7,15},{8,0},{9,1},... | collective-permute-start | bytes 172040 | tf_op jit(solution)/shard_map/ppermute | solution.py:20

commit v5 on v4

--- a/solution.py
+++ b/solution.py
@@ -235,20 +235,17 @@
     return local_call(kernel, [shape], [*operands, *after])[0]
 
 
-def fold_kernel(near, far, *outs):
+def fold_kernel(rows, groups, near, far, *refs):
     total = near[...].astype(jnp.float32) + far[...].astype(jnp.float32)
-    at = 0
-    for out in outs:
-        out[...] = total[at : at + out.shape[0]].astype(jnp.bfloat16)
-        at += out.shape[0]
-
-
-def split_kernel(count, rows, head, head_got, *refs):
-    top = head[...].astype(jnp.float32) + head_got[...].astype(jnp.float32)
-    low = sum(r[...].astype(jnp.float32) for r in refs[:count])
-    both = jnp.concatenate([top, low], axis=0)
+    for group, out in zip(groups, refs[len(refs) - len(groups) :]):
+        pieces = [total[i * rows : (i + 1) * rows] for i in group]
+        out[...] = jnp.concatenate(pieces, axis=0).astype(jnp.bfloat16)
+
+
+def split_kernel(count, rows, *refs):
+    total = sum(r[...].astype(jnp.float32) for r in refs[:count])
     for i, out in enumerate(refs[count:]):
-        out[...] = both[i * rows : (i + 1) * rows].astype(jnp.bfloat16)
+        out[...] = total[i * rows : (i + 1) * rows].astype(jnp.bfloat16)
 
 
 def shards(tokens, node_list, gates, row_source, expert_in, expert_out):
@@ -270,20 +267,39 @@
     near_out, far_out = experts(
         gates.shape[1], rows, near, swap(near, locals_, count), weights, (*early, late)
     )
-    sizes = [head.shape[0], tail.shape[0], head.shape[0]] + [tail.shape[0]] * len(across)
-    head, tail, side, *sides = local_call(
-        fold_kernel, [(s, width) for s in sizes], [near_out, swap(far_out, locals_, count)]
-    )
-    head_got = swap(side, 1, count)
-    tail_got = [swap(v, a * step, count) for a, v in zip(across, sides)]
-    own, *others = local_call(
-        functools.partial(split_kernel, 1 + len(across), rows),
-        [(rows, width)] * (1 + len(across) + len(beyond)),
-        [head, head_got, tail, *tail_got],
-    )
-    masks = [a * step for a in across] + list(beyond)
-    got = [swap(v, m, count) for m, v in reversed(list(zip(masks, others)))]
-    return sum(v.astype(jnp.float32) for v in [own, *got]).astype(jnp.bfloat16)
+    everywhere = [0, *across]
+    places = [(a, 0) for a in everywhere] + [(0, b) for b in beyond]
+    places += [(a, 1) for a in everywhere] + [(a, b) for a in across for b in beyond]
+    index = {place: i for i, place in enumerate(places)}
+    far_got = swap(far_out, locals_, count)
+    merged = [0, *range(2, locals_, 2)]
+
+    def fold(groups, *after):
+        return local_call(
+            functools.partial(fold_kernel, rows, [[index[p] for p in g] for g in groups]),
+            [(len(g) * rows, width) for g in groups],
+            [near_out, far_got, *after],
+        )
+
+    def send(blocks, after):
+        arrays = fold([[p] for p in blocks], after)
+        return [swap(v, a * step + b, count) for v, (a, b) in zip(arrays, blocks)], arrays[0]
+
+    kept, *crossing = fold([[(a, b) for b in merged] for a in everywhere])
+    crossed = [swap(v, a * step, count) for a, v in zip(across, crossing)]
+    middle, done = [], kept
+    for b in range(3, locals_, 2):
+        for a in reversed(everywhere):
+            sent, done = send([(a, b)], done)
+            middle += sent
+    beside, _ = send([(a, 1) for a in everywhere], done)
+    own, *last = local_call(
+        functools.partial(split_kernel, 1 + len(crossed), rows),
+        [(rows, width)] * len(merged),
+        [kept, *crossed],
+    )
+    last = [swap(v, b, count) for v, b in zip(last, merged[1:])]
+    return sum(v.astype(jnp.float32) for v in [own, *middle, *beside, *last]).astype(jnp.bfloat16)
 
 
 def solution(mesh):

time: 41.7 us -> 40.6 us (0.974)
  waiting for transfers between devices: 9.26 us -> 4.5 us
  starting transfers between devices: 15.9 us -> 19.4 us
    ppermute x12 -> x13, waiting for transfers between devices: 9.26 us -> 4.5 us  [swap(): return lax.ppermute(value, AXES, [(i, i ^ mask) for i in range(count)])]
    ppermute x12 -> x13, starting transfers between devices: 15.9 us -> 19.4 us  [swap(): return lax.ppermute(value, AXES, [(i, i ^ mask) for i in range(count)])]
  transfers between devices with their start and end apart: 12 -> 13, of which waited for: 6 -> 4; matrix products, arithmetic and copies ran while one was open for 0% -> 0% of each run, Pallas kernels for 25% -> 26%
where the time goes in v5:
time: 40.6 us; the launch traced here: 40.4 us
  starting transfers between devices  19.4 us (48%)
  Pallas kernels  15.6 us (38%)
  waiting for transfers between devices  4.5 us (11%)
  other arithmetic  0.72 us (2%)
    ppermute x13, starting transfers between devices, swap(): return lax.ppermute(value, AXES, [(i, i ^ mask) for i in range(count)])  19.4 us
    pallas_call x2, Pallas kernels, sort_weights(): pl.pallas_call(functools.partial(sort_kernel, chunk, kinds, expert, ends[...  8.36 us
    ppermute x13, waiting for transfers between devices, swap(): return lax.ppermute(value, AXES, [(i, i ^ mask) for i in range(count)])  4.5 us
    pallas_call x1, Pallas kernels, experts(): pl.pallas_call(functools.partial(expert_kernel, chosen, pair, rows), out_...  4.11 us
    pallas_call x1, Pallas kernels, load(): pl.pallas_call(functools.partial(load_kernel, begin), out_shape=VMEM((hei...  1.9 us
    pallas_call x1, Pallas kernels, pack(): pl.pallas_call(pack_kernel, out_shape=VMEM((rows, width + LANES), jnp.bfl...  0.85 us
  transfers between devices with their start and end apart: 13, of which 4 were waited for; matrix products, arithmetic and copies ran while one was open for 0% of the time, Pallas kernels for 26%

profile of v5, /device:TPU:0, one launch (start us, length us, event | category | flops | bytes accessed | tf_op | source)
XLA Modules:
  0.0 40.4 jit_solution(7250099309267457204)
XLA Ops:
  0.0 0.9 %shard_map.64.refs_0_ = bf16[4,7296]{1,0:T(4,128)(2,1)S(1)} custom-call(bf16[4,7168]{1,0:T(4,128)(2,1)} %tokens.1, bf16[4,4]{1,0:T(4,128)(2,1)} %gates.1, s32[2,4]{1,0:T(2,128)} %bitcast.12, s32[1,4]{1,0:T(1,128)} %source.1), custom_call_target="tpu_custom_call" | custom-call | tf_op jit(solution)/shard_map/pallas_call | solution.py:60
  0.9 3.0 %collective-permute-start = (bf16[4,7296]{1,0:T(4,128)(2,1)S(1)}, bf16[4,7296]{1,0:T(4,128)(2,1)S(1)}, u32[]{:S(2)}, u32[]{:S(2)}) collective-permute-start(bf16[4,7296]{1,0:T(4,128)(2,1)S(1)} %shard_map.64.refs_0_), channel_id=1, source_target_pairs={{0,8},{1,9},{2,10},{3,11},{4,12},{5,13},{6,14},{7,15},{8,0},{9,1},... | collective-permute-start | bytes 175112 | tf_op jit(solution)/shard_map/ppermute | solution.py:20
  3.9 3.6 %collective-permute-start.2 = (bf16[4,7296]{1,0:T(4,128)(2,1)S(1)}, bf16[4,7296]{1,0:T(4,128)(2,1)S(1)}, u32[]{:S(2)}, u32[]{:S(2)}) collective-permute-start(bf16[4,7296]{1,0:T(4,128)(2,1)S(1)} %shard_map.64.refs_0_), channel_id=1, source_target_pairs={{0,3},{1,2},{2,1},{3,0},{4,7},{5,6},{6,5},{7,4},{8,11},{9,10},{10,... | collective-permute-start | bytes 175112 | tf_op jit(solution)/shard_map/ppermute | solution.py:20
  7.5 0.0 collective-permute-start.1
  7.5 4.2 %shard_map.65 = (bf16[7168,512]{1,0:T(8,128)(2,1)S(1)}, bf16[512,2048]{1,0:T(8,128)(2,1)S(1)}) custom-call(bf16[2,28672,128]{2,1,0:T(8,128)(2,1)} %bitcast.10, bf16[512,7168]{1,0:T(8,128)(2,1)} %bitcast.7), custom_call_target="tpu_custom_call" | custom-call | bytes 14680064 | tf_op jit(solution)/shard_map/pallas_call | solution.py:118
  11.7 0.0 collective-permute-done.refs_1_
  11.7 0.8 %collective-permute-start.3 = (bf16[8,7296]{1,0:T(8,128)(2,1)S(1)}, bf16[8,7296]{1,0:T(8,128)(2,1)S(1)}, u32[]{:S(2)}, u32[]{:S(2)}) collective-permute-start(bf16[8,7296]{1,0:T(8,128)(2,1)S(1)} %shard_map.66.refs_0_), channel_id=1, source_target_pairs={{0,1},{1,0},{2,3},{3,2},{4,5},{5,4},{6,7},{7,6},{8,9},{9,8},{10,11... | collective-permute-start | bytes 350216 | tf_op jit(solution)/shard_map/ppermute | solution.py:20
  12.6 0.0 collective-permute-done.2.refs_1_
  12.6 0.0 collective-permute-done.1.refs_0_
  12.6 0.6 %collective-permute-start.4 = (bf16[8,7296]{1,0:T(8,128)(2,1)S(1)}, bf16[8,7296]{1,0:T(8,128)(2,1)S(1)}, u32[]{:S(2)}, u32[]{:S(2)}) collective-permute-start(bf16[8,7296]{1,0:T(8,128)(2,1)S(1)} %shard_map.67.refs_1_), channel_id=1, source_target_pairs={{0,8},{1,9},{2,10},{3,11},{4,12},{5,13},{6,14},{7,15},{8,0},{9,1},... | collective-permute-start | bytes 350216 | tf_op jit(solution)/shard_map/ppermute | solution.py:20
  13.2 4.2 %shard_map.68 = (bf16[7168,512]{1,0:T(8,128)(2,1)S(1)}, bf16[512,2048]{1,0:T(8,128)(2,1)S(1)}) custom-call(bf16[2,28672,128]{2,1,0:T(8,128)(2,1)} %bitcast.11, bf16[512,7168]{1,0:T(8,128)(2,1)} %bitcast.8), custom_call_target="tpu_custom_call" | custom-call | bytes 14680064 | tf_op jit(solution)/shard_map/pallas_call | solution.py:118
  17.4 0.0 collective-permute-done.3.refs_2_
  17.4 0.1 collective-permute-done.4.refs_3_
  17.5 0.1 shard_map.69.after.near
  17.6 0.1 collective-permute-start.5
  17.6 1.9 %shard_map.70.refs_4_ = bf16[512,3072]{1,0:T(8,128)(2,1)S(1)} custom-call(bf16[512,7168]{1,0:T(8,128)(2,1)} %bitcast.9, bf16[32,7296]{1,0:T(8,128)(2,1)S(1)} %shard_map.69.after.near), custom_call_target="tpu_custom_call" | custom-call | bytes 3145728 | tf_op jit(solution)/shard_map/pallas_call | solution.py:195
  19.6 0.0 collective-permute-done.5.far
  19.6 4.1 %shard_map.71 = (bf16[32,7168]{1,0:T(8,128)(2,1)S(1)}, bf16[32,7168]{1,0:T(8,128)(2,1)S(1)}) custom-call(bf16[32,7296]{1,0:T(8,128)(2,1)S(1)} %shard_map.69.after.near, bf16[32,7296]{1,0:T(8,128)(2,1)S(1)} %collective-permute-done.5.far, bf16[7168,512]{1,0:T(8,128)(2,1)S(1)} %get-tuple-element.19.refs_0_, bf16[7168,512]{1,0:T(8,128)(2,1)S(1)} %get-tuple-element.20.refs_1_, ...), custom_call_target="tpu_custom_call" | custom-call | flops 1409286144 | bytes 8388608 | tf_op jit(solution)/shard_map/pallas_call | solution.py:212
  23.7 0.6 %collective-permute-start.6 = (bf16[32,7168]{1,0:T(8,128)(2,1)S(1)}, bf16[32,7168]{1,0:T(8,128)(2,1)S(1)}, u32[]{:S(2)}, u32[]{:S(2)}) collective-permute-start(bf16[32,7168]{1,0:T(8,128)(2,1)S(1)} %get-tuple-element.22), channel_id=1, source_target_pairs={{0,4},{1,5},{2,6},{3,7},{4,0},{5,1},{6,2},{7,3},{8,12},{9,13},{10,... | collective-permute-start | bytes 1376264 | tf_op jit(solution)/shard_map/ppermute | solution.py:20
  24.2 1.4 %collective-permute-done.6.far = bf16[32,7168]{1,0:T(8,128)(2,1)S(1)} collective-permute-done((bf16[32,7168]{1,0:T(8,128)(2,1)S(1)}, bf16[32,7168]{1,0:T(8,128)(2,1)S(1)}, u32[]{:S(2)}, u32[]{:S(2)}) %collective-permute-start.6) | collective-permute-done | bytes 458784 | tf_op jit(solution)/shard_map/ppermute | solution.py:20
  25.7 0.1 shard_map.72
  25.8 1.5 %collective-permute-start.7 = (bf16[8,7168]{1,0:T(8,128)(2,1)S(1)}, bf16[8,7168]{1,0:T(8,128)(2,1)S(1)}, u32[]{:S(2)}, u32[]{:S(2)}) collective-permute-start(bf16[8,7168]{1,0:T(8,128)(2,1)S(1)} %get-tuple-element.24), channel_id=1, source_target_pairs={{0,8},{1,9},{2,10},{3,11},{4,12},{5,13},{6,14},{7,15},{8,0},{9,1},... | collective-permute-start | bytes 344072 | tf_op jit(solution)/shard_map/ppermute | solution.py:20
  27.3 3.7 %collective-permute-start.8 = (bf16[4,7168]{1,0:T(4,128)(2,1)S(1)}, bf16[4,7168]{1,0:T(4,128)(2,1)S(1)}, u32[]{:S(2)}, u32[]{:S(2)}) collective-permute-start(bf16[4,7168]{1,0:T(4,128)(2,1)S(1)} %shard_map.74.refs_0_), channel_id=1, source_target_pairs={{0,11},{1,10},{2,9},{3,8},{4,15},{5,14},{6,13},{7,12},{8,3},{9,2},... | collective-permute-start | bytes 172040 | tf_op jit(solution)/shard_map/ppermute | solution.py:20
  31.1 0.3 collective-permute-start.9
  31.4 0.1 collective-permute-start.10
  31.5 2.9 %collective-permute-start.11 = (bf16[4,7168]{1,0:T(4,128)(2,1)S(1)}, bf16[4,7168]{1,0:T(4,128)(2,1)S(1)}, u32[]{:S(2)}, u32[]{:S(2)}) collective-permute-start(bf16[4,7168]{1,0:T(4,128)(2,1)S(1)} %get-tuple-element.27), channel_id=1, source_target_pairs={{0,9},{1,8},{2,11},{3,10},{4,13},{5,12},{6,15},{7,14},{8,1},{9,0},... | collective-permute-start | bytes 172040 | tf_op jit(solution)/shard_map/ppermute | solution.py:20
  34.4 2.3 %collective-permute-start.12 = (bf16[4,7168]{1,0:T(4,128)(2,1)S(1)}, bf16[4,7168]{1,0:T(4,128)(2,1)S(1)}, u32[]{:S(2)}, u32[]{:S(2)}) collective-permute-start(bf16[4,7168]{1,0:T(4,128)(2,1)S(1)} %get-tuple-element.28), channel_id=1, source_target_pairs={{0,2},{1,3},{2,0},{3,1},{4,6},{5,7},{6,4},{7,5},{8,10},{9,11},{10,... | collective-permute-start | bytes 172040 | tf_op jit(solution)/shard_map/ppermute | solution.py:20
  36.7 2.3 %collective-permute-done.11 = bf16[4,7168]{1,0:T(4,128)(2,1)S(1)} collective-permute-done((bf16[4,7168]{1,0:T(4,128)(2,1)S(1)}, bf16[4,7168]{1,0:T(4,128)(2,1)S(1)}, u32[]{:S(2)}, u32[]{:S(2)}) %collective-permute-start.11) | collective-permute-done | bytes 57376 | tf_op jit(solution)/shard_map/ppermute | solution.py:20
  39.0 0.0 collective-permute-done.9
  39.0 0.0 collective-permute-done.8
  39.0 0.7 %collective-permute-done.12 = bf16[4,7168]{1,0:T(4,128)(2,1)S(1)} collective-permute-done((bf16[4,7168]{1,0:T(4,128)(2,1)S(1)}, bf16[4,7168]{1,0:T(4,128)(2,1)S(1)}, u32[]{:S(2)}, u32[]{:S(2)}) %collective-permute-start.12) | collective-permute-done | bytes 57376 | tf_op jit(solution)/shard_map/ppermute | solution.py:20
  39.6 0.7 %add_convert_fusion = bf16[4,7168]{1,0:T(4,128)(2,1)} fusion(bf16[4,7168]{1,0:T(4,128)(2,1)S(1)} %collective-permute-done.12, bf16[4,7168]{1,0:T(4,128)(2,1)S(1)} %collective-permute-done.11, bf16[4,7168]{1,0:T(4,128)(2,1)S(1)} %collective-permute-done.10, bf16[4,7168]{1,0:T(4,128)(2,1)S(1)} %collective-permute-done.9, ...), kind=kLoop, calls=%fused_computation | loop fusion | flops 344064 | bytes 401408 | tf_op jit(solution)/shard_map/convert_element_type | solution.py:302
  (8 shorter events, 0.2 us)
Async XLA Ops:
  0.9 10.8 %collective-permute-start = (bf16[4,7296]{1,0:T(4,128)(2,1)S(1)}, bf16[4,7296]{1,0:T(4,128)(2,1)S(1)}, u32[]{:S(2)}, u32[]{:S(2)}) collective-permute-start(bf16[4,7296]{1,0:T(4,128)(2,1)S(1)} %shard_map.64.refs_0_), channel_id=1, source_target_pairs={{0,8},{1,9},{2,10},{3,11},{4,12},{5,13},{6,14},{7,15},{8,0},{9,1},... | collective-permute-start | bytes 175112 | tf_op jit(solution)/shard_map/ppermute | solution.py:20
  3.9 8.7 %collective-permute-start.2 = (bf16[4,7296]{1,0:T(4,128)(2,1)S(1)}, bf16[4,7296]{1,0:T(4,128)(2,1)S(1)}, u32[]{:S(2)}, u32[]{:S(2)}) collective-permute-start(bf16[4,7296]{1,0:T(4,128)(2,1)S(1)} %shard_map.64.refs_0_), channel_id=1, source_target_pairs={{0,3},{1,2},{2,1},{3,0},{4,7},{5,6},{6,5},{7,4},{8,11},{9,10},{10,... | collective-permute-start | bytes 175112 | tf_op jit(solution)/shard_map/ppermute | solution.py:20
  7.5 5.1 %collective-permute-start.1 = (bf16[4,7296]{1,0:T(4,128)(2,1)S(1)}, bf16[4,7296]{1,0:T(4,128)(2,1)S(1)}, u32[]{:S(2)}, u32[]{:S(2)}) collective-permute-start(bf16[4,7296]{1,0:T(4,128)(2,1)S(1)} %shard_map.64.refs_0_), channel_id=1, source_target_pairs={{0,2},{1,3},{2,0},{3,1},{4,6},{5,7},{6,4},{7,5},{8,10},{9,11},{10,... | collective-permute-start | bytes 175112 | tf_op jit(solution)/shard_map/ppermute | solution.py:20
  11.7 5.7 %collective-permute-start.3 = (bf16[8,7296]{1,0:T(8,128)(2,1)S(1)}, bf16[8,7296]{1,0:T(8,128)(2,1)S(1)}, u32[]{:S(2)}, u32[]{:S(2)}) collective-permute-start(bf16[8,7296]{1,0:T(8,128)(2,1)S(1)} %shard_map.66.refs_0_), channel_id=1, source_target_pairs={{0,1},{1,0},{2,3},{3,2},{4,5},{5,4},{6,7},{7,6},{8,9},{9,8},{10,11... | collective-permute-start | bytes 350216 | tf_op jit(solution)/shard_map/ppermute | solution.py:20
  12.6 4.9 %collective-permute-start.4 = (bf16[8,7296]{1,0:T(8,128)(2,1)S(1)}, bf16[8,7296]{1,0:T(8,128)(2,1)S(1)}, u32[]{:S(2)}, u32[]{:S(2)}) collective-permute-start(bf16[8,7296]{1,0:T(8,128)(2,1)S(1)} %shard_map.67.refs_1_), channel_id=1, source_target_pairs={{0,8},{1,9},{2,10},{3,11},{4,12},{5,13},{6,14},{7,15},{8,0},{9,1},... | collective-permute-start | bytes 350216 | tf_op jit(solution)/shard_map/ppermute | solution.py:20
  17.6 2.0 %collective-permute-start.5 = (bf16[32,7296]{1,0:T(8,128)(2,1)S(1)}, bf16[32,7296]{1,0:T(8,128)(2,1)S(1)}, u32[]{:S(2)}, u32[]{:S(2)}) collective-permute-start(bf16[32,7296]{1,0:T(8,128)(2,1)S(1)} %shard_map.69.after.near), channel_id=1, source_target_pairs={{0,4},{1,5},{2,6},{3,7},{4,0},{5,1},{6,2},{7,3},{8,12},{9,13},{10,... | collective-permute-start | bytes 1400840 | tf_op jit(solution)/shard_map/ppermute | solution.py:20
  23.7 2.0 %collective-permute-start.6 = (bf16[32,7168]{1,0:T(8,128)(2,1)S(1)}, bf16[32,7168]{1,0:T(8,128)(2,1)S(1)}, u32[]{:S(2)}, u32[]{:S(2)}) collective-permute-start(bf16[32,7168]{1,0:T(8,128)(2,1)S(1)} %get-tuple-element.22), channel_id=1, source_target_pairs={{0,4},{1,5},{2,6},{3,7},{4,0},{5,1},{6,2},{7,3},{8,12},{9,13},{10,... | collective-permute-start | bytes 1376264 | tf_op jit(solution)/shard_map/ppermute | solution.py:20
  25.8 8.6 %collective-permute-start.7 = (bf16[8,7168]{1,0:T(8,128)(2,1)S(1)}, bf16[8,7168]{1,0:T(8,128)(2,1)S(1)}, u32[]{:S(2)}, u32[]{:S(2)}) collective-permute-start(bf16[8,7168]{1,0:T(8,128)(2,1)S(1)} %get-tuple-element.24), channel_id=1, source_target_pairs={{0,8},{1,9},{2,10},{3,11},{4,12},{5,13},{6,14},{7,15},{8,0},{9,1},... | collective-permute-start | bytes 344072 | tf_op jit(solution)/shard_map/ppermute | solution.py:20
  27.3 11.6 %collective-permute-start.8 = (bf16[4,7168]{1,0:T(4,128)(2,1)S(1)}, bf16[4,7168]{1,0:T(4,128)(2,1)S(1)}, u32[]{:S(2)}, u32[]{:S(2)}) collective-permute-start(bf16[4,7168]{1,0:T(4,128)(2,1)S(1)} %shard_map.74.refs_0_), channel_id=1, source_target_pairs={{0,11},{1,10},{2,9},{3,8},{4,15},{5,14},{6,13},{7,12},{8,3},{9,2},... | collective-permute-start | bytes 172040 | tf_op jit(solution)/shard_map/ppermute | solution.py:20
  31.1 7.9 %collective-permute-start.9 = (bf16[4,7168]{1,0:T(4,128)(2,1)S(1)}, bf16[4,7168]{1,0:T(4,128)(2,1)S(1)}, u32[]{:S(2)}, u32[]{:S(2)}) collective-permute-start(bf16[4,7168]{1,0:T(4,128)(2,1)S(1)} %shard_map.75.refs_0_), channel_id=1, source_target_pairs={{0,3},{1,2},{2,1},{3,0},{4,7},{5,6},{6,5},{7,4},{8,11},{9,10},{10,... | collective-permute-start | bytes 172040 | tf_op jit(solution)/shard_map/ppermute | solution.py:20
  31.4 5.3 %collective-permute-start.10 = (bf16[4,7168]{1,0:T(4,128)(2,1)S(1)}, bf16[4,7168]{1,0:T(4,128)(2,1)S(1)}, u32[]{:S(2)}, u32[]{:S(2)}) collective-permute-start(bf16[4,7168]{1,0:T(4,128)(2,1)S(1)} %get-tuple-element.26), channel_id=1, source_target_pairs={{0,1},{1,0},{2,3},{3,2},{4,5},{5,4},{6,7},{7,6},{8,9},{9,8},{10,11... | collective-permute-start | bytes 172040 | tf_op jit(solution)/shard_map/ppermute | solution.py:20
  31.5 7.5 %collective-permute-start.11 = (bf16[4,7168]{1,0:T(4,128)(2,1)S(1)}, bf16[4,7168]{1,0:T(4,128)(2,1)S(1)}, u32[]{:S(2)}, u32[]{:S(2)}) collective-permute-start(bf16[4,7168]{1,0:T(4,128)(2,1)S(1)} %get-tuple-element.27), channel_id=1, source_target_pairs={{0,9},{1,8},{2,11},{3,10},{4,13},{5,12},{6,15},{7,14},{8,1},{9,0},... | collective-permute-start | bytes 172040 | tf_op jit(solution)/shard_map/ppermute | solution.py:20
  34.4 5.2 %collective-permute-start.12 = (bf16[4,7168]{1,0:T(4,128)(2,1)S(1)}, bf16[4,7168]{1,0:T(4,128)(2,1)S(1)}, u32[]{:S(2)}, u32[]{:S(2)}) collective-permute-start(bf16[4,7168]{1,0:T(4,128)(2,1)S(1)} %get-tuple-element.28), channel_id=1, source_target_pairs={{0,2},{1,3},{2,0},{3,1},{4,6},{5,7},{6,4},{7,5},{8,10},{9,11},{10,... | collective-permute-start | bytes 172040 | tf_op jit(solution)/shard_map/ppermute | solution.py:20

commit v6 on v5

--- a/solution.py
+++ b/solution.py
@@ -11,8 +11,6 @@
 VMEM = pltpu.VMEM
 LANES = 128
 BUFFERS = 8
-PIECE = 1024
-EARLY = (2, 2)
 SMALL = pltpu.CompilerParams(vmem_limit_bytes=4 << 20)
 
 
@@ -65,7 +63,7 @@
     )(tokens, gates, node_list.T, row_source)
 
 
-def sort_kernel(chunk, kinds, expert, start_at, source, down, out, part, buffer, wide, sem, down_sem):
+def sort_kernel(chunk, kinds, expert, source, out, token, buffer, wide, sem):
     _, total, _ = source.shape
     count = total // chunk
     depth = chunk // kinds
@@ -78,8 +76,6 @@
 
     for i in range(BUFFERS - 1):
         fetch(i, i).start()
-    extra = pltpu.make_async_copy(down.at[:, pl.ds(start_at, part.shape[1])], part, down_sem)
-    extra.start()
 
     @pl.loop(0, count)
     def _(i):
@@ -98,10 +94,10 @@
                 pl.ds(k, depth, stride=kinds), :
             ].astype(jnp.bfloat16)
 
-    extra.wait()
-
-
-def sort_weights(weight, down):
+    token[...] = jnp.zeros_like(token)
+
+
+def sort_weights(weight):
     pair, depth, two, units = weight.shape
     blocks = units // LANES
     kinds = two * blocks
@@ -111,36 +107,33 @@
         .reshape(pair, depth * kinds, LANES)
     )
     chunk = 512 * kinds
-    down = down.reshape(-1, depth)
-    ends = [sum(EARLY[:e]) * PIECE for e in range(pair + 1)]
-    source = [pltpu.with_memory_space_constraint(a, pltpu.HBM) for a in (view, down)]
+    view = pltpu.with_memory_space_constraint(view, pltpu.HBM)
     return [
         pl.pallas_call(
-            functools.partial(sort_kernel, chunk, kinds, expert, ends[expert]),
+            functools.partial(sort_kernel, chunk, kinds, expert),
             out_shape=(
                 VMEM((depth, two * units), jnp.bfloat16),
-                VMEM((down.shape[0], ends[expert + 1] - ends[expert]), jnp.bfloat16),
+                VMEM((16, LANES), jnp.bfloat16),
             ),
-            in_specs=[pl.BlockSpec(memory_space=pltpu.HBM)] * 2,
+            in_specs=[pl.BlockSpec(memory_space=pltpu.HBM)],
             out_specs=tuple(in_vmem(2)),
             scratch_shapes=[
                 VMEM((BUFFERS, chunk, LANES), jnp.bfloat16),
                 VMEM((chunk, LANES), jnp.float32),
                 pltpu.SemaphoreType.DMA((BUFFERS,)),
-                pltpu.SemaphoreType.DMA,
             ],
             compiler_params=pltpu.CompilerParams(vmem_limit_bytes=8 << 20),
             cost_estimate=pl.CostEstimate(
                 flops=0, bytes_accessed=2 * weight.size, transcendentals=0
             ),
-        )(*source)
+        )(view)
         for expert in range(pair)
     ]
 
 
 def expert_kernel(chosen, pair, rows, near, far, *refs):
-    weight_in, weight_out = refs[:pair], refs[pair:-4]
-    near_out, far_out, held, hidden = refs[-4:]
+    weight_in = refs[:pair]
+    hidden, held = refs[pair:]
     half = near.shape[0]
     depth, columns = weight_in[0].shape
     units = columns // 2
@@ -168,61 +161,25 @@
     hidden[...] = jnp.dot(
         order, jnp.concatenate(active, axis=1), preferred_element_type=jnp.float32
     ).astype(jnp.bfloat16)
-    at = 0
-    for down in weight_out:
-        for i in range(down.shape[1] // PIECE):
-            result = jnp.dot(
-                hidden[...],
-                down[:, i * PIECE : (i + 1) * PIECE],
-                preferred_element_type=jnp.float32,
-            ).astype(jnp.bfloat16)
-            near_out[:, at : at + PIECE] = result[:half]
-            far_out[:, at : at + PIECE] = result[half:]
-            at += PIECE
-
-
-def load_kernel(begin, source, after, out, sem):
-    copy = pltpu.make_async_copy(source.at[:, pl.ds(begin, out.shape[1])], out, sem)
-    copy.start()
-    copy.wait()
-
-
-def load(weight_out, begin, after):
-    weight_out = pltpu.with_memory_space_constraint(
-        weight_out.reshape(-1, weight_out.shape[-1]), pltpu.HBM
-    )
-    height, depth = weight_out.shape
-    return pl.pallas_call(
-        functools.partial(load_kernel, begin),
-        out_shape=VMEM((height, depth - begin), jnp.bfloat16),
-        in_specs=[pl.BlockSpec(memory_space=pltpu.HBM)] + in_vmem(1),
-        out_specs=pl.BlockSpec(memory_space=VMEM),
-        scratch_shapes=[pltpu.SemaphoreType.DMA],
-        compiler_params=SMALL,
-        cost_estimate=pl.CostEstimate(
-            flops=0, bytes_accessed=2 * height * (depth - begin), transcendentals=0
-        ),
-    )(weight_out, *hold(after))
-
-
-def experts(chosen, rows, near, far, weight_in, weight_out):
+
+
+def experts(chosen, rows, near, far, weight_in):
     half = near.shape[0]
     pair = len(weight_in)
     depth, columns = weight_in[0].shape
     return pl.pallas_call(
         functools.partial(expert_kernel, chosen, pair, rows),
-        out_shape=(VMEM((half, depth), jnp.bfloat16),) * 2,
-        in_specs=in_vmem(2 + pair + len(weight_out)),
-        out_specs=tuple(in_vmem(2)),
+        out_shape=VMEM((2 * half, pair * columns // 2), jnp.bfloat16),
+        in_specs=in_vmem(2 + pair),
+        out_specs=pl.BlockSpec(memory_space=VMEM),
         scratch_shapes=[
             VMEM((2 * half, near.shape[1]), jnp.bfloat16),
-            VMEM((2 * half, weight_out[0].shape[0]), jnp.bfloat16),
         ],
         compiler_params=pltpu.CompilerParams(vmem_limit_bytes=20 << 20),
         cost_estimate=pl.CostEstimate(
             flops=6 * half * pair * weight_in[0].size, bytes_accessed=8 << 20, transcendentals=0
         ),
-    )(*hold(near, far, *weight_in, *weight_out))
+    )(*hold(near, far, *weight_in))
 
 
 def join(operands, *after):
@@ -257,16 +214,17 @@
     across = range(1, nodes // 2)
     beyond = range(2, locals_)
     message = pack(tokens, gates, node_list, row_source)
-    weights, early = zip(*sort_weights(expert_in, expert_out))
+    weights, early = zip(*sort_weights(expert_in))
     tail = [swap(message, k, count) for k in beyond]
     head = [message] + [swap(message, a * step, count) for a in across]
     head, tail = join(head, early[0]), join(tail, early[0])
     near = [head, tail, swap(head, 1, count)] + [swap(tail, a * step, count) for a in across]
     near = join(near, *early[1:])
-    late = load(expert_out, sum(a.shape[1] for a in early), near)
-    near_out, far_out = experts(
-        gates.shape[1], rows, near, swap(near, locals_, count), weights, (*early, late)
-    )
+    hidden = experts(gates.shape[1], rows, near, swap(near, locals_, count), weights)
+    down = expert_out.reshape(-1, width)
+    half = near.shape[0]
+    out = jnp.dot(hidden, down, preferred_element_type=jnp.float32).astype(jnp.bfloat16)
+    near_out, far_out = out[:half], out[half:]
     everywhere = [0, *across]
     places = [(a, 0) for a in everywhere] + [(0, b) for b in beyond]
     places += [(a, 1) for a in everywhere] + [(a, b) for a in across for b in beyond]
@@ -292,7 +250,7 @@
         for a in reversed(everywhere):
             sent, done = send([(a, b)], done)
             middle += sent
-    beside, _ = send([(a, 1) for a in everywhere], done)
+    beside, _ = send([(a, 1) for a in reversed(everywhere)], done)
     own, *last = local_call(
         functools.partial(split_kernel, 1 + len(crossed), rows),
         [(rows, width)] * len(merged),

time: 40.6 us -> 39.8 us (0.980)
  Pallas kernels: 15.6 us -> 11.2 us
  waiting for transfers between devices: 4.5 us -> 8.31 us
  starting transfers between devices: 19.4 us -> 17.8 us
  matrix products: 0 us -> 1.39 us
    ppermute x13, waiting for transfers between devices: 4.5 us -> 8.31 us  [swap(): return lax.ppermute(value, AXES, [(i, i ^ mask) for i in range(count)])]
    pallas_call x3 -> x2, Pallas kernels: 10.3 us -> 7.17 us  [sort_weights(): pl.pallas_call(functools.partial(sort_kernel, chunk, kinds, expert), out_...]
    ppermute x13, starting transfers between devices: 19.4 us -> 17.8 us  [swap(): return lax.ppermute(value, AXES, [(i, i ^ mask) for i in range(count)])]
    dot_general x0 -> x1, matrix products: none -> 1.39 us  [shards(): jnp.dot(hidden, down, preferred_element_type=jnp.float32)]
    pallas_call x1, Pallas kernels: 4.11 us -> 2.78 us  [experts(): pl.pallas_call(functools.partial(expert_kernel, chosen, pair, rows), out_...]
  transfers between devices with their start and end apart: 13 -> 13, of which waited for: 4 -> 6; matrix products, arithmetic and copies ran while one was open for 0% -> 0% of each run, Pallas kernels for 26% -> 19%
where the time goes in v6:
time: 39.8 us; the launch traced here: 39.6 us
  starting transfers between devices  17.8 us (45%)
  Pallas kernels  11.2 us (28%)
  waiting for transfers between devices  8.31 us (21%)
  matrix products  1.39 us (3%)
  other arithmetic  0.72 us (2%)
    ppermute x13, starting transfers between devices, swap(): return lax.ppermute(value, AXES, [(i, i ^ mask) for i in range(count)])  17.8 us
    ppermute x13, waiting for transfers between devices, swap(): return lax.ppermute(value, AXES, [(i, i ^ mask) for i in range(count)])  8.31 us
    pallas_call x2, Pallas kernels, sort_weights(): pl.pallas_call(functools.partial(sort_kernel, chunk, kinds, expert), out_...  7.17 us
    pallas_call x1, Pallas kernels, experts(): pl.pallas_call(functools.partial(expert_kernel, chosen, pair, rows), out_...  2.78 us
    dot_general x1, matrix products, shards(): jnp.dot(hidden, down, preferred_element_type=jnp.float32)  1.39 us
    pallas_call x1, Pallas kernels, pack(): pl.pallas_call(pack_kernel, out_shape=VMEM((rows, width + LANES), jnp.bfl...  0.85 us
  transfers between devices with their start and end apart: 13, of which 6 were waited for; matrix products, arithmetic and copies ran while one was open for 0% of the time, Pallas kernels for 19%

profile of v6, /device:TPU:0, one launch (start us, length us, event | category | flops | bytes accessed | tf_op | source)
XLA Modules:
  0.0 39.6 jit_solution(10848755036120746505)
XLA Ops:
  0.0 0.9 %shard_map.64.refs_0_ = bf16[4,7296]{1,0:T(4,128)(2,1)S(1)} custom-call(bf16[4,7168]{1,0:T(4,128)(2,1)} %tokens.1, bf16[4,4]{1,0:T(4,128)(2,1)} %gates.1, s32[2,4]{1,0:T(2,128)} %bitcast.14, s32[1,4]{1,0:T(1,128)} %source.1), custom_call_target="tpu_custom_call" | custom-call | tf_op jit(solution)/shard_map/pallas_call | solution.py:58
  0.9 3.0 %collective-permute-start = (bf16[4,7296]{1,0:T(4,128)(2,1)S(1)}, bf16[4,7296]{1,0:T(4,128)(2,1)S(1)}, u32[]{:S(2)}, u32[]{:S(2)}) collective-permute-start(bf16[4,7296]{1,0:T(4,128)(2,1)S(1)} %shard_map.64.refs_0_), channel_id=1, source_target_pairs={{0,8},{1,9},{2,10},{3,11},{4,12},{5,13},{6,14},{7,15},{8,0},{9,1},... | collective-permute-start | bytes 175112 | tf_op jit(solution)/shard_map/ppermute | solution.py:18
  3.9 3.6 %collective-permute-start.2 = (bf16[4,7296]{1,0:T(4,128)(2,1)S(1)}, bf16[4,7296]{1,0:T(4,128)(2,1)S(1)}, u32[]{:S(2)}, u32[]{:S(2)}) collective-permute-start(bf16[4,7296]{1,0:T(4,128)(2,1)S(1)} %shard_map.64.refs_0_), channel_id=1, source_target_pairs={{0,3},{1,2},{2,1},{3,0},{4,7},{5,6},{6,5},{7,4},{8,11},{9,10},{10,... | collective-permute-start | bytes 175112 | tf_op jit(solution)/shard_map/ppermute | solution.py:18
  7.5 0.0 collective-permute-start.1
  7.5 3.6 %shard_map.65 = (bf16[7168,512]{1,0:T(8,128)(2,1)S(1)}, bf16[16,128]{1,0:T(8,128)(2,1)S(1)}) custom-call(bf16[2,28672,128]{2,1,0:T(8,128)(2,1)} %bitcast.9), custom_call_target="tpu_custom_call" | custom-call | bytes 14680064 | tf_op jit(solution)/shard_map/pallas_call | solution.py:112
  11.1 0.8 %collective-permute-start.3 = (bf16[8,7296]{1,0:T(8,128)(2,1)S(1)}, bf16[8,7296]{1,0:T(8,128)(2,1)S(1)}, u32[]{:S(2)}, u32[]{:S(2)}) collective-permute-start(bf16[8,7296]{1,0:T(8,128)(2,1)S(1)} %shard_map.66.refs_0_), channel_id=1, source_target_pairs={{0,1},{1,0},{2,3},{3,2},{4,5},{5,4},{6,7},{7,6},{8,9},{9,8},{10,11... | collective-permute-start | bytes 350216 | tf_op jit(solution)/shard_map/ppermute | solution.py:18
  12.0 0.0 collective-permute-done.2.refs_1_
  12.0 0.6 %collective-permute-done.1.refs_0_ = bf16[4,7296]{1,0:T(4,128)(2,1)S(1)} collective-permute-done((bf16[4,7296]{1,0:T(4,128)(2,1)S(1)}, bf16[4,7296]{1,0:T(4,128)(2,1)S(1)}, u32[]{:S(2)}, u32[]{:S(2)}) %collective-permute-start.1) | collective-permute-done | bytes 58400 | tf_op jit(solution)/shard_map/ppermute | solution.py:18
  12.6 0.6 %collective-permute-start.4 = (bf16[8,7296]{1,0:T(8,128)(2,1)S(1)}, bf16[8,7296]{1,0:T(8,128)(2,1)S(1)}, u32[]{:S(2)}, u32[]{:S(2)}) collective-permute-start(bf16[8,7296]{1,0:T(8,128)(2,1)S(1)} %shard_map.67.refs_1_), channel_id=1, source_target_pairs={{0,8},{1,9},{2,10},{3,11},{4,12},{5,13},{6,14},{7,15},{8,0},{9,1},... | collective-permute-start | bytes 350216 | tf_op jit(solution)/shard_map/ppermute | solution.py:18
  13.2 3.6 %shard_map.68 = (bf16[7168,512]{1,0:T(8,128)(2,1)S(1)}, bf16[16,128]{1,0:T(8,128)(2,1)S(1)}) custom-call(bf16[2,28672,128]{2,1,0:T(8,128)(2,1)} %bitcast.10), custom_call_target="tpu_custom_call" | custom-call | bytes 14680064 | tf_op jit(solution)/shard_map/pallas_call | solution.py:112
  16.8 0.0 collective-permute-done.3.refs_2_
  16.8 0.7 %collective-permute-done.4.refs_3_ = bf16[8,7296]{1,0:T(8,128)(2,1)S(1)} collective-permute-done((bf16[8,7296]{1,0:T(8,128)(2,1)S(1)}, bf16[8,7296]{1,0:T(8,128)(2,1)S(1)}, u32[]{:S(2)}, u32[]{:S(2)}) %collective-permute-start.4) | collective-permute-done | bytes 116768 | tf_op jit(solution)/shard_map/ppermute | solution.py:18
  17.5 0.1 shard_map.69.near
  17.6 0.1 collective-permute-start.5
  17.6 1.8 %collective-permute-done.5.far = bf16[32,7296]{1,0:T(8,128)(2,1)S(1)} collective-permute-done((bf16[32,7296]{1,0:T(8,128)(2,1)S(1)}, bf16[32,7296]{1,0:T(8,128)(2,1)S(1)}, u32[]{:S(2)}, u32[]{:S(2)}) %collective-permute-start.5) | collective-permute-done | bytes 466976 | tf_op jit(solution)/shard_map/ppermute | solution.py:18
  19.5 2.8 %shard_map.70 = bf16[64,512]{1,0:T(8,128)(2,1)S(1)} custom-call(bf16[32,7296]{1,0:T(8,128)(2,1)S(1)} %shard_map.69.near, bf16[32,7296]{1,0:T(8,128)(2,1)S(1)} %collective-permute-done.5.far, bf16[7168,512]{1,0:T(8,128)(2,1)S(1)} %get-tuple-element.17.refs_0_, bf16[7168,512]{1,0:T(8,128)(2,1)S(1)} %get-tuple-element.18.refs_1_), custom_call_target="tpu_custom_call" | custom-call | flops 1409286144 | bytes 8388608 | tf_op jit(solution)/shard_map/pallas_call | solution.py:170
  22.3 1.4 %convolution_convert_fusion = bf16[64,7168]{1,0:T(8,128)(2,1)S(1)} fusion(bf16[64,512]{1,0:T(8,128)(2,1)S(1)} %shard_map.70, bf16[512,7168]{1,0:T(8,128)(2,1)S(1)} %bitcast.13), kind=kOutput, calls=%fused_computation | convolution fusion | flops 470220800 | bytes 8323072 | tf_op jit(solution)/shard_map/dot_general | solution.py:226
  23.7 0.1 fusion
  23.7 0.2 collective-permute-start.6
  23.9 1.7 %collective-permute-done.6.far = bf16[32,7168]{1,0:T(8,128)(2,1)S(1)} collective-permute-done((bf16[32,7168]{1,0:T(8,128)(2,1)S(1)}, bf16[32,7168]{1,0:T(8,128)(2,1)S(1)}, u32[]{:S(2)}, u32[]{:S(2)}) %collective-permute-start.6) | collective-permute-done | bytes 458784 | tf_op jit(solution)/shard_map/ppermute | solution.py:18
  25.6 0.1 shard_map.71
  25.7 0.9 %collective-permute-start.7 = (bf16[8,7168]{1,0:T(8,128)(2,1)S(1)}, bf16[8,7168]{1,0:T(8,128)(2,1)S(1)}, u32[]{:S(2)}, u32[]{:S(2)}) collective-permute-start(bf16[8,7168]{1,0:T(8,128)(2,1)S(1)} %get-tuple-element.20), channel_id=1, source_target_pairs={{0,8},{1,9},{2,10},{3,11},{4,12},{5,13},{6,14},{7,15},{8,0},{9,1},... | collective-permute-start | bytes 344072 | tf_op jit(solution)/shard_map/ppermute | solution.py:18
  26.7 3.7 %collective-permute-start.8 = (bf16[4,7168]{1,0:T(4,128)(2,1)S(1)}, bf16[4,7168]{1,0:T(4,128)(2,1)S(1)}, u32[]{:S(2)}, u32[]{:S(2)}) collective-permute-start(bf16[4,7168]{1,0:T(4,128)(2,1)S(1)} %shard_map.73.refs_0_), channel_id=1, source_target_pairs={{0,11},{1,10},{2,9},{3,8},{4,15},{5,14},{6,13},{7,12},{8,3},{9,2},... | collective-permute-start | bytes 172040 | tf_op jit(solution)/shard_map/ppermute | solution.py:18
  30.4 0.9 %collective-permute-start.9 = (bf16[4,7168]{1,0:T(4,128)(2,1)S(1)}, bf16[4,7168]{1,0:T(4,128)(2,1)S(1)}, u32[]{:S(2)}, u32[]{:S(2)}) collective-permute-start(bf16[4,7168]{1,0:T(4,128)(2,1)S(1)} %shard_map.74.refs_0_), channel_id=1, source_target_pairs={{0,3},{1,2},{2,1},{3,0},{4,7},{5,6},{6,5},{7,4},{8,11},{9,10},{10,... | collective-permute-start | bytes 172040 | tf_op jit(solution)/shard_map/ppermute | solution.py:18
  31.3 0.1 collective-permute-start.10
  31.4 2.3 %collective-permute-start.11 = (bf16[4,7168]{1,0:T(4,128)(2,1)S(1)}, bf16[4,7168]{1,0:T(4,128)(2,1)S(1)}, u32[]{:S(2)}, u32[]{:S(2)}) collective-permute-start(bf16[4,7168]{1,0:T(4,128)(2,1)S(1)} %get-tuple-element.23), channel_id=1, source_target_pairs={{0,1},{1,0},{2,3},{3,2},{4,5},{5,4},{6,7},{7,6},{8,9},{9,8},{10,11... | collective-permute-start | bytes 172040 | tf_op jit(solution)/shard_map/ppermute | solution.py:18
  33.7 1.6 %collective-permute-start.12 = (bf16[4,7168]{1,0:T(4,128)(2,1)S(1)}, bf16[4,7168]{1,0:T(4,128)(2,1)S(1)}, u32[]{:S(2)}, u32[]{:S(2)}) collective-permute-start(bf16[4,7168]{1,0:T(4,128)(2,1)S(1)} %get-tuple-element.24), channel_id=1, source_target_pairs={{0,2},{1,3},{2,0},{3,1},{4,6},{5,7},{6,4},{7,5},{8,10},{9,11},{10,... | collective-permute-start | bytes 172040 | tf_op jit(solution)/shard_map/ppermute | solution.py:18
  35.4 2.5 %collective-permute-done.10 = bf16[4,7168]{1,0:T(4,128)(2,1)S(1)} collective-permute-done((bf16[4,7168]{1,0:T(4,128)(2,1)S(1)}, bf16[4,7168]{1,0:T(4,128)(2,1)S(1)}, u32[]{:S(2)}, u32[]{:S(2)}) %collective-permute-start.10) | collective-permute-done | bytes 57376 | tf_op jit(solution)/shard_map/ppermute | solution.py:18
  37.9 0.0 collective-permute-done.11
  37.9 0.0 collective-permute-done.9
  37.9 1.0 %collective-permute-done.12 = bf16[4,7168]{1,0:T(4,128)(2,1)S(1)} collective-permute-done((bf16[4,7168]{1,0:T(4,128)(2,1)S(1)}, bf16[4,7168]{1,0:T(4,128)(2,1)S(1)}, u32[]{:S(2)}, u32[]{:S(2)}) %collective-permute-start.12) | collective-permute-done | bytes 57376 | tf_op jit(solution)/shard_map/ppermute | solution.py:18
  38.9 0.7 %add_convert_fusion = bf16[4,7168]{1,0:T(4,128)(2,1)} fusion(bf16[4,7168]{1,0:T(4,128)(2,1)S(1)} %collective-permute-done.12, bf16[4,7168]{1,0:T(4,128)(2,1)S(1)} %collective-permute-done.11, bf16[4,7168]{1,0:T(4,128)(2,1)S(1)} %collective-permute-done.10, bf16[4,7168]{1,0:T(4,128)(2,1)S(1)} %collective-permute-done.9, ...), kind=kLoop, calls=%fused_computation.1 | loop fusion | flops 344064 | bytes 401408 | tf_op jit(solution)/shard_map/convert_element_type | solution.py:260
  (14 shorter events, 0.2 us)
Async XLA Ops:
  0.9 10.2 %collective-permute-start = (bf16[4,7296]{1,0:T(4,128)(2,1)S(1)}, bf16[4,7296]{1,0:T(4,128)(2,1)S(1)}, u32[]{:S(2)}, u32[]{:S(2)}) collective-permute-start(bf16[4,7296]{1,0:T(4,128)(2,1)S(1)} %shard_map.64.refs_0_), channel_id=1, source_target_pairs={{0,8},{1,9},{2,10},{3,11},{4,12},{5,13},{6,14},{7,15},{8,0},{9,1},... | collective-permute-start | bytes 175112 | tf_op jit(solution)/shard_map/ppermute | solution.py:18
  3.9 8.1 %collective-permute-start.2 = (bf16[4,7296]{1,0:T(4,128)(2,1)S(1)}, bf16[4,7296]{1,0:T(4,128)(2,1)S(1)}, u32[]{:S(2)}, u32[]{:S(2)}) collective-permute-start(bf16[4,7296]{1,0:T(4,128)(2,1)S(1)} %shard_map.64.refs_0_), channel_id=1, source_target_pairs={{0,3},{1,2},{2,1},{3,0},{4,7},{5,6},{6,5},{7,4},{8,11},{9,10},{10,... | collective-permute-start | bytes 175112 | tf_op jit(solution)/shard_map/ppermute | solution.py:18
  7.5 5.1 %collective-permute-start.1 = (bf16[4,7296]{1,0:T(4,128)(2,1)S(1)}, bf16[4,7296]{1,0:T(4,128)(2,1)S(1)}, u32[]{:S(2)}, u32[]{:S(2)}) collective-permute-start(bf16[4,7296]{1,0:T(4,128)(2,1)S(1)} %shard_map.64.refs_0_), channel_id=1, source_target_pairs={{0,2},{1,3},{2,0},{3,1},{4,6},{5,7},{6,4},{7,5},{8,10},{9,11},{10,... | collective-permute-start | bytes 175112 | tf_op jit(solution)/shard_map/ppermute | solution.py:18
  11.1 5.7 %collective-permute-start.3 = (bf16[8,7296]{1,0:T(8,128)(2,1)S(1)}, bf16[8,7296]{1,0:T(8,128)(2,1)S(1)}, u32[]{:S(2)}, u32[]{:S(2)}) collective-permute-start(bf16[8,7296]{1,0:T(8,128)(2,1)S(1)} %shard_map.66.refs_0_), channel_id=1, source_target_pairs={{0,1},{1,0},{2,3},{3,2},{4,5},{5,4},{6,7},{7,6},{8,9},{9,8},{10,11... | collective-permute-start | bytes 350216 | tf_op jit(solution)/shard_map/ppermute | solution.py:18
  12.6 4.9 %collective-permute-start.4 = (bf16[8,7296]{1,0:T(8,128)(2,1)S(1)}, bf16[8,7296]{1,0:T(8,128)(2,1)S(1)}, u32[]{:S(2)}, u32[]{:S(2)}) collective-permute-start(bf16[8,7296]{1,0:T(8,128)(2,1)S(1)} %shard_map.67.refs_1_), channel_id=1, source_target_pairs={{0,8},{1,9},{2,10},{3,11},{4,12},{5,13},{6,14},{7,15},{8,0},{9,1},... | collective-permute-start | bytes 350216 | tf_op jit(solution)/shard_map/ppermute | solution.py:18
  17.5 4.8 %slice-start = ((s8[7340032]{0:T(1024)(128)(4,1)}), s8[4194304]{0:T(1024)(128)(4,1)S(1)}, s32[]{:S(2)}) async-start(s8[7340032]{0:T(1024)(128)(4,1)} %bitcast.11), calls=%async_computation | async-start | bytes 8388608
  17.6 1.9 %collective-permute-start.5 = (bf16[32,7296]{1,0:T(8,128)(2,1)S(1)}, bf16[32,7296]{1,0:T(8,128)(2,1)S(1)}, u32[]{:S(2)}, u32[]{:S(2)}) collective-permute-start(bf16[32,7296]{1,0:T(8,128)(2,1)S(1)} %shard_map.69.near), channel_id=1, source_target_pairs={{0,4},{1,5},{2,6},{3,7},{4,0},{5,1},{6,2},{7,3},{8,12},{9,13},{10,... | collective-permute-start | bytes 1400840 | tf_op jit(solution)/shard_map/ppermute | solution.py:18
  19.4 2.8 %slice-start.1 = ((s8[7340032]{0:T(1024)(128)(4,1)}), s8[3145728]{0:T(1024)(128)(4,1)S(1)}, s32[]{:S(2)}) async-start(s8[7340032]{0:T(1024)(128)(4,1)} %bitcast.11), calls=%async_computation.1 | async-start | bytes 6291456
  23.7 1.9 %collective-permute-start.6 = (bf16[32,7168]{1,0:T(8,128)(2,1)S(1)}, bf16[32,7168]{1,0:T(8,128)(2,1)S(1)}, u32[]{:S(2)}, u32[]{:S(2)}) collective-permute-start(bf16[32,7168]{1,0:T(8,128)(2,1)S(1)} %get-tuple-element.25), channel_id=1, source_target_pairs={{0,4},{1,5},{2,6},{3,7},{4,0},{5,1},{6,2},{7,3},{8,12},{9,13},{10,... | collective-permute-start | bytes 1376264 | tf_op jit(solution)/shard_map/ppermute | solution.py:18
  25.7 8.0 %collective-permute-start.7 = (bf16[8,7168]{1,0:T(8,128)(2,1)S(1)}, bf16[8,7168]{1,0:T(8,128)(2,1)S(1)}, u32[]{:S(2)}, u32[]{:S(2)}) collective-permute-start(bf16[8,7168]{1,0:T(8,128)(2,1)S(1)} %get-tuple-element.20), channel_id=1, source_target_pairs={{0,8},{1,9},{2,10},{3,11},{4,12},{5,13},{6,14},{7,15},{8,0},{9,1},... | collective-permute-start | bytes 344072 | tf_op jit(solution)/shard_map/ppermute | solution.py:18
  26.7 11.2 %collective-permute-start.8 = (bf16[4,7168]{1,0:T(4,128)(2,1)S(1)}, bf16[4,7168]{1,0:T(4,128)(2,1)S(1)}, u32[]{:S(2)}, u32[]{:S(2)}) collective-permute-start(bf16[4,7168]{1,0:T(4,128)(2,1)S(1)} %shard_map.73.refs_0_), channel_id=1, source_target_pairs={{0,11},{1,10},{2,9},{3,8},{4,15},{5,14},{6,13},{7,12},{8,3},{9,2},... | collective-permute-start | bytes 172040 | tf_op jit(solution)/shard_map/ppermute | solution.py:18
  30.4 7.5 %collective-permute-start.9 = (bf16[4,7168]{1,0:T(4,128)(2,1)S(1)}, bf16[4,7168]{1,0:T(4,128)(2,1)S(1)}, u32[]{:S(2)}, u32[]{:S(2)}) collective-permute-start(bf16[4,7168]{1,0:T(4,128)(2,1)S(1)} %shard_map.74.refs_0_), channel_id=1, source_target_pairs={{0,3},{1,2},{2,1},{3,0},{4,7},{5,6},{6,5},{7,4},{8,11},{9,10},{10,... | collective-permute-start | bytes 172040 | tf_op jit(solution)/shard_map/ppermute | solution.py:18
  31.3 6.5 %collective-permute-start.10 = (bf16[4,7168]{1,0:T(4,128)(2,1)S(1)}, bf16[4,7168]{1,0:T(4,128)(2,1)S(1)}, u32[]{:S(2)}, u32[]{:S(2)}) collective-permute-start(bf16[4,7168]{1,0:T(4,128)(2,1)S(1)} %get-tuple-element.22), channel_id=1, source_target_pairs={{0,9},{1,8},{2,11},{3,10},{4,13},{5,12},{6,15},{7,14},{8,1},{9,0},... | collective-permute-start | bytes 172040 | tf_op jit(solution)/shard_map/ppermute | solution.py:18
  31.4 6.5 %collective-permute-start.11 = (bf16[4,7168]{1,0:T(4,128)(2,1)S(1)}, bf16[4,7168]{1,0:T(4,128)(2,1)S(1)}, u32[]{:S(2)}, u32[]{:S(2)}) collective-permute-start(bf16[4,7168]{1,0:T(4,128)(2,1)S(1)} %get-tuple-element.23), channel_id=1, source_target_pairs={{0,1},{1,0},{2,3},{3,2},{4,5},{5,4},{6,7},{7,6},{8,9},{9,8},{10,11... | collective-permute-start | bytes 172040 | tf_op jit(solution)/shard_map/ppermute | solution.py:18
  33.7 5.2 %collective-permute-start.12 = (bf16[4,7168]{1,0:T(4,128)(2,1)S(1)}, bf16[4,7168]{1,0:T(4,128)(2,1)S(1)}, u32[]{:S(2)}, u32[]{:S(2)}) collective-permute-start(bf16[4,7168]{1,0:T(4,128)(2,1)S(1)} %get-tuple-element.24), channel_id=1, source_target_pairs={{0,2},{1,3},{2,0},{3,1},{4,6},{5,7},{6,4},{7,5},{8,10},{9,11},{10,... | collective-permute-start | bytes 172040 | tf_op jit(solution)/shard_map/ppermute | solution.py:18

commit v7 on v6

--- a/solution.py
+++ b/solution.py
@@ -131,16 +131,17 @@
     ]
 
 
-def expert_kernel(chosen, pair, rows, near, far, *refs):
-    weight_in = refs[:pair]
-    hidden, held = refs[pair:]
-    half = near.shape[0]
+def expert_kernel(chosen, pair, rows, blocks, *refs):
+    weight_in = refs[blocks:-2]
+    hidden, held = refs[-2:]
+    total = held.shape[0]
     depth, columns = weight_in[0].shape
     units = columns // 2
     slots = chosen // pair
-    total = 2 * half
-    held[:half] = near[...]
-    held[half:] = far[...]
+    at = 0
+    for block in refs[:blocks]:
+        held[at : at + block.shape[0]] = block[...]
+        at += block.shape[0]
     tail = held[:, depth:].astype(jnp.float32)
     node = lax.axis_index("node").astype(jnp.float32)
     active = []
@@ -163,23 +164,21 @@
     ).astype(jnp.bfloat16)
 
 
-def experts(chosen, rows, near, far, weight_in):
-    half = near.shape[0]
+def experts(chosen, rows, blocks, weight_in):
+    total = sum(a.shape[0] for a in blocks)
     pair = len(weight_in)
-    depth, columns = weight_in[0].shape
+    columns = weight_in[0].shape[1]
     return pl.pallas_call(
-        functools.partial(expert_kernel, chosen, pair, rows),
-        out_shape=VMEM((2 * half, pair * columns // 2), jnp.bfloat16),
-        in_specs=in_vmem(2 + pair),
+        functools.partial(expert_kernel, chosen, pair, rows, len(blocks)),
+        out_shape=VMEM((total, pair * columns // 2), jnp.bfloat16),
+        in_specs=in_vmem(len(blocks) + pair),
         out_specs=pl.BlockSpec(memory_space=VMEM),
-        scratch_shapes=[
-            VMEM((2 * half, near.shape[1]), jnp.bfloat16),
-        ],
+        scratch_shapes=[VMEM((total, blocks[0].shape[1]), jnp.bfloat16)],
         compiler_params=pltpu.CompilerParams(vmem_limit_bytes=20 << 20),
         cost_estimate=pl.CostEstimate(
-            flops=6 * half * pair * weight_in[0].size, bytes_accessed=8 << 20, transcendentals=0
+            flops=3 * total * pair * weight_in[0].size, bytes_accessed=8 << 20, transcendentals=0
         ),
-    )(*hold(near, far, *weight_in))
+    )(*hold(*blocks, *weight_in))
 
 
 def join(operands, *after):
@@ -199,9 +198,12 @@
         out[...] = jnp.concatenate(pieces, axis=0).astype(jnp.bfloat16)
 
 
-def split_kernel(count, rows, *refs):
-    total = sum(r[...].astype(jnp.float32) for r in refs[:count])
-    for i, out in enumerate(refs[count:]):
+def split_kernel(rows, tops, count, begin, kept, *refs):
+    outs = refs[len(refs) - tops :] if tops else refs[count:]
+    size = len(outs) * rows
+    total = kept[...].astype(jnp.float32)[begin : begin + size]
+    total += sum(r[...].astype(jnp.float32) for r in refs[:count])
+    for i, out in enumerate(outs):
         out[...] = total[i * rows : (i + 1) * rows].astype(jnp.bfloat16)
 
 
@@ -218,11 +220,13 @@
     tail = [swap(message, k, count) for k in beyond]
     head = [message] + [swap(message, a * step, count) for a in across]
     head, tail = join(head, early[0]), join(tail, early[0])
-    near = [head, tail, swap(head, 1, count)] + [swap(tail, a * step, count) for a in across]
-    near = join(near, *early[1:])
-    hidden = experts(gates.shape[1], rows, near, swap(near, locals_, count), weights)
+    near = join([head, tail])
+    far = swap(near, locals_, count)
+    side = [swap(head, 1, count)] + [swap(tail, a * step, count) for a in across]
+    side = join(side, *early[1:])
+    hidden = experts(gates.shape[1], rows, [near, side, far, swap(side, locals_, count)], weights)
     down = expert_out.reshape(-1, width)
-    half = near.shape[0]
+    half = hidden.shape[0] // 2
     out = jnp.dot(hidden, down, preferred_element_type=jnp.float32).astype(jnp.bfloat16)
     near_out, far_out = out[:half], out[half:]
     everywhere = [0, *across]
@@ -230,7 +234,7 @@
     places += [(a, 1) for a in everywhere] + [(a, b) for a in across for b in beyond]
     index = {place: i for i, place in enumerate(places)}
     far_got = swap(far_out, locals_, count)
-    merged = [0, *range(2, locals_, 2)]
+    even = range(2, locals_, 2)
 
     def fold(groups, *after):
         return local_call(
@@ -243,21 +247,32 @@
         arrays = fold([[p] for p in blocks], after)
         return [swap(v, a * step + b, count) for v, (a, b) in zip(arrays, blocks)], arrays[0]
 
-    kept, *crossing = fold([[(a, b) for b in merged] for a in everywhere])
+    tops = [(a, 0) for a in everywhere]
+    lows = [(0, b) for b in even]
+    kept, *crossing = fold(
+        [tops + lows, *[[(a, b) for b in even] for a in across]]
+    )
     crossed = [swap(v, a * step, count) for a, v in zip(across, crossing)]
     middle, done = [], kept
     for b in range(3, locals_, 2):
         for a in reversed(everywhere):
             sent, done = send([(a, b)], done)
             middle += sent
-    beside, _ = send([(a, 1) for a in reversed(everywhere)], done)
-    own, *last = local_call(
-        functools.partial(split_kernel, 1 + len(crossed), rows),
-        [(rows, width)] * len(merged),
+    side, = fold([[(a, 1) for a in everywhere]], done)
+    side = swap(side, 1, count)
+    low_parts = local_call(
+        functools.partial(split_kernel, rows, 0, len(crossed), len(tops) * rows),
+        [(rows, width)] * len(lows),
         [kept, *crossed],
     )
-    last = [swap(v, b, count) for v, b in zip(last, merged[1:])]
-    return sum(v.astype(jnp.float32) for v in [own, *middle, *beside, *last]).astype(jnp.bfloat16)
+    own, *top_parts = local_call(
+        functools.partial(split_kernel, rows, len(tops), 1, 0),
+        [(rows, width)] * len(tops),
+        [kept, side, low_parts[0]],
+    )
+    last = [swap(v, b, count) for v, (_, b) in zip(low_parts, lows)]
+    last += [swap(v, a * step, count) for v, (a, _) in zip(top_parts, tops[1:])]
+    return sum(v.astype(jnp.float32) for v in [own, *middle, *last]).astype(jnp.bfloat16)
 
 
 def solution(mesh):

time: 39.8 us -> 39.3 us (0.987)
    ppermute x13 -> x14, starting transfers between devices: 17.8 us -> 17.5 us  [swap(): return lax.ppermute(value, AXES, [(i, i ^ mask) for i in range(count)])]
    ppermute x13 -> x14, waiting for transfers between devices: 8.31 us -> 8.08 us  [swap(): return lax.ppermute(value, AXES, [(i, i ^ mask) for i in range(count)])]
  transfers between devices with their start and end apart: 13 -> 14, of which waited for: 6 -> 7; matrix products, arithmetic and copies ran while one was open for 0% -> 0% of each run, Pallas kernels for 19% -> 19%
where the time goes in v7:
time: 39.3 us; the launch traced here: 39.1 us
  starting transfers between devices  17.5 us (45%)
  Pallas kernels  11.2 us (28%)
  waiting for transfers between devices  8.08 us (21%)
  matrix products  1.39 us (4%)
  other arithmetic  0.7 us (2%)
    ppermute x14, starting transfers between devices, swap(): return lax.ppermute(value, AXES, [(i, i ^ mask) for i in range(count)])  17.5 us
    ppermute x14, waiting for transfers between devices, swap(): return lax.ppermute(value, AXES, [(i, i ^ mask) for i in range(count)])  8.08 us
    pallas_call x2, Pallas kernels, sort_weights(): pl.pallas_call(functools.partial(sort_kernel, chunk, kinds, expert), out_...  7.17 us
    pallas_call x1, Pallas kernels, experts(): pl.pallas_call(functools.partial(expert_kernel, chosen, pair, rows, len(b...  2.8 us
    dot_general x1, matrix products, shards(): jnp.dot(hidden, down, preferred_element_type=jnp.float32)  1.39 us
    pallas_call x1, Pallas kernels, pack(): pl.pallas_call(pack_kernel, out_shape=VMEM((rows, width + LANES), jnp.bfl...  0.85 us
  transfers between devices with their start and end apart: 14, of which 7 were waited for; matrix products, arithmetic and copies ran while one was open for 0% of the time, Pallas kernels for 19%

profile of v7, /device:TPU:0, one launch (start us, length us, event | category | flops | bytes accessed | tf_op | source)
XLA Modules:
  0.0 39.1 jit_solution(4168477006275423402)
XLA Ops:
  0.0 0.9 %shard_map.64.refs_0_ = bf16[4,7296]{1,0:T(4,128)(2,1)S(1)} custom-call(bf16[4,7168]{1,0:T(4,128)(2,1)} %tokens.1, bf16[4,4]{1,0:T(4,128)(2,1)} %gates.1, s32[2,4]{1,0:T(2,128)} %bitcast.14, s32[1,4]{1,0:T(1,128)} %source.1), custom_call_target="tpu_custom_call" | custom-call | tf_op jit(solution)/shard_map/pallas_call | solution.py:58
  0.9 3.0 %collective-permute-start = (bf16[4,7296]{1,0:T(4,128)(2,1)S(1)}, bf16[4,7296]{1,0:T(4,128)(2,1)S(1)}, u32[]{:S(2)}, u32[]{:S(2)}) collective-permute-start(bf16[4,7296]{1,0:T(4,128)(2,1)S(1)} %shard_map.64.refs_0_), channel_id=1, source_target_pairs={{0,8},{1,9},{2,10},{3,11},{4,12},{5,13},{6,14},{7,15},{8,0},{9,1},... | collective-permute-start | bytes 175112 | tf_op jit(solution)/shard_map/ppermute | solution.py:18
  3.9 3.6 %collective-permute-start.2 = (bf16[4,7296]{1,0:T(4,128)(2,1)S(1)}, bf16[4,7296]{1,0:T(4,128)(2,1)S(1)}, u32[]{:S(2)}, u32[]{:S(2)}) collective-permute-start(bf16[4,7296]{1,0:T(4,128)(2,1)S(1)} %shard_map.64.refs_0_), channel_id=1, source_target_pairs={{0,3},{1,2},{2,1},{3,0},{4,7},{5,6},{6,5},{7,4},{8,11},{9,10},{10,... | collective-permute-start | bytes 175112 | tf_op jit(solution)/shard_map/ppermute | solution.py:18
  7.5 3.6 %shard_map.65 = (bf16[7168,512]{1,0:T(8,128)(2,1)S(1)}, bf16[16,128]{1,0:T(8,128)(2,1)S(1)}) custom-call(bf16[2,28672,128]{2,1,0:T(8,128)(2,1)} %bitcast.9), custom_call_target="tpu_custom_call" | custom-call | bytes 14680064 | tf_op jit(solution)/shard_map/pallas_call | solution.py:112
  11.1 0.0 collective-permute-done.refs_1_
  11.1 0.8 %collective-permute-start.3 = (bf16[8,7296]{1,0:T(8,128)(2,1)S(1)}, bf16[8,7296]{1,0:T(8,128)(2,1)S(1)}, u32[]{:S(2)}, u32[]{:S(2)}) collective-permute-start(bf16[8,7296]{1,0:T(8,128)(2,1)S(1)} %shard_map.66.refs_0_), channel_id=1, source_target_pairs={{0,1},{1,0},{2,3},{3,2},{4,5},{5,4},{6,7},{7,6},{8,9},{9,8},{10,11... | collective-permute-start | bytes 350216 | tf_op jit(solution)/shard_map/ppermute | solution.py:18
  12.0 0.6 %collective-permute-done.1.refs_0_ = bf16[4,7296]{1,0:T(4,128)(2,1)S(1)} collective-permute-done((bf16[4,7296]{1,0:T(4,128)(2,1)S(1)}, bf16[4,7296]{1,0:T(4,128)(2,1)S(1)}, u32[]{:S(2)}, u32[]{:S(2)}) %collective-permute-start.1) | collective-permute-done | bytes 58400 | tf_op jit(solution)/shard_map/ppermute | solution.py:18
  12.6 0.6 %collective-permute-start.4 = (bf16[8,7296]{1,0:T(8,128)(2,1)S(1)}, bf16[8,7296]{1,0:T(8,128)(2,1)S(1)}, u32[]{:S(2)}, u32[]{:S(2)}) collective-permute-start(bf16[8,7296]{1,0:T(8,128)(2,1)S(1)} %shard_map.67.refs_1_), channel_id=1, source_target_pairs={{0,8},{1,9},{2,10},{3,11},{4,12},{5,13},{6,14},{7,15},{8,0},{9,1},... | collective-permute-start | bytes 350216 | tf_op jit(solution)/shard_map/ppermute | solution.py:18
  13.2 3.6 %shard_map.69 = (bf16[7168,512]{1,0:T(8,128)(2,1)S(1)}, bf16[16,128]{1,0:T(8,128)(2,1)S(1)}) custom-call(bf16[2,28672,128]{2,1,0:T(8,128)(2,1)} %bitcast.10), custom_call_target="tpu_custom_call" | custom-call | bytes 14680064 | tf_op jit(solution)/shard_map/pallas_call | solution.py:112
  16.8 0.1 collective-permute-start.5
  16.9 0.0 collective-permute-done.3.refs_0_
  16.9 0.6 %collective-permute-done.4.refs_1_ = bf16[8,7296]{1,0:T(8,128)(2,1)S(1)} collective-permute-done((bf16[8,7296]{1,0:T(8,128)(2,1)S(1)}, bf16[8,7296]{1,0:T(8,128)(2,1)S(1)}, u32[]{:S(2)}, u32[]{:S(2)}) %collective-permute-start.4) | collective-permute-done | bytes 116768 | tf_op jit(solution)/shard_map/ppermute | solution.py:18
  17.5 0.1 collective-permute-start.6
  17.6 0.8 %collective-permute-done.5.refs_2_ = bf16[16,7296]{1,0:T(8,128)(2,1)S(1)} collective-permute-done((bf16[16,7296]{1,0:T(8,128)(2,1)S(1)}, bf16[16,7296]{1,0:T(8,128)(2,1)S(1)}, u32[]{:S(2)}, u32[]{:S(2)}) %collective-permute-start.5) | collective-permute-done | bytes 233504 | tf_op jit(solution)/shard_map/ppermute | solution.py:18
  18.4 0.7 %collective-permute-done.6.refs_3_ = bf16[16,7296]{1,0:T(8,128)(2,1)S(1)} collective-permute-done((bf16[16,7296]{1,0:T(8,128)(2,1)S(1)}, bf16[16,7296]{1,0:T(8,128)(2,1)S(1)}, u32[]{:S(2)}, u32[]{:S(2)}) %collective-permute-start.6) | collective-permute-done | bytes 233504 | tf_op jit(solution)/shard_map/ppermute | solution.py:18
  19.1 2.8 %shard_map.71 = bf16[64,512]{1,0:T(8,128)(2,1)S(1)} custom-call(bf16[16,7296]{1,0:T(8,128)(2,1)S(1)} %shard_map.68.refs_0_, bf16[16,7296]{1,0:T(8,128)(2,1)S(1)} %shard_map.70.refs_1_, bf16[16,7296]{1,0:T(8,128)(2,1)S(1)} %collective-permute-done.5.refs_2_, bf16[16,7296]{1,0:T(8,128)(2,1)S(1)} %collective-permute-done.6.refs_3_, ...), custom_call_target="tpu_custom_call" | custom-call | flops 1409286144 | bytes 8388608 | tf_op jit(solution)/shard_map/pallas_call | solution.py:171
  21.9 1.4 %convolution_convert_fusion = bf16[64,7168]{1,0:T(8,128)(2,1)S(1)} fusion(bf16[64,512]{1,0:T(8,128)(2,1)S(1)} %shard_map.71, bf16[512,7168]{1,0:T(8,128)(2,1)S(1)} %bitcast.13), kind=kOutput, calls=%fused_computation | convolution fusion | flops 470220800 | bytes 8323072 | tf_op jit(solution)/shard_map/dot_general | solution.py:230
  23.3 0.1 fusion
  23.4 0.2 collective-permute-start.7
  23.6 1.7 %collective-permute-done.7.far = bf16[32,7168]{1,0:T(8,128)(2,1)S(1)} collective-permute-done((bf16[32,7168]{1,0:T(8,128)(2,1)S(1)}, bf16[32,7168]{1,0:T(8,128)(2,1)S(1)}, u32[]{:S(2)}, u32[]{:S(2)}) %collective-permute-start.7) | collective-permute-done | bytes 458784 | tf_op jit(solution)/shard_map/ppermute | solution.py:18
  25.3 0.1 shard_map.72
  25.5 0.7 %collective-permute-start.8 = (bf16[8,7168]{1,0:T(8,128)(2,1)S(1)}, bf16[8,7168]{1,0:T(8,128)(2,1)S(1)}, u32[]{:S(2)}, u32[]{:S(2)}) collective-permute-start(bf16[8,7168]{1,0:T(8,128)(2,1)S(1)} %shard_map.75), channel_id=1, source_target_pairs={{0,1},{1,0},{2,3},{3,2},{4,5},{5,4},{6,7},{7,6},{8,9},{9,8},{10,11... | collective-permute-start | bytes 344072 | tf_op jit(solution)/shard_map/ppermute | solution.py:18
  26.2 1.2 %collective-permute-start.9 = (bf16[4,7168]{1,0:T(4,128)(2,1)S(1)}, bf16[4,7168]{1,0:T(4,128)(2,1)S(1)}, u32[]{:S(2)}, u32[]{:S(2)}) collective-permute-start(bf16[4,7168]{1,0:T(4,128)(2,1)S(1)} %get-tuple-element.18), channel_id=1, source_target_pairs={{0,8},{1,9},{2,10},{3,11},{4,12},{5,13},{6,14},{7,15},{8,0},{9,1},... | collective-permute-start | bytes 172040 | tf_op jit(solution)/shard_map/ppermute | solution.py:18
  27.4 2.4 %collective-permute-start.11 = (bf16[4,7168]{1,0:T(4,128)(2,1)S(1)}, bf16[4,7168]{1,0:T(4,128)(2,1)S(1)}, u32[]{:S(2)}, u32[]{:S(2)}) collective-permute-start(bf16[4,7168]{1,0:T(4,128)(2,1)S(1)} %shard_map.74.refs_0_), channel_id=1, source_target_pairs={{0,3},{1,2},{2,1},{3,0},{4,7},{5,6},{6,5},{7,4},{8,11},{9,10},{10,... | collective-permute-start | bytes 172040 | tf_op jit(solution)/shard_map/ppermute | solution.py:18
  29.8 1.7 %collective-permute-start.10 = (bf16[4,7168]{1,0:T(4,128)(2,1)S(1)}, bf16[4,7168]{1,0:T(4,128)(2,1)S(1)}, u32[]{:S(2)}, u32[]{:S(2)}) collective-permute-start(bf16[4,7168]{1,0:T(4,128)(2,1)S(1)} %shard_map.73.refs_0_), channel_id=1, source_target_pairs={{0,11},{1,10},{2,9},{3,8},{4,15},{5,14},{6,13},{7,12},{8,3},{9,2},... | collective-permute-start | bytes 172040 | tf_op jit(solution)/shard_map/ppermute | solution.py:18
  31.5 0.0 collective-permute-done.9.refs_0_
  31.5 1.9 %collective-permute-start.12 = (bf16[4,7168]{1,0:T(4,128)(2,1)S(1)}, bf16[4,7168]{1,0:T(4,128)(2,1)S(1)}, u32[]{:S(2)}, u32[]{:S(2)}) collective-permute-start(bf16[4,7168]{1,0:T(4,128)(2,1)S(1)} %shard_map.76.refs_1_), channel_id=1, source_target_pairs={{0,2},{1,3},{2,0},{3,1},{4,6},{5,7},{6,4},{7,5},{8,10},{9,11},{10,... | collective-permute-start | bytes 172040 | tf_op jit(solution)/shard_map/ppermute | solution.py:18
  33.4 0.0 collective-permute-done.8.refs_0_
  33.5 1.2 %collective-permute-start.13 = (bf16[4,7168]{1,0:T(4,128)(2,1)S(1)}, bf16[4,7168]{1,0:T(4,128)(2,1)S(1)}, u32[]{:S(2)}, u32[]{:S(2)}) collective-permute-start(bf16[4,7168]{1,0:T(4,128)(2,1)S(1)} %get-tuple-element.20), channel_id=1, source_target_pairs={{0,8},{1,9},{2,10},{3,11},{4,12},{5,13},{6,14},{7,15},{8,0},{9,1},... | collective-permute-start | bytes 172040 | tf_op jit(solution)/shard_map/ppermute | solution.py:18
  34.7 2.1 %collective-permute-done.10 = bf16[4,7168]{1,0:T(4,128)(2,1)S(1)} collective-permute-done((bf16[4,7168]{1,0:T(4,128)(2,1)S(1)}, bf16[4,7168]{1,0:T(4,128)(2,1)S(1)}, u32[]{:S(2)}, u32[]{:S(2)}) %collective-permute-start.10) | collective-permute-done | bytes 57376 | tf_op jit(solution)/shard_map/ppermute | solution.py:18
  36.8 1.7 %collective-permute-done.12 = bf16[4,7168]{1,0:T(4,128)(2,1)S(1)} collective-permute-done((bf16[4,7168]{1,0:T(4,128)(2,1)S(1)}, bf16[4,7168]{1,0:T(4,128)(2,1)S(1)}, u32[]{:S(2)}, u32[]{:S(2)}) %collective-permute-start.12) | collective-permute-done | bytes 57376 | tf_op jit(solution)/shard_map/ppermute | solution.py:18
  38.4 0.7 %add_convert_fusion = bf16[4,7168]{1,0:T(4,128)(2,1)} fusion(bf16[4,7168]{1,0:T(4,128)(2,1)S(1)} %collective-permute-done.13, bf16[4,7168]{1,0:T(4,128)(2,1)S(1)} %collective-permute-done.12, bf16[4,7168]{1,0:T(4,128)(2,1)S(1)} %collective-permute-done.11, bf16[4,7168]{1,0:T(4,128)(2,1)S(1)} %collective-permute-done.10, bf16[4,7168]{1,0:T(4,128)(2,1)S(1)} %get-tuple-element.19), kind=kLoop, calls=%fused_computation.1 | loop fusion | flops 286720 | bytes 344064 | tf_op jit(solution)/shard_map/convert_element_type | solution.py:275
  (18 shorter events, 0.4 us)
Async XLA Ops:
  0.9 10.2 %collective-permute-start = (bf16[4,7296]{1,0:T(4,128)(2,1)S(1)}, bf16[4,7296]{1,0:T(4,128)(2,1)S(1)}, u32[]{:S(2)}, u32[]{:S(2)}) collective-permute-start(bf16[4,7296]{1,0:T(4,128)(2,1)S(1)} %shard_map.64.refs_0_), channel_id=1, source_target_pairs={{0,8},{1,9},{2,10},{3,11},{4,12},{5,13},{6,14},{7,15},{8,0},{9,1},... | collective-permute-start | bytes 175112 | tf_op jit(solution)/shard_map/ppermute | solution.py:18
  3.9 8.1 %collective-permute-start.2 = (bf16[4,7296]{1,0:T(4,128)(2,1)S(1)}, bf16[4,7296]{1,0:T(4,128)(2,1)S(1)}, u32[]{:S(2)}, u32[]{:S(2)}) collective-permute-start(bf16[4,7296]{1,0:T(4,128)(2,1)S(1)} %shard_map.64.refs_0_), channel_id=1, source_target_pairs={{0,3},{1,2},{2,1},{3,0},{4,7},{5,6},{6,5},{7,4},{8,11},{9,10},{10,... | collective-permute-start | bytes 175112 | tf_op jit(solution)/shard_map/ppermute | solution.py:18
  7.5 5.1 %collective-permute-start.1 = (bf16[4,7296]{1,0:T(4,128)(2,1)S(1)}, bf16[4,7296]{1,0:T(4,128)(2,1)S(1)}, u32[]{:S(2)}, u32[]{:S(2)}) collective-permute-start(bf16[4,7296]{1,0:T(4,128)(2,1)S(1)} %shard_map.64.refs_0_), channel_id=1, source_target_pairs={{0,2},{1,3},{2,0},{3,1},{4,6},{5,7},{6,4},{7,5},{8,10},{9,11},{10,... | collective-permute-start | bytes 175112 | tf_op jit(solution)/shard_map/ppermute | solution.py:18
  11.1 5.8 %collective-permute-start.3 = (bf16[8,7296]{1,0:T(8,128)(2,1)S(1)}, bf16[8,7296]{1,0:T(8,128)(2,1)S(1)}, u32[]{:S(2)}, u32[]{:S(2)}) collective-permute-start(bf16[8,7296]{1,0:T(8,128)(2,1)S(1)} %shard_map.66.refs_0_), channel_id=1, source_target_pairs={{0,1},{1,0},{2,3},{3,2},{4,5},{5,4},{6,7},{7,6},{8,9},{9,8},{10,11... | collective-permute-start | bytes 350216 | tf_op jit(solution)/shard_map/ppermute | solution.py:18
  12.6 4.9 %collective-permute-start.4 = (bf16[8,7296]{1,0:T(8,128)(2,1)S(1)}, bf16[8,7296]{1,0:T(8,128)(2,1)S(1)}, u32[]{:S(2)}, u32[]{:S(2)}) collective-permute-start(bf16[8,7296]{1,0:T(8,128)(2,1)S(1)} %shard_map.67.refs_1_), channel_id=1, source_target_pairs={{0,8},{1,9},{2,10},{3,11},{4,12},{5,13},{6,14},{7,15},{8,0},{9,1},... | collective-permute-start | bytes 350216 | tf_op jit(solution)/shard_map/ppermute | solution.py:18
  16.8 1.6 %collective-permute-start.5 = (bf16[16,7296]{1,0:T(8,128)(2,1)S(1)}, bf16[16,7296]{1,0:T(8,128)(2,1)S(1)}, u32[]{:S(2)}, u32[]{:S(2)}) collective-permute-start(bf16[16,7296]{1,0:T(8,128)(2,1)S(1)} %shard_map.68.refs_0_), channel_id=1, source_target_pairs={{0,4},{1,5},{2,6},{3,7},{4,0},{5,1},{6,2},{7,3},{8,12},{9,13},{10,... | collective-permute-start | bytes 700424 | tf_op jit(solution)/shard_map/ppermute | solution.py:18
  17.5 4.4 %slice-start = ((s8[7340032]{0:T(1024)(128)(4,1)}), s8[4194304]{0:T(1024)(128)(4,1)S(1)}, s32[]{:S(2)}) async-start(s8[7340032]{0:T(1024)(128)(4,1)} %bitcast.11), calls=%async_computation | async-start | bytes 8388608
  17.5 1.6 %collective-permute-start.6 = (bf16[16,7296]{1,0:T(8,128)(2,1)S(1)}, bf16[16,7296]{1,0:T(8,128)(2,1)S(1)}, u32[]{:S(2)}, u32[]{:S(2)}) collective-permute-start(bf16[16,7296]{1,0:T(8,128)(2,1)S(1)} %shard_map.70.refs_1_), channel_id=1, source_target_pairs={{0,4},{1,5},{2,6},{3,7},{4,0},{5,1},{6,2},{7,3},{8,12},{9,13},{10,... | collective-permute-start | bytes 700424 | tf_op jit(solution)/shard_map/ppermute | solution.py:18
  19.1 2.8 %slice-start.1 = ((s8[7340032]{0:T(1024)(128)(4,1)}), s8[3145728]{0:T(1024)(128)(4,1)S(1)}, s32[]{:S(2)}) async-start(s8[7340032]{0:T(1024)(128)(4,1)} %bitcast.11), calls=%async_computation.1 | async-start | bytes 6291456
  23.4 1.9 %collective-permute-start.7 = (bf16[32,7168]{1,0:T(8,128)(2,1)S(1)}, bf16[32,7168]{1,0:T(8,128)(2,1)S(1)}, u32[]{:S(2)}, u32[]{:S(2)}) collective-permute-start(bf16[32,7168]{1,0:T(8,128)(2,1)S(1)} %get-tuple-element.21), channel_id=1, source_target_pairs={{0,4},{1,5},{2,6},{3,7},{4,0},{5,1},{6,2},{7,3},{8,12},{9,13},{10,... | collective-permute-start | bytes 1376264 | tf_op jit(solution)/shard_map/ppermute | solution.py:18
  25.5 7.9 %collective-permute-start.8 = (bf16[8,7168]{1,0:T(8,128)(2,1)S(1)}, bf16[8,7168]{1,0:T(8,128)(2,1)S(1)}, u32[]{:S(2)}, u32[]{:S(2)}) collective-permute-start(bf16[8,7168]{1,0:T(8,128)(2,1)S(1)} %shard_map.75), channel_id=1, source_target_pairs={{0,1},{1,0},{2,3},{3,2},{4,5},{5,4},{6,7},{7,6},{8,9},{9,8},{10,11... | collective-permute-start | bytes 344072 | tf_op jit(solution)/shard_map/ppermute | solution.py:18
  26.2 5.3 %collective-permute-start.9 = (bf16[4,7168]{1,0:T(4,128)(2,1)S(1)}, bf16[4,7168]{1,0:T(4,128)(2,1)S(1)}, u32[]{:S(2)}, u32[]{:S(2)}) collective-permute-start(bf16[4,7168]{1,0:T(4,128)(2,1)S(1)} %get-tuple-element.18), channel_id=1, source_target_pairs={{0,8},{1,9},{2,10},{3,11},{4,12},{5,13},{6,14},{7,15},{8,0},{9,1},... | collective-permute-start | bytes 172040 | tf_op jit(solution)/shard_map/ppermute | solution.py:18
  27.4 7.3 %collective-permute-start.11 = (bf16[4,7168]{1,0:T(4,128)(2,1)S(1)}, bf16[4,7168]{1,0:T(4,128)(2,1)S(1)}, u32[]{:S(2)}, u32[]{:S(2)}) collective-permute-start(bf16[4,7168]{1,0:T(4,128)(2,1)S(1)} %shard_map.74.refs_0_), channel_id=1, source_target_pairs={{0,3},{1,2},{2,1},{3,0},{4,7},{5,6},{6,5},{7,4},{8,11},{9,10},{10,... | collective-permute-start | bytes 172040 | tf_op jit(solution)/shard_map/ppermute | solution.py:18
  29.8 7.0 %collective-permute-start.10 = (bf16[4,7168]{1,0:T(4,128)(2,1)S(1)}, bf16[4,7168]{1,0:T(4,128)(2,1)S(1)}, u32[]{:S(2)}, u32[]{:S(2)}) collective-permute-start(bf16[4,7168]{1,0:T(4,128)(2,1)S(1)} %shard_map.73.refs_0_), channel_id=1, source_target_pairs={{0,11},{1,10},{2,9},{3,8},{4,15},{5,14},{6,13},{7,12},{8,3},{9,2},... | collective-permute-start | bytes 172040 | tf_op jit(solution)/shard_map/ppermute | solution.py:18
  31.5 6.9 %collective-permute-start.12 = (bf16[4,7168]{1,0:T(4,128)(2,1)S(1)}, bf16[4,7168]{1,0:T(4,128)(2,1)S(1)}, u32[]{:S(2)}, u32[]{:S(2)}) collective-permute-start(bf16[4,7168]{1,0:T(4,128)(2,1)S(1)} %shard_map.76.refs_1_), channel_id=1, source_target_pairs={{0,2},{1,3},{2,0},{3,1},{4,6},{5,7},{6,4},{7,5},{8,10},{9,11},{10,... | collective-permute-start | bytes 172040 | tf_op jit(solution)/shard_map/ppermute | solution.py:18
  33.5 5.0 %collective-permute-start.13 = (bf16[4,7168]{1,0:T(4,128)(2,1)S(1)}, bf16[4,7168]{1,0:T(4,128)(2,1)S(1)}, u32[]{:S(2)}, u32[]{:S(2)}) collective-permute-start(bf16[4,7168]{1,0:T(4,128)(2,1)S(1)} %get-tuple-element.20), channel_id=1, source_target_pairs={{0,8},{1,9},{2,10},{3,11},{4,12},{5,13},{6,14},{7,15},{8,0},{9,1},... | collective-permute-start | bytes 172040 | tf_op jit(solution)/shard_map/ppermute | solution.py:18
